TPU v7x, 32 devices: a whole 2x2x4 slice. The times are simulated.
32 devices in a mesh: half: 2 (over core), prow: 8 (over z, x), pcol: 2 (over y).
Axes of the slice: x: 2, y: 2, z: 4, core: 2. Of those that a mesh axis runs over, the one named last changes fastest.
Arguments:
- child_update: float32 [2, 8192, 8192], P('half', 'prow', 'pcol'), may hold values from -6 to 6, as said below
- child_panel: float32 [2, 8192, 1024], P('half', 'prow'), may hold values from -3 to 3
- root_front: float32 [12288, 12288], P('prow', ('half', 'pcol')), may hold values from -29 to 6144, as said below
- index_map: int32 [2, 64], replicated, may hold values from 0 to 95, as said below
Outputs:
- root_next: float32 [12288, 12288], P('prow', ('half', 'pcol'))
Inputs may be any that keep to these rules, and one draw needn't show every extreme that they name: `child_update`: each child's matrix is symmetric. `root_front`: Symmetric. `index_map`: for each child the entries are distinct, and child 0 names the blocks 0 to 1. Of the 16 blocks of one process row of both children (blocks p * 8 on), at most 2 share one root process row v // 12; of the 32 blocks of one child process column (blocks q * 32 on), at most 8 share one root column group v // 24; both bounds are reached.
All inputs are finite; a program needn't handle non-finite values.
Results may differ from a plain program's by a relative error of at most 0.00016.
Values sent between devices are 32-bit elements; how exact they have to be, the bound alone decides.
No kernel may reach another device: no remote copies, remote signals or barrier semaphores. Data moves between devices by JAX's collectives and lax.ppermute only.
A program may use at most 192 MiB of HBM per device.

v0:
```python
import jax
import jax.numpy as jnp
from jax import lax
from jax.sharding import PartitionSpec as P

BLK = 128
RP = 256


def spread_2(value, axis, source):
    kept = jnp.where(lax.axis_index(axis) == source, value, 0).astype(value.dtype)
    return lax.psum(kept, axis)


def ranking(labels, count):
    onehot = (labels[..., None] == jnp.arange(count, dtype=jnp.int32)).astype(jnp.int32)
    return jnp.sum((jnp.cumsum(onehot, axis=-2) - 1) * onehot, axis=-1)


def solve_rows(factor, raw_rows, global_rows):
    solved = lax.linalg.triangular_solve(
        factor, raw_rows, left_side=False, lower=True, transpose_a=True
    )
    leading = jnp.concatenate(
        [factor, jnp.zeros((raw_rows.shape[0] - RP, RP), jnp.float32)], axis=0
    )
    return jnp.where(global_rows[:, None] < RP, leading, solved)


def shards(child_update, child_panel, root_front, index_map):
    highest = lax.Precision.HIGHEST
    rows_dev = child_update.shape[1]
    cols_dev = child_update.shape[2]
    col_count = lax.axis_size("pcol")
    row_count = lax.axis_size("prow")
    row_ratio = row_count // col_count
    group_count = 2 * col_count
    column_index = lax.axis_index("pcol")
    child_index = lax.axis_index("half")
    row_index = lax.axis_index("prow")
    group_index = lax.axis_index(("half", "pcol"))
    own_panel = child_panel[0]
    pieces = []
    for offset in range(row_ratio):
        remote = spread_2(own_panel, "prow", column_index * row_ratio + offset)
        product = lax.dot_general(
            own_panel,
            remote,
            (((1,), (1,)), ((), ())),
            precision=highest,
            preferred_element_type=jnp.float32,
        )
        pieces.append(child_update[0, :, offset * rows_dev : (offset + 1) * rows_dev] - product)
    schur_part = jnp.concatenate(pieces, axis=1)
    root_rows = root_front.shape[0]
    root_cols = root_front.shape[1]
    child_blocks = rows_dev // BLK
    col_blocks = cols_dev // BLK
    row_blocks = root_rows // BLK
    group_cols = root_cols // BLK
    cap_col = max(1, col_blocks // group_count)
    cap_row = max(1, 2 * child_blocks // row_count)
    by_column = index_map.reshape(2, col_count, col_blocks)
    by_row = index_map.reshape(2, row_count, child_blocks)
    col_groups = by_column // group_cols
    col_ranks = ranking(col_groups, group_count)
    row_owners = by_row // row_blocks
    arrives = col_groups == group_index
    col_slots = by_column - group_index * group_cols
    col_place = (
        arrives[:, :, :, None, None]
        & (col_ranks[:, :, :, None, None] == jnp.arange(cap_col, dtype=jnp.int32)[:, None])
        & (col_slots[:, :, :, None, None] == jnp.arange(group_cols, dtype=jnp.int32))
    ).astype(jnp.float32)
    col_place = jnp.sum(col_place, axis=2)
    row_local = by_row - row_index * row_blocks
    local_onehot = (row_local[..., None] == jnp.arange(row_blocks, dtype=jnp.int32)).astype(
        jnp.float32
    )
    own_groups = col_groups[child_index, column_index]
    own_col_ranks = col_ranks[child_index, column_index]
    col_select = (
        (own_groups[None, None, :] == jnp.arange(group_count, dtype=jnp.int32)[:, None, None])
        & (own_col_ranks[None, None, :] == jnp.arange(cap_col, dtype=jnp.int32)[None, :, None])
    ).astype(jnp.float32)
    outgoing = jnp.einsum(
        "guj,rjk->gurk",
        col_select,
        schur_part.reshape(rows_dev, col_blocks, BLK),
        precision=highest,
    )
    incoming = lax.all_to_all(outgoing, ("half", "pcol"), split_axis=0, concat_axis=0, tiled=True)
    incoming = incoming.reshape(2, col_count, cap_col, rows_dev, BLK)
    joint_owners = row_owners.transpose(1, 0, 2).reshape(row_count, 2 * child_blocks)
    joint_ranks = ranking(joint_owners, row_count)
    own_owner = joint_owners[row_index]
    own_rank = joint_ranks[row_index]
    row_select = (
        (own_owner[None, None, :] == jnp.arange(row_count, dtype=jnp.int32)[:, None, None])
        & (own_rank[None, None, :] == jnp.arange(cap_row, dtype=jnp.int32)[None, :, None])
    ).astype(jnp.float32)
    row_select = row_select.reshape(row_count, cap_row, 2, child_blocks)
    in_tiles = incoming.reshape(2, col_count, cap_col, child_blocks, BLK, BLK)
    outgoing_rows = jnp.einsum("trci,cquiyz->trquyz", row_select, in_tiles, precision=highest)
    arrived = lax.all_to_all(outgoing_rows, "prow", split_axis=0, concat_axis=0, tiled=True)
    slot_item = (
        (joint_owners[:, None, :] == row_index)
        & (joint_ranks[:, None, :] == jnp.arange(cap_row, dtype=jnp.int32)[None, :, None])
    ).astype(jnp.float32)
    slot_item = slot_item.reshape(row_count, cap_row, 2, child_blocks)
    row_place = jnp.einsum("prci,cpiw->prw", slot_item, local_onehot, precision=highest)
    slot_child = jnp.sum(slot_item, axis=3)
    col_slot = jnp.einsum("prc,cqus->prqus", slot_child, col_place, precision=highest)
    spread = jnp.einsum("prqus,prquyz->prysz", col_slot, arrived, precision=highest)
    extended = jnp.einsum("prw,prysz->wysz", row_place, spread, precision=highest)
    assembled = root_front + extended.reshape(root_rows, root_cols)
    global_rows = row_index * root_rows + jnp.arange(root_rows, dtype=jnp.int32)
    global_cols = group_index * root_cols + jnp.arange(root_cols, dtype=jnp.int32)
    group_ratio = row_count // group_count
    raw_panel = assembled[:, :RP]
    across = []
    pivot_block = spread_2(assembled[:RP, :RP], "prow", 0)
    factor = jnp.linalg.cholesky(pivot_block)
    own_rows = solve_rows(factor, raw_panel, global_rows)
    row_panel = spread_2(own_rows, ("half", "pcol"), 0)
    for offset in range(group_ratio):
        across.append(spread_2(row_panel, "prow", group_index * group_ratio + offset))
    columns = jnp.concatenate(across, axis=0)
    update = lax.dot_general(
        row_panel,
        columns,
        (((1,), (1,)), ((), ())),
        precision=highest,
        preferred_element_type=jnp.float32,
    )
    trailing_mask = (global_rows[:, None] >= RP) & (global_cols[None, :] >= RP)
    trailing = assembled - jnp.where(trailing_mask, update, 0.0)
    first_group = group_index == 0
    panel_cols = jnp.where(first_group, row_panel, trailing[:, :RP])
    return jnp.concatenate([panel_cols, trailing[:, RP:]], axis=1)


def solution(mesh):
    return jax.shard_map(
        shards,
        mesh=mesh,
        in_specs=(
            P("half", "prow", "pcol"),
            P("half", "prow", None),
            P("prow", ("half", "pcol")),
            P(),
        ),
        out_specs=P("prow", ("half", "pcol")),
        check_vma=False,
    )
```

profile of v0, /device:TPU:0, one launch (start us, length us, event | category | flops | bytes accessed | tf_op | source)
XLA Modules:
  0.0 1733.1 jit_solution(14603986457369241170)
XLA Ops:
  6.5 9.5 bitcast_select_fusion.3
  16.1 12.6 fusion.76
  28.7 5.3 copy.170
  34.0 5.4 copy.171
  39.4 5.4 copy.172
  44.8 5.4 copy.173
  50.6 0.2 select_reduce_fusion.2
  50.8 480.7 %all-reduce.15.cloned.1.call-done = (f32[1024,1024]{1,0:T(8,128)}, f32[1024,1024]{1,0:T(8,128)}, f32[1024,1024]{1,0:T(8,128)}, f32[1024,1024]{1,0:T(8,128)}) async-done(((f32[1024,1024]{1,0:T(8,128)}, f32[1024,1024]{1,0:T(8,128)}, f32[1024,1024]{1,0:T(8,128)}, f32[1024,1024]{1,0:T(8,128)}), (f32[1024,1024]{1,0:T(8,128)}, f32[1024,1024]{1,0:T(8,128)}, f32[1024,1024]{1,0:T(8,128)}, ...) | async-done | bytes 16777232 | tf_op jit(solution)/shard_map/psum | solution.py:12
  531.5 18.2 %bitcast_subtract_fusion.3 = f32[1024,1024]{0,1:T(8,128)S(1)} fusion(f32[1,1024,1024]{1,2,0:T(8,128)} %copy.170, f32[1024,1024]{1,0:T(8,128)} %get-tuple-element.50, f32[1,1024,1024]{2,1,0:T(8,128)} %param.5), kind=kOutput, calls=%fused_computation.21 | convolution fusion | flops 12885950464 | bytes 16777216 | tf_op jit(solution)/shard_map/dot_general | solution.py:46
  549.8 14.1 bitcast_subtract_fusion.2
  563.9 14.3 bitcast_subtract_fusion.1
  578.3 14.1 bitcast_subtract_fusion
  592.4 7.1 pad_maximum_fusion.1
  599.5 17.4 %copy.129 = f32[1024,32,128]{2,1,0:T(8,128)} copy(f32[1024,32,128]{0,2,1:T(8,128)} %bitcast.129) | data formatting | bytes 33554432 | tf_op jit(solution)/shard_map/reshape | solution.py:89
  616.9 15.1 fusion.4
  632.0 7.2 all-to-all-start
  639.5 0.4 fusion.77
  639.9 0.2 dynamic-slice_reduce_fusion
  640.3 181.9 %all-to-all-done = f32[4,8,1024,128]{3,1,2,0:T(8,128)} async-done(((f32[4,8,1024,128]{3,1,2,0:T(8,128)}), f32[4,8,1024,128]{3,1,2,0:T(8,128)}, u32[]{:S(2)}, u32[]{:S(2)}) %all-to-all-start) | async-done | bytes 16777248 | tf_op jit(solution)/shard_map/all_to_all | solution.py:92
  822.2 25.7 %fusion.15 = f32[8,2,2,8,128,128]{5,0,4,3,2,1:T(8,128)} fusion(f32[2,2,8,8,128,128]{5,2,4,3,1,0:T(8,128)} %bitcast.22, pred[2,2,8]{2,1,0:T(4,128)(4,1)S(1)} %iota_compare_fusion.13, pred[8,2,8]{2,0,1:T(8,128)(4,1)S(1)} %iota_compare_fusion.10), kind=kOutput, calls=%fused_computation.17 | convolution fusion | flops 805306624 | bytes 33554592 | tf_op jit(solution)/shard_map/trci,cquiyz->trquyz/dot_general | solution.py:104
  847.9 14.5 copy.131
  862.4 5.8 all-to-all-start.1
  868.4 0.1 convert_reduce_fusion.1
  868.7 18.6 %copy.139 = f32[1536,3072]{0,1:T(8,128)} copy(f32[1536,3072]{1,0:T(8,128)} %param.6) | data formatting | bytes 37748736 | tf_op args[2]
  887.4 0.2 convert_reduce_fusion
  887.6 0.3 convolution_bitcast_fusion
  887.9 0.2 convolution_bitcast_fusion.1
  888.1 343.0 %all-to-all-done.1 = f32[8,2,2,8,128,128]{5,4,3,2,1,0:T(8,128)} async-done(((f32[8,2,2,8,128,128]{5,4,3,2,1,0:T(8,128)}), f32[8,2,2,8,128,128]{5,4,3,2,1,0:T(8,128)}, u32[]{:S(2)}, u32[]{:S(2)}) %all-to-all-start.1) | async-done | bytes 16777248 | tf_op jit(solution)/shard_map/all_to_all | solution.py:105
  1231.1 34.6 %fusion.12 = f32[8,2,128,24,128]{4,3,2,1,0:T(8,128)S(1)} fusion(f32[8,2,2,8,128,128]{5,4,3,2,1,0:T(8,128)} %all-to-all-done.1, f32[8,2,2,8,24,1]{4,0,3,2,1,5:T(8,128)S(1)} %convolution_bitcast_fusion), kind=kOutput, calls=%fused_computation.16 | convolution fusion | flops 1207959552 | bytes 41967616 | tf_op jit(solution)/shard_map/prqus,prquyz->prysz/dot_general | solution.py:114
  1265.7 33.6 %fusion.9 = f32[12,128,24,128]{3,0,2,1:T(8,128)} fusion(f32[8,2,128,24,128]{4,3,2,1,0:T(8,128)S(1)} %fusion.12, f32[8,2,12,1,1]{2,1,0,4,3:T(2,128)S(1)} %convolution_bitcast_fusion.1), kind=kOutput, calls=%fused_computation.15 | convolution fusion | flops 905969664 | bytes 44040960 | tf_op jit(solution)/shard_map/prw,prysz->wysz/dot_general | solution.py:115
  1299.3 25.1 %copy.167 = f32[12,128,24,128]{1,0,3,2:T(8,128)} copy(f32[12,128,24,128]{3,0,2,1:T(8,128)} %fusion.9) | data formatting | bytes 37748736 | tf_op jit(solution)/shard_map/reshape | solution.py:116
  1324.4 17.4 %bitcast_add_fusion = f32[1536,3072]{0,1:T(8,128)S(1)} fusion(f32[1536,3072]{0,1:T(8,128)} %copy.139, f32[384,8,12,128]{3,2,1,0:T(8,128)} %bitcast.128), kind=kLoop, calls=%fused_computation.4 | loop fusion | flops 4718592 | bytes 56623104 | tf_op jit(solution)/shard_map/add | solution.py:116
  1341.9 6.8 copy-done
  1348.7 0.7 slice_select_fusion.1
  1349.4 0.3 all-reduce.11.cloned.1.call-start
  1349.8 68.6 %all-reduce.9.cloned.1.call-done = f32[256,256]{0,1:T(8,128)} async-done(((f32[256,256]{0,1:T(8,128)}), f32[256,256]{0,1:T(8,128)}) %all-reduce.9.cloned.1.call-update) | async-done | bytes 262160 | tf_op jit(solution)/shard_map/psum | solution.py:12
  1418.3 1.1 copy.141
  1419.4 1.0 fusion.41
  1420.4 11.7 cholesky.49
  1432.2 9.8 custom-call.14
  1442.0 0.2 fusion.46
  1442.2 0.3 convolution_subtract_fusion.1
  1442.5 11.7 cholesky.103
  1454.5 0.6 compare_reduce_fusion
  1455.1 0.7 compare_reduce_fusion.1
  1457.3 4.5 while.1
  1457.5 0.7 fusion.89
  1458.2 1.3 dynamic-slice.7
  1459.7 0.7 fusion.89
  1460.4 1.3 dynamic-slice.7
  1461.8 19.7 %custom-call.15 = f32[2,128,128]{1,2,0:T(8,128)S(1)} custom-call(f32[2,128,128]{2,1,0:T(8,128)S(1)} %get-tuple-element.12), custom_call_target="InvertDiagBlocksLowerTriangular" | custom-call | tf_op jit(solution)/shard_map/triangular_solve | solution.py:21
  1481.5 2.0 fusion.39
  1483.5 2.0 convolution_subtract_fusion
  1485.5 0.9 fusion.44
  1486.3 1.3 fusion.37
  1487.8 42.2 %all-reduce.11.cloned.1.call-done = f32[1536,256]{0,1:T(8,128)} async-done(((f32[1536,256]{0,1:T(8,128)}), f32[1536,256]{0,1:T(8,128)}) %all-reduce.11.cloned.1.call-update) | async-done | bytes 1572880 | tf_op jit(solution)/shard_map/psum | solution.py:12
  1530.0 3.6 broadcast_select_fusion.1
  1533.7 129.9 %all-reduce.13.cloned.1.call-done = (f32[1536,256]{0,1:T(8,128)}, f32[1536,256]{0,1:T(8,128)}) async-done(((f32[1536,256]{0,1:T(8,128)}, f32[1536,256]{0,1:T(8,128)}), (f32[1536,256]{0,1:T(8,128)}, f32[1536,256]{0,1:T(8,128)})) %all-reduce.13.cloned.1.call-update) | async-done | bytes 3145744 | tf_op jit(solution)/shard_map/psum | solution.py:12
  1663.5 23.4 %select_subtract_fusion = f32[1536,3072]{0,1:T(8,128)} fusion(f32[1536,3072]{0,1:T(8,128)} %copy-done, f32[1536,256]{0,1:T(8,128)S(1)} %copy-done.3, pred[1536]{0:T(1024)(128)(4,1)S(1)} %fusion.64, pred[3072]{0:T(1024)(128)(4,1)S(1)} %add_compare_fusion, f32[1536,256]{0,1:T(8,128)} %get-tuple-element.45, f32[1536,256]{0,1:T(8,128)} %get-tuple-element.46), kind=kOutput, calls=%fused_computation.6 | convolution fusion | flops 14510456832 | bytes 42471936 | tf_op jit(solution)/shard_map/dot_general | solution.py:129
  1686.9 6.4 copy-done.2
  1693.3 3.6 slice_select_fusion
  1696.8 2.4 slice-done
  1699.2 8.2 pad_maximum_fusion
  1707.5 18.6 %copy.148 = f32[1536,3072]{1,0:T(8,128)} copy(f32[1536,3072]{0,1:T(8,128)} %pad_maximum_fusion) | data formatting | bytes 37748736 | tf_op jit(solution)/shard_map/concatenate | solution.py:140
  (79 shorter events, 2.2 us)
Async XLA Ops:
  6.5 524.9 %all-reduce.15.cloned.1.call-start = ((), (), s32[]{:S(2)}) async-start(), calls=%async_computation.5 | async-start | bytes 33554432 | tf_op jit(solution)/shard_map/psum | solution.py:12
  44.8 5.4 copy-start.10
  531.5 18.2 %copy-start.1 = (f32[1,1024,1024]{2,1,0:T(8,128)S(1)}, f32[1,1024,1024]{2,1,0:T(8,128)}, u32[]{:S(2)}) copy-start(f32[1,1024,1024]{2,1,0:T(8,128)} %param.5) | copy-start | bytes 12582916
  531.5 18.3 %copy-start.6 = (f32[1,1024,1024]{1,2,0:T(8,128)S(1)}, f32[1,1024,1024]{1,2,0:T(8,128)}, u32[]{:S(2)}) copy-start(f32[1,1024,1024]{1,2,0:T(8,128)} %copy.171) | copy-start | bytes 12582916
  531.5 18.3 %copy-start.9 = (f32[1024,1024]{1,0:T(8,128)S(1)}, f32[1024,1024]{1,0:T(8,128)}, u32[]{:S(2)}) copy-start(f32[1024,1024]{1,0:T(8,128)} %get-tuple-element.49) | copy-start | bytes 12582916
  549.8 14.1 copy-start.5
  549.8 14.1 copy-start.8
  563.9 14.3 copy-start.4
  563.9 14.3 copy-start.7
  632.0 190.2 %all-to-all-start = ((f32[4,8,1024,128]{3,1,2,0:T(8,128)}), f32[4,8,1024,128]{3,1,2,0:T(8,128)}, u32[]{:S(2)}, u32[]{:S(2)}) async-start(f32[4,8,1024,128]{3,1,2,0:T(8,128)} %fusion.4), calls=%async_computation | async-start | bytes 33554432 | tf_op jit(solution)/shard_map/all_to_all | solution.py:92
  862.4 368.7 %all-to-all-start.1 = ((f32[8,2,2,8,128,128]{5,4,3,2,1,0:T(8,128)}), f32[8,2,2,8,128,128]{5,4,3,2,1,0:T(8,128)}, u32[]{:S(2)}, u32[]{:S(2)}) async-start(f32[8,2,2,8,128,128]{5,4,3,2,1,0:T(8,128)} %copy.131), calls=%async_computation.1 | async-start | bytes 33554432 | tf_op jit(solution)/shard_map/all_to_all | solution.py:105
  868.2 550.1 %all-reduce.9.cloned.1.call-start = ((), (), s32[]{:S(2)}) async-start(), calls=%async_computation.2 | async-start | bytes 524288 | tf_op jit(solution)/shard_map/psum | solution.py:12
  1341.9 6.9 copy-start
  1349.4 180.6 %all-reduce.11.cloned.1.call-start = ((), (), s32[]{:S(2)}) async-start(), calls=%async_computation.3 | async-start | bytes 3145728 | tf_op jit(solution)/shard_map/psum | solution.py:12
  1487.7 175.8 %all-reduce.13.cloned.1.call-start = ((), (), s32[]{:S(2)}) async-start(), calls=%async_computation.4 | async-start | bytes 6291456 | tf_op jit(solution)/shard_map/psum | solution.py:12
  1530.0 133.5 %copy-start.3 = (f32[1536,256]{0,1:T(8,128)S(1)}, f32[1536,256]{0,1:T(8,128)}, u32[]{:S(2)}) copy-start(f32[1536,256]{0,1:T(8,128)} %all-reduce.11.cloned.1.call-done) | copy-start | bytes 4718596
  1686.9 6.4 copy-start.2
  1686.9 12.3 slice-start
Sparse Core Ops, SparseCore 0:
  16.2 515.2 all-reduce.14
  1349.6 68.7 all-reduce.8
  1487.8 42.1 all-reduce.10
  1534.0 129.5 all-reduce.12
where the time goes:
time: 1740 us; the launch traced here: 1730 us
  waiting for transfers between devices  1250 us (72%)
  matrix products  199 us (11%)
  local copies, waits for them, and re-layouts  151 us (9%)
  other arithmetic  108 us (6%)
    psum x4, waiting for transfers between devices, spread_2(): return lax.psum(kept, axis)  721 us
    all_to_all x1, waiting for transfers between devices, shards(): lax.all_to_all(outgoing_rows, 'prow', split_axis=0, concat_axis=0, tiled=...  343 us
    all_to_all x1, waiting for transfers between devices, shards(): lax.all_to_all(outgoing, ('half', 'pcol'), split_axis=0, concat_axis=0, t...  182 us
    dot_general x4, matrix products, shards(): lax.dot_general(own_panel, remote, (((1,), (1,)), ((), ())), precision=hi...  60.7 us
    unnamed x27, local copies, waits for them, and re-layouts  53.4 us
  transfers between devices with their start and end apart: 6, of which 6 were waited for; matrix products, arithmetic and copies ran while one was open for 3% of the time, Pallas kernels for 0%

commit v1 on v0

v1 whole, which is shorter than its diff:
```python
import functools

import jax
import jax.numpy as jnp
from jax import lax
from jax.experimental import pallas as pl
from jax.experimental.pallas import tpu as pltpu
from jax.sharding import PartitionSpec as P

BLK = 128
RP = 256
F32 = jnp.float32
BF16 = jnp.bfloat16
HIGHEST = lax.Precision.HIGHEST
NT = (((1,), (1,)), ((), ()))
VMEM_LIMIT = 56 * 1024 * 1024


def split(x):
    hi = x.astype(BF16)
    lo = (x - hi.astype(F32)).astype(BF16)
    return hi, lo


def dot_nt(a, b):
    return lax.dot_general(a, b, NT, preferred_element_type=F32)


def params():
    return pltpu.CompilerParams(vmem_limit_bytes=VMEM_LIMIT)


def cost(flops, nbytes):
    return pl.CostEstimate(flops=int(flops), bytes_accessed=int(nbytes), transcendentals=0)


def pack_columns(update, chosen):
    rows = update.shape[0]
    groups, width = chosen.shape

    def body(chosen_ref, in_ref, out_ref):
        out_ref[0, 0] = in_ref[...]

    return pl.pallas_call(
        body,
        grid_spec=pltpu.PrefetchScalarGridSpec(
            num_scalar_prefetch=1,
            grid=(groups, width),
            in_specs=[pl.BlockSpec((rows, BLK), lambda g, u, s: (0, s[g * width + u]))],
            out_specs=pl.BlockSpec((1, 1, rows, BLK), lambda g, u, s: (g, u, 0, 0)),
        ),
        out_shape=jax.ShapeDtypeStruct((groups, width, rows, BLK), F32),
        compiler_params=params(),
        cost_estimate=cost(0, 8 * groups * width * rows * BLK),
    )(chosen.reshape(-1), update)


def pick_rows(own, other, block, mine):
    count = block.shape[0]
    depth = own.shape[1]

    def body(block_ref, mine_ref, own_ref, other_ref, out_ref):
        s = pl.program_id(0)

        @pl.when(mine_ref[s] == 1)
        def _():
            out_ref[0] = own_ref[...]

        @pl.when(mine_ref[s] == 0)
        def _():
            out_ref[0] = other_ref[...]

    spec = pl.BlockSpec((BLK, depth), lambda s, b, m: (b[s], 0))
    return pl.pallas_call(
        body,
        grid_spec=pltpu.PrefetchScalarGridSpec(
            num_scalar_prefetch=2,
            grid=(count,),
            in_specs=[spec, spec],
            out_specs=pl.BlockSpec((1, BLK, depth), lambda s, b, m: (s, 0, 0)),
        ),
        out_shape=jax.ShapeDtypeStruct((count, BLK, depth), F32),
        compiler_params=params(),
        cost_estimate=cost(0, 12 * count * BLK * depth),
    )(block, mine, own, other)


def schur_rows(own, other, columns, panel_blocks, child, block, mine, places):
    slots = child.shape[0]
    depth = own.shape[1]
    _, col_count, width, rows, _ = columns.shape
    wide = col_count * width * BLK
    per_child = col_count * width

    def body(child_ref, block_ref, mine_ref, place_ref, own_ref, other_ref, col_ref, *rest):
        b_refs = rest[: 2 * per_child]
        out_ref, hi_ref, lo_ref = rest[2 * per_child :]
        s = pl.program_id(0)

        @pl.when(s == 0)
        def _():
            for k in range(2 * per_child):
                at = pl.ds((k % per_child) * BLK, BLK)
                hi, lo = split(b_refs[k][0])
                hi_ref[k // per_child, at, :] = hi
                lo_ref[k // per_child, at, :] = lo

        c = child_ref[s]
        rows_f32 = jnp.where(mine_ref[s] == 1, own_ref[...], other_ref[...])
        a_hi, a_lo = split(rows_f32)
        both = dot_nt(jnp.concatenate([a_hi, a_lo], axis=0), hi_ref[c])
        total = both[:BLK] + both[BLK:] + dot_nt(a_hi, lo_ref[c])
        for q in range(col_count):
            for u in range(width):
                k = q * width + u
                out_ref[0, q, u] = col_ref[0, q, u] - total[:, k * BLK : (k + 1) * BLK]

    row_spec = pl.BlockSpec((BLK, depth), lambda s, c, b, m, p: (b[s], 0))
    b_specs = [
        pl.BlockSpec((1, BLK, depth), functools.partial(lambda k, s, c, b, m, p: (p[k], 0, 0), k))
        for k in range(2 * per_child)
    ]
    return pl.pallas_call(
        body,
        grid_spec=pltpu.PrefetchScalarGridSpec(
            num_scalar_prefetch=4,
            grid=(slots,),
            in_specs=[
                row_spec,
                row_spec,
                pl.BlockSpec(
                    (1, col_count, width, BLK, BLK), lambda s, c, b, m, p: (c[s], 0, 0, b[s], 0)
                ),
            ]
            + b_specs,
            out_specs=pl.BlockSpec(
                (1, col_count, width, BLK, BLK), lambda s, c, b, m, p: (s, 0, 0, 0, 0)
            ),
            scratch_shapes=[
                pltpu.VMEM((2, wide, depth), BF16),
                pltpu.VMEM((2, wide, depth), BF16),
            ],
        ),
        out_shape=jax.ShapeDtypeStruct((slots, col_count, width, BLK, BLK), F32),
        compiler_params=params(),
        cost_estimate=cost(
            6 * slots * BLK * wide * depth, slots * BLK * (2 * depth + 2 * wide) * 4 + 8 * wide * depth
        ),
    )(child, block, mine, places, own, other, columns, *([panel_blocks] * (2 * per_child)))


def first_panel(root, part, row_slot, row_valid, col_place):
    row_blocks = root.shape[0] // BLK
    _, col_count, width, _, _ = part.shape

    def body(slot_ref, valid_ref, place_ref, root_ref, a0_ref, a1_ref, out_ref):
        r = pl.program_id(0)
        out_ref[...] = root_ref[...]
        for c, a_ref in enumerate((a0_ref, a1_ref)):
            for q in range(col_count):
                for u in range(width):
                    col = place_ref[c, q * width + u]
                    ok = (valid_ref[c * row_blocks + r] == 1) & (col >= 0) & (col < RP // BLK)

                    @pl.when(ok)
                    def _():
                        at = pl.ds(pl.multiple_of(col * BLK, BLK), BLK)
                        out_ref[:, at] += a_ref[0, q, u]

    def arrived(c):
        return pl.BlockSpec(
            (1, col_count, width, BLK, BLK), lambda r, s, v, p: (s[c * row_blocks + r], 0, 0, 0, 0)
        )

    return pl.pallas_call(
        body,
        grid_spec=pltpu.PrefetchScalarGridSpec(
            num_scalar_prefetch=3,
            grid=(row_blocks,),
            in_specs=[pl.BlockSpec((BLK, RP), lambda r, s, v, p: (r, 0)), arrived(0), arrived(1)],
            out_specs=pl.BlockSpec((BLK, RP), lambda r, s, v, p: (r, 0)),
        ),
        out_shape=jax.ShapeDtypeStruct((root.shape[0], RP), F32),
        compiler_params=params(),
        cost_estimate=cost(0, 8 * root.shape[0] * RP + 4 * part.size),
    )(row_slot, row_valid, col_place, root, part, part)


def finish(root, parts, own_rows, columns, row_slot, row_valid, col_place, flags):
    rows, cols = root.shape
    row_blocks = rows // BLK
    count = len(parts)
    _, col_count, width, _, _ = parts[0].shape
    step = next(w for w in (512, 384, 256) if cols % w == 0)

    def body(slot_ref, valid_ref, place_ref, flag_ref, root_ref, *rest):
        a_refs = rest[: 2 * count]
        own_ref, col_ref, out_ref, hi_ref, lo_ref = rest[2 * count :]
        r = pl.program_id(0)

        @pl.when(r == 0)
        def _():
            hi, lo = split(col_ref[...])
            hi_ref[...] = hi
            lo_ref[...] = lo

        pivot_rows = (flag_ref[0] == 1) & (r < RP // BLK)

        @pl.when(pivot_rows)
        def _():
            out_ref[...] = root_ref[...]

        @pl.when(jnp.logical_not(pivot_rows))
        def _():
            a_hi, a_lo = split(own_ref[...])
            stacked = jnp.concatenate([a_hi, a_lo], axis=0)
            for n in range(0, cols, step):
                both = dot_nt(stacked, hi_ref[n : n + step, :])
                total = both[:BLK] + both[BLK:] + dot_nt(a_hi, lo_ref[n : n + step, :])
                out_ref[:, n : n + step] = root_ref[:, n : n + step] - total

        for c in range(2):
            for j in range(count):
                for q in range(col_count):
                    for u in range(width):
                        col = place_ref[c, (j * col_count + q) * width + u]

                        @pl.when((valid_ref[c * row_blocks + r] == 1) & (col >= 0))
                        def _():
                            at = pl.ds(pl.multiple_of(col * BLK, BLK), BLK)
                            out_ref[:, at] += a_refs[c * count + j][0, q, u]

        @pl.when(flag_ref[1] == 1)
        def _():
            out_ref[:, :RP] = own_ref[...]

    def arrived(c):
        return pl.BlockSpec(
            (1, col_count, width, BLK, BLK),
            lambda r, s, v, p, f: (s[c * row_blocks + r], 0, 0, 0, 0),
        )

    return pl.pallas_call(
        body,
        grid_spec=pltpu.PrefetchScalarGridSpec(
            num_scalar_prefetch=4,
            grid=(row_blocks,),
            in_specs=[pl.BlockSpec((BLK, cols), lambda r, s, v, p, f: (r, 0))]
            + [arrived(0)] * count
            + [arrived(1)] * count
            + [
                pl.BlockSpec((BLK, RP), lambda r, s, v, p, f: (r, 0)),
                pl.BlockSpec((cols, RP), lambda r, s, v, p, f: (0, 0)),
            ],
            out_specs=pl.BlockSpec((BLK, cols), lambda r, s, v, p, f: (r, 0)),
            scratch_shapes=[pltpu.VMEM((cols, RP), BF16), pltpu.VMEM((cols, RP), BF16)],
        ),
        out_shape=jax.ShapeDtypeStruct((rows, cols), F32),
        compiler_params=params(),
        cost_estimate=cost(6 * rows * cols * RP, 8 * rows * cols + 4 * sum(p.size for p in parts)),
    )(row_slot, row_valid, col_place, flags, root, *parts, *parts, own_rows, columns)


def shards(child_update, child_panel, root_front, index_map):
    col_count = lax.axis_size("pcol")
    row_count = lax.axis_size("prow")
    group_count = 2 * col_count
    half = lax.axis_index("half")
    pcol = lax.axis_index("pcol")
    prow = lax.axis_index("prow")
    group = half * col_count + pcol
    rows_dev = child_update.shape[1]
    root_rows, root_cols = root_front.shape
    child_blocks = rows_dev // BLK
    col_blocks = child_update.shape[2] // BLK
    row_blocks = root_rows // BLK
    group_cols = root_cols // BLK
    ratio = root_cols // root_rows
    cap_col = max(1, col_blocks // group_count)
    cap_row = max(1, 2 * child_blocks // row_count)
    cap_pick = cap_row * ratio
    width = 2 if cap_col % 2 == 0 else 1
    chunks = cap_col // width
    iota = functools.partial(jnp.arange, dtype=jnp.int32)
    own_panel = child_panel[0]
    other_panel = lax.ppermute(own_panel, "half", [(0, 1), (1, 0)])

    by_col = index_map.reshape(2, col_count, col_blocks)
    col_group = by_col // group_cols
    before = (by_col[..., None, :] < by_col[..., :, None]) & (
        col_group[..., None, :] == col_group[..., :, None]
    )
    col_rank = jnp.sum(before.astype(jnp.int32), axis=-1)
    col_key = col_group * cap_col + col_rank
    own_key = lax.dynamic_index_in_dim(
        col_key.reshape(group_count, col_blocks), group, 0, keepdims=False
    )
    chosen = jnp.sum(
        jnp.where(own_key[None, :] == iota(group_count * cap_col)[:, None], iota(col_blocks), 0),
        axis=1,
    ).reshape(group_count, cap_col)

    by_row = index_map.reshape(2, row_count, child_blocks)
    joint = by_row.transpose(1, 0, 2).reshape(row_count, 2 * child_blocks)
    items = 2 * child_blocks
    earlier = iota(items)[None, :] < iota(items)[:, None]
    owner = joint // row_blocks
    row_rank = jnp.sum(
        ((owner[:, None, :] == owner[:, :, None]) & earlier).astype(jnp.int32), axis=-1
    )
    joint_group = joint // group_cols
    pick_rank = jnp.sum(
        ((joint_group[:, None, :] == joint_group[:, :, None]) & earlier).astype(jnp.int32), axis=-1
    )
    here = lax.dynamic_index_in_dim
    own_owner = here(owner, prow, 0, keepdims=False)
    own_row_rank = here(row_rank, prow, 0, keepdims=False)
    own_pick_group = here(joint_group, prow, 0, keepdims=False)
    own_pick_rank = here(pick_rank, prow, 0, keepdims=False)
    pick_item = jnp.sum(
        jnp.where(
            (own_pick_group[None, :] == group) & (own_pick_rank[None, :] == iota(cap_pick)[:, None]),
            iota(items),
            0,
        ),
        axis=1,
    )
    send_item = jnp.sum(
        jnp.where(
            (own_owner * cap_row + own_row_rank)[None, :] == iota(row_count * cap_row)[:, None],
            iota(items),
            0,
        ),
        axis=1,
    )

    def to_child(item):
        child = item // child_blocks
        return child, item % child_blocks, (child == half).astype(jnp.int32)

    slot_of = (iota(row_count)[:, None] * cap_pick + pick_rank).reshape(
        row_count, 2, child_blocks
    )
    slot_of = slot_of.transpose(1, 0, 2).reshape(2, col_count, col_blocks)
    match = col_key[:, :, None, :] == (group * cap_col + iota(cap_col))[:, None]
    place = jnp.sum(jnp.where(match, slot_of[:, :, None, :], 0), axis=-1)
    col_local = (
        jnp.sum(jnp.where(match, by_col[:, :, None, :] - group * group_cols + 1, 0), axis=-1) - 1
    )

    def chunked(table):
        table = table.reshape(2, col_count, chunks, width).transpose(2, 0, 1, 3)
        return table.reshape(chunks, 2, col_count * width)

    place = chunked(place)
    col_local = chunked(col_local)
    row_slot = (iota(row_count)[:, None] * cap_row + row_rank).reshape(row_count, 2, child_blocks)
    row_match = by_row[..., None] == prow * row_blocks + iota(row_blocks)
    row_slot = jnp.sum(
        jnp.where(row_match, row_slot.transpose(1, 0, 2)[..., None] + 1, 0), axis=(1, 2)
    )
    row_valid = (row_slot > 0).astype(jnp.int32).reshape(-1)
    row_slot = jnp.maximum(row_slot - 1, 0).reshape(-1)

    _, pick_block, pick_mine = to_child(pick_item)
    picked = pick_rows(own_panel, other_panel, pick_block, pick_mine)
    panel_blocks = lax.all_gather(picked, "prow", axis=0, tiled=True)

    columns = []
    for j in range(chunks):
        packed = pack_columns(child_update[0], chosen[:, j * width : (j + 1) * width])
        got = lax.all_to_all(packed, ("half", "pcol"), split_axis=0, concat_axis=0, tiled=True)
        columns.append(got.reshape(2, col_count, width, rows_dev, BLK))

    send_child, send_block, send_mine = to_child(send_item)
    parts = []
    for j in range(chunks):
        outgoing = schur_rows(
            own_panel,
            other_panel,
            columns[j],
            panel_blocks,
            send_child,
            send_block,
            send_mine,
            place[j].reshape(-1),
        )
        parts.append(lax.all_to_all(outgoing, "prow", split_axis=0, concat_axis=0, tiled=True))

    raw = first_panel(root_front, parts[0], row_slot, row_valid, col_local[0])

    def to_groups(value):
        span = 1
        while span < col_count:
            got = lax.ppermute(value, "pcol", [(i, i + span) for i in range(min(span, col_count - span))])
            value = jnp.where((pcol >= span) & (pcol < 2 * span), got, value)
            span *= 2
        got = lax.ppermute(value, "half", [(0, 1)])
        return jnp.where(half == 1, got, value)

    pivot = to_groups(raw[:RP])
    span = 1
    while span < row_count:
        got = lax.ppermute(pivot, "prow", [(i, i + span) for i in range(min(span, row_count - span))])
        pivot = jnp.where((prow >= span) & (prow < 2 * span), got, pivot)
        span *= 2
    factor = jnp.linalg.cholesky(pivot)
    inverse = lax.linalg.triangular_solve(
        factor, jnp.eye(RP, dtype=F32), left_side=True, lower=True
    )
    raw_rows = to_groups(raw)
    bands = row_count // ratio
    device = lambda g, r: ((g // col_count) * row_count + r) * col_count + g % col_count
    shift = (prow // ratio - group) % bands
    tile = jnp.where(shift == 0, raw_rows, 0.0)
    for k in range(1, bands):
        pairs = [
            (device(g, g * ratio + o), device(g, ((g + k) % bands) * ratio + o))
            for g in range(group_count)
            for o in range(ratio)
        ]
        got = lax.ppermute(raw_rows, ("half", "prow", "pcol"), pairs)
        tile = jnp.where(shift == k, got, tile)
    tiles = [tile]
    for o in range(1, ratio):
        pairs = [
            (r, (r // ratio) * ratio + (r % ratio + o) % ratio) for r in range(row_count)
        ]
        tiles.append(lax.ppermute(tile, "prow", pairs))
    offset = prow % ratio
    ordered = []
    for o in range(ratio):
        value = tiles[0]
        for k in range(1, ratio):
            value = jnp.where((offset - k) % ratio == o, tiles[k], value)
        ordered.append(value)
    raw_cols = jnp.concatenate(ordered, axis=0)
    solved = lax.dot_general(raw_rows, inverse, NT, precision=HIGHEST, preferred_element_type=F32)
    lower_cols = lax.dot_general(
        raw_cols, inverse, NT, precision=HIGHEST, preferred_element_type=F32
    )
    top = jnp.where(prow == 0, factor, solved[:RP])
    own_rows = jnp.concatenate([top, solved[RP:]], axis=0)
    flags = jnp.stack([(prow == 0), (group == 0)]).astype(jnp.int32)
    col_all = col_local.transpose(1, 0, 2).reshape(2, -1)
    return finish(root_front, parts, own_rows, lower_cols, row_slot, row_valid, col_all, flags)


def solution(mesh):
    return jax.shard_map(
        shards,
        mesh=mesh,
        in_specs=(
            P("half", "prow", "pcol"),
            P("half", "prow", None),
            P("prow", ("half", "pcol")),
            P(),
        ),
        out_specs=P("prow", ("half", "pcol")),
        check_vma=False,
    )
```

time: 1740 us -> 825 us (0.47)
  the two profiles are of different devices: /device:TPU:0 before, /device:TPU:24 now
where the time goes in v1:
time: 825 us; the launch traced here: 821 us
  waiting for transfers between devices  486 us (59%)
  Pallas kernels  161 us (20%)
  other arithmetic  66.4 us (8%)
  starting transfers between devices  63.3 us (8%)
  local copies, waits for them, and re-layouts  19.9 us (2%)
  between operations  15.2 us (2%)
  matrix products  9.57 us (1%)
    all_to_all x4, waiting for transfers between devices, shards(): lax.all_to_all(outgoing, 'prow', split_axis=0, concat_axis=0, tiled=True)  149 us
    ppermute x3, waiting for transfers between devices, shards(): lax.ppermute(pivot, 'prow', [(i, i + span) for i in range(min(span, row_c...  126 us
    all_to_all x4, waiting for transfers between devices, shards(): lax.all_to_all(packed, ('half', 'pcol'), split_axis=0, concat_axis=0, til...  121 us
    pallas_call x4, Pallas kernels, schur_rows(): pl.pallas_call(body, grid_spec=pltpu.PrefetchScalarGridSpec(num_scalar_pr...  86.8 us
    all_gather x1, waiting for transfers between devices, shards(): panel_blocks = lax.all_gather(picked, 'prow', axis=0, tiled=True)  50.3 us
    another operation x7, other arithmetic, shards(): factor = jnp.linalg.cholesky(pivot)  34.7 us
    ppermute x2, waiting for transfers between devices, to_groups(): lax.ppermute(value, 'pcol', [(i, i + span) for i in range(min(span, col_c...  34 us
    pallas_call x1, Pallas kernels, finish(): pl.pallas_call(body, grid_spec=pltpu.PrefetchScalarGridSpec(num_scalar_pr...  30.4 us
  transfers between devices with their start and end apart: 21, of which 11 were waited for; matrix products, arithmetic and copies ran while one was open for 12% of the time, Pallas kernels for 15%

profile of v1, /device:TPU:24, one launch (start us, length us, event | category | flops | bytes accessed | tf_op | source)
XLA Modules:
  0.0 821.2 jit_solution(932547652133486640)
XLA Ops:
  6.5 0.8 eq.171
  10.2 3.9 collective-permute-done.other_ref
  14.0 5.0 shard_map.47
  20.5 0.7 reshape.292.chosen_ref
  21.2 7.4 shard_map.46
  28.6 4.9 all-to-all-start
  34.2 7.3 shard_map.49
  41.5 40.2 %all-to-all-done = f32[4,2,1024,128]{3,2,1,0:T(8,128)} async-done(((f32[4,2,1024,128]{3,2,1,0:T(8,128)}), f32[4,2,1024,128]{3,2,1,0:T(8,128)}, u32[]{:S(2)}, u32[]{:S(2)}) %all-to-all-start) | async-done | bytes 4194336 | tf_op jit(solution)/shard_map/all_to_all | solution.py:372
  81.8 4.9 all-to-all-start.2
  87.3 7.3 shard_map.51
  94.6 40.3 %all-to-all-done.2 = f32[4,2,1024,128]{3,2,1,0:T(8,128)} async-done(((f32[4,2,1024,128]{3,2,1,0:T(8,128)}), f32[4,2,1024,128]{3,2,1,0:T(8,128)}, u32[]{:S(2)}, u32[]{:S(2)}) %all-to-all-start.2) | async-done | bytes 4194336 | tf_op jit(solution)/shard_map/all_to_all | solution.py:372
  134.9 4.9 all-to-all-start.4
  140.5 7.3 shard_map.53
  147.8 40.2 %all-to-all-done.4 = f32[4,2,1024,128]{3,2,1,0:T(8,128)} async-done(((f32[4,2,1024,128]{3,2,1,0:T(8,128)}), f32[4,2,1024,128]{3,2,1,0:T(8,128)}, u32[]{:S(2)}, u32[]{:S(2)}) %all-to-all-start.4) | async-done | bytes 4194336 | tf_op jit(solution)/shard_map/all_to_all | solution.py:372
  188.0 4.8 all-to-all-start.6
  193.6 0.7 reshape_squeeze.12.place_ref
  195.5 50.3 %all-gather.2.cloned.1.call-done.rest_0_.rest_1_.rest_2_.rest_3_.rest_4_.rest_5_.rest_6_.rest_7_ = f32[32,128,1024]{2,1,0:T(8,128)} async-done(((f32[4,128,1024]{2,1,0:T(8,128)}), f32[32,128,1024]{2,1,0:T(8,128)}) %all-gather.2.cloned.1.call-update) | async-done | bytes 16777232 | tf_op jit(solution)/shard_map/all_gather | solution.py:367
  245.8 21.7 %shard_map.48 = f32[16,2,2,128,128]{4,3,2,1,0:T(8,128)} custom-call(s32[16]{0:T(128)} %get-tuple-element.30.child_ref, s32[16]{0:T(128)} %and_select_fusion.3.block_ref, s32[16]{0:T(128)} %get-tuple-element.29.mine_ref, s32[8]{0:T(128)} %reshape_squeeze.12.place_ref, f32[1024,1024]{1,0:T(8,128)} %bitcast.74, f32[1024,1024]{1,0:T(8,128)} %collective-permute-done.other_ref, ...), custom_call_target="tpu_custom_call" | custom-call | flops 6442450944 | bytes 29360128 | tf_op jit(solution)/shard_map/pallas_call | solution.py:123
  267.5 7.0 all-to-all-start.1
  275.1 21.7 %shard_map.50 = f32[16,2,2,128,128]{4,3,2,1,0:T(8,128)} custom-call(s32[16]{0:T(128)} %get-tuple-element.30.child_ref, s32[16]{0:T(128)} %and_select_fusion.3.block_ref, s32[16]{0:T(128)} %get-tuple-element.29.mine_ref, s32[8]{0:T(128)} %reshape_squeeze.13.place_ref, f32[1024,1024]{1,0:T(8,128)} %bitcast.75, f32[1024,1024]{1,0:T(8,128)} %collective-permute-done.other_ref, ...), custom_call_target="tpu_custom_call" | custom-call | flops 6442450944 | bytes 29360128 | tf_op jit(solution)/shard_map/pallas_call | solution.py:123
  296.8 69.3 %all-to-all-done.1.a0_ref.a1_ref.rest_0_.rest_4_ = f32[16,2,2,128,128]{4,3,2,1,0:T(8,128)} async-done(((f32[16,2,2,128,128]{4,3,2,1,0:T(8,128)}), f32[16,2,2,128,128]{4,3,2,1,0:T(8,128)}, u32[]{:S(2)}, u32[]{:S(2)}) %all-to-all-start.1) | async-done | bytes 4194336 | tf_op jit(solution)/shard_map/all_to_all | solution.py:388
  366.1 6.0 all-to-all-start.3
  372.7 21.7 %shard_map.52 = f32[16,2,2,128,128]{4,3,2,1,0:T(8,128)} custom-call(s32[16]{0:T(128)} %get-tuple-element.30.child_ref, s32[16]{0:T(128)} %and_select_fusion.3.block_ref, s32[16]{0:T(128)} %get-tuple-element.29.mine_ref, s32[8]{0:T(128)} %reshape_squeeze.14.place_ref, f32[1024,1024]{1,0:T(8,128)} %bitcast.76, f32[1024,1024]{1,0:T(8,128)} %collective-permute-done.other_ref, ...), custom_call_target="tpu_custom_call" | custom-call | flops 6442450944 | bytes 29360128 | tf_op jit(solution)/shard_map/pallas_call | solution.py:123
  394.5 68.7 %all-to-all-done.3.rest_1_.rest_5_ = f32[16,2,2,128,128]{4,3,2,1,0:T(8,128)} async-done(((f32[16,2,2,128,128]{4,3,2,1,0:T(8,128)}), f32[16,2,2,128,128]{4,3,2,1,0:T(8,128)}, u32[]{:S(2)}, u32[]{:S(2)}) %all-to-all-start.3) | async-done | bytes 4194336 | tf_op jit(solution)/shard_map/all_to_all | solution.py:388
  463.2 6.1 all-to-all-start.5
  470.8 0.7 squeeze.21.place_ref
  471.5 9.3 %shard_map.55 = f32[1536,256]{1,0:T(8,128)} custom-call(s32[24]{0:T(128)} %max.8.slot_ref, s32[24]{0:T(128)} %reshape.319.valid_ref, s32[2,4]{1,0:T(2,128)} %squeeze.21.place_ref, f32[1536,3072]{1,0:T(8,128)} %root_ref.3, f32[16,2,2,128,128]{4,3,2,1,0:T(8,128)} %all-to-all-done.1.a0_ref.a1_ref.rest_0_.rest_4_, ...), custom_call_target="tpu_custom_call" | custom-call | bytes 7340032 | tf_op jit(solution)/shard_map/pallas_call | solution.py:175
  480.8 4.6 collective-permute-start.6
  485.4 1.0 slice.112
  486.6 1.3 collective-permute-start.1
  488.5 34.0 %collective-permute-done.1 = f32[256,256]{0,1:T(8,128)S(1)} collective-permute-done((f32[256,256]{0,1:T(8,128)S(1)}, f32[256,256]{0,1:T(8,128)S(1)}, u32[]{:S(2)}, u32[]{:S(2)}) %collective-permute-start.1) | collective-permute-done | bytes 262176 | tf_op jit(solution)/shard_map/ppermute | solution.py:395
  522.6 2.0 collective-permute-start.2
  524.8 2.5 collective-permute-start.7
  527.2 21.7 %shard_map.54 = f32[16,2,2,128,128]{4,3,2,1,0:T(8,128)} custom-call(s32[16]{0:T(128)} %get-tuple-element.30.child_ref, s32[16]{0:T(128)} %and_select_fusion.3.block_ref, s32[16]{0:T(128)} %get-tuple-element.29.mine_ref, s32[8]{0:T(128)} %reshape_squeeze.15.place_ref, f32[1024,1024]{1,0:T(8,128)} %bitcast.77, f32[1024,1024]{1,0:T(8,128)} %collective-permute-done.other_ref, ...), custom_call_target="tpu_custom_call" | custom-call | flops 6442450944 | bytes 29360128 | tf_op jit(solution)/shard_map/pallas_call | solution.py:123
  548.9 11.3 %all-to-all-done.5.rest_2_.rest_6_ = f32[16,2,2,128,128]{4,3,2,1,0:T(8,128)} async-done(((f32[16,2,2,128,128]{4,3,2,1,0:T(8,128)}), f32[16,2,2,128,128]{4,3,2,1,0:T(8,128)}, u32[]{:S(2)}, u32[]{:S(2)}) %all-to-all-start.5) | async-done | bytes 4194336 | tf_op jit(solution)/shard_map/all_to_all | solution.py:388
  560.3 6.0 all-to-all-start.7
  566.4 0.7 collective-permute-start.3
  567.1 0.7 collective-permute-start.4
  568.0 0.7 reshape.289.place_ref
  569.4 1.3 collective-permute-start.5
  570.9 1.3 collective-permute-start.8
  572.2 1.8 collective-permute-start.9
  574.1 1.8 collective-permute-start.10
  575.9 126.4 %collective-permute-done.5 = f32[256,256]{0,1:T(8,128)S(1)} collective-permute-done((f32[256,256]{0,1:T(8,128)S(1)}, f32[256,256]{0,1:T(8,128)S(1)}, u32[]{:S(2)}, u32[]{:S(2)}) %collective-permute-start.5) | collective-permute-done | bytes 262176 | tf_op jit(solution)/shard_map/ppermute | solution.py:404
  702.5 11.7 %cholesky.50 = f32[128,128]{1,0:T(8,128)S(1)} custom-call(f32[128,128]{1,0:T(8,128)S(1)} %cholesky.118), custom_call_target="Cholesky" | custom-call | tf_op jit(solution)/shard_map/jit(cholesky)/cholesky | solution.py:407
  714.3 9.8 %custom-call.14 = f32[1,128,128]{1,2,0:T(8,128)S(1)} custom-call(f32[1,128,128]{2,1,0:T(8,128)S(1)} %get-tuple-element.38), custom_call_target="InvertDiagBlocksLowerTriangular" | custom-call | tf_op jit(solution)/shard_map/jit(cholesky)/cholesky | solution.py:407
  724.6 11.7 %cholesky.105 = f32[128,128]{1,0:T(8,128)S(1)} custom-call(f32[128,128]{1,0:T(8,128)S(1)} %slice_subtract_fusion), custom_call_target="Cholesky" | custom-call | tf_op jit(solution)/shard_map/jit(cholesky)/cholesky | solution.py:407
  736.9 0.7 compare_reduce_fusion
  739.0 0.7 fusion.5
  739.7 1.8 select_select_fusion
  741.6 0.7 collective-permute-start.11
  742.3 7.2 while.1
  743.0 2.9 bitcast_dynamic-update-slice_fusion.2
  746.6 2.9 bitcast_dynamic-update-slice_fusion.2
  749.5 21.1 %custom-call.15 = f32[2,128,128]{1,2,0:T(8,128)} custom-call(f32[2,128,128]{2,1,0:T(8,128)} %get-tuple-element.12), custom_call_target="InvertDiagBlocksLowerTriangular" | custom-call | tf_op jit(solution)/shard_map/triangular_solve | solution.py:408
  770.6 1.1 fusion.7
  771.7 1.1 convolution_subtract_fusion
  772.8 1.1 fusion.10
  773.9 1.4 fusion.6
  775.5 1.2 pad_maximum_fusion.rest_8_
  776.7 1.3 collective-permute-done.11
  778.1 1.6 broadcast_select_fusion.1
  779.7 4.3 fusion.rest_9_
  784.0 30.4 %shard_map.56 = f32[1536,3072]{1,0:T(8,128)} custom-call(s32[24]{0:T(128)} %max.8.slot_ref, s32[24]{0:T(128)} %reshape.319.valid_ref, s32[2,16]{1,0:T(2,128)} %reshape.289.place_ref, s32[2]{0:T(128)} %add_convert_fusion.flag_ref, f32[1536,3072]{1,0:T(8,128)} %root_ref.3, f32[16,2,2,128,128]{4,3,2,1,0:T(8,128)} %all-to-all-done.1.a0_ref.a1_ref.rest_0_.rest_4_, ...), custom_call_target="tpu_custom_call" | custom-call | flops 7247757312 | bytes 54525952 | tf_op jit(solution)/shard_map/pallas_call | solution.py:243
  (118 shorter events, 16.2 us)
Async XLA Ops:
  6.5 239.2 %all-gather.2.cloned.1.call-start = ((), (), s32[]{:S(2)}) async-start(), calls=%async_computation.8 | async-start | bytes 18874368 | tf_op jit(solution)/shard_map/all_gather | solution.py:367
  6.5 7.5 collective-permute-start
  7.3 11.7 %copy-start.1 = (s32[2,8,8]{2,1,0:T(8,128)}, s32[2,8,8]{2,1,0:T(8,128)S(1)}, u32[]{:S(2)}) copy-start(s32[2,8,8]{2,1,0:T(8,128)S(1)} %eq.171) | copy-start | bytes 1540
  8.3 0.6 copy-start.3
  19.0 0.7 copy-start.5
  28.6 53.2 %all-to-all-start = ((f32[4,2,1024,128]{3,2,1,0:T(8,128)}), f32[4,2,1024,128]{3,2,1,0:T(8,128)}, u32[]{:S(2)}, u32[]{:S(2)}) async-start(f32[4,2,1024,128]{3,2,1,0:T(8,128)} %shard_map.46), calls=%async_computation | async-start | bytes 8388608 | tf_op jit(solution)/shard_map/all_to_all | solution.py:372
  81.8 53.1 %all-to-all-start.2 = ((f32[4,2,1024,128]{3,2,1,0:T(8,128)}), f32[4,2,1024,128]{3,2,1,0:T(8,128)}, u32[]{:S(2)}, u32[]{:S(2)}) async-start(f32[4,2,1024,128]{3,2,1,0:T(8,128)} %shard_map.49), calls=%async_computation.2 | async-start | bytes 8388608 | tf_op jit(solution)/shard_map/all_to_all | solution.py:372
  134.9 53.2 %all-to-all-start.4 = ((f32[4,2,1024,128]{3,2,1,0:T(8,128)}), f32[4,2,1024,128]{3,2,1,0:T(8,128)}, u32[]{:S(2)}, u32[]{:S(2)}) async-start(f32[4,2,1024,128]{3,2,1,0:T(8,128)} %shard_map.51), calls=%async_computation.4 | async-start | bytes 8388608 | tf_op jit(solution)/shard_map/all_to_all | solution.py:372
  188.0 79.4 %all-to-all-start.6 = ((f32[4,2,1024,128]{3,2,1,0:T(8,128)}), f32[4,2,1024,128]{3,2,1,0:T(8,128)}, u32[]{:S(2)}, u32[]{:S(2)}) async-start(f32[4,2,1024,128]{3,2,1,0:T(8,128)} %shard_map.53), calls=%async_computation.6 | async-start | bytes 8388608 | tf_op jit(solution)/shard_map/all_to_all | solution.py:372
  267.5 98.6 %all-to-all-start.1 = ((f32[16,2,2,128,128]{4,3,2,1,0:T(8,128)}), f32[16,2,2,128,128]{4,3,2,1,0:T(8,128)}, u32[]{:S(2)}, u32[]{:S(2)}) async-start(f32[16,2,2,128,128]{4,3,2,1,0:T(8,128)} %shard_map.48), calls=%async_computation.1 | async-start | bytes 8388608 | tf_op jit(solution)/shard_map/all_to_all | solution.py:388
  366.1 97.1 %all-to-all-start.3 = ((f32[16,2,2,128,128]{4,3,2,1,0:T(8,128)}), f32[16,2,2,128,128]{4,3,2,1,0:T(8,128)}, u32[]{:S(2)}, u32[]{:S(2)}) async-start(f32[16,2,2,128,128]{4,3,2,1,0:T(8,128)} %shard_map.50), calls=%async_computation.3 | async-start | bytes 8388608 | tf_op jit(solution)/shard_map/all_to_all | solution.py:388
  394.5 74.8 %copy-start.4 = (s32[8,16]{1,0:T(8,128)S(1)}, s32[8,16]{1,0:T(8,128)}, u32[]{:S(2)}) copy-start(s32[8,16]{1,0:T(8,128)} %copy-done.3) | copy-start | bytes 1540
  394.5 75.0 %copy-start.2 = (s32[2,8,8]{2,1,0:T(8,128)S(1)}, s32[2,8,8]{2,1,0:T(8,128)}, u32[]{:S(2)}) copy-start(s32[2,8,8]{2,1,0:T(8,128)} %copy-done.1) | copy-start | bytes 1540
  463.2 97.1 %all-to-all-start.5 = ((f32[16,2,2,128,128]{4,3,2,1,0:T(8,128)}), f32[16,2,2,128,128]{4,3,2,1,0:T(8,128)}, u32[]{:S(2)}, u32[]{:S(2)}) async-start(f32[16,2,2,128,128]{4,3,2,1,0:T(8,128)} %shard_map.52), calls=%async_computation.5 | async-start | bytes 8388608 | tf_op jit(solution)/shard_map/all_to_all | solution.py:388
  480.8 43.8 %copy-start = (f32[1536,256]{1,0:T(8,128)S(1)}, f32[1536,256]{1,0:T(8,128)}, u32[]{:S(2)}) copy-start(f32[1536,256]{1,0:T(8,128)} %shard_map.55) | copy-start | bytes 4718596
  480.8 43.7 %collective-permute-start.6 = (f32[1536,256]{1,0:T(8,128)}, f32[1536,256]{1,0:T(8,128)}, u32[]{:S(2)}, u32[]{:S(2)}) collective-permute-start(f32[1536,256]{1,0:T(8,128)} %shard_map.55), channel_id=1, source_target_pairs={{0,1},{2,3},{4,5},{6,7},{8,9},{10,11},{12,13},{14,15},{16,17},{18,... | collective-permute-start | bytes 4718600 | tf_op jit(solution)/shard_map/ppermute | solution.py:395
  486.6 36.0 %collective-permute-start.1 = (f32[256,256]{0,1:T(8,128)S(1)}, f32[256,256]{0,1:T(8,128)S(1)}, u32[]{:S(2)}, u32[]{:S(2)}) collective-permute-start(f32[256,256]{0,1:T(8,128)S(1)} %copy.74), channel_id=1, source_target_pairs={{0,1},{2,3},{4,5},{6,7},{8,9},{10,11},{12,13},{14,15},{16,17},{18,... | collective-permute-start | bytes 786440 | tf_op jit(solution)/shard_map/ppermute | solution.py:395
  522.6 43.8 %collective-permute-start.2 = (f32[256,256]{0,1:T(8,128)S(1)}, f32[256,256]{0,1:T(8,128)}, u32[]{:S(2)}, u32[]{:S(2)}) collective-permute-start(f32[256,256]{0,1:T(8,128)S(1)} %broadcast_select_fusion.4), channel_id=1, source_target_pairs={{0,16},{1,17},{2,18},{3,19},{4,20},{5,21},{6,22},{7,23},{8,24},{9,... | collective-permute-start | bytes 786440 | tf_op jit(solution)/shard_map/ppermute | solution.py:398
  524.8 45.9 %collective-permute-start.7 = (f32[1536,256]{1,0:T(8,128)S(1)}, f32[1536,256]{1,0:T(8,128)}, u32[]{:S(2)}, u32[]{:S(2)}) collective-permute-start(f32[1536,256]{1,0:T(8,128)S(1)} %broadcast_select_fusion.2), channel_id=1, source_target_pairs={{0,16},{1,17},{2,18},{3,19},{4,20},{5,21},{6,22},{7,23},{8,24},{9,... | collective-permute-start | bytes 4718600 | tf_op jit(solution)/shard_map/ppermute | solution.py:398
  560.3 223.7 %all-to-all-start.7 = ((f32[16,2,2,128,128]{4,3,2,1,0:T(8,128)}), f32[16,2,2,128,128]{4,3,2,1,0:T(8,128)}, u32[]{:S(2)}, u32[]{:S(2)}) async-start(f32[16,2,2,128,128]{4,3,2,1,0:T(8,128)} %shard_map.54), calls=%async_computation.7 | async-start | bytes 8388608 | tf_op jit(solution)/shard_map/all_to_all | solution.py:388
  566.4 0.7 collective-permute-start.3
  567.1 2.2 collective-permute-start.4
  569.4 132.8 %collective-permute-start.5 = (f32[256,256]{0,1:T(8,128)S(1)}, f32[256,256]{0,1:T(8,128)S(1)}, u32[]{:S(2)}, u32[]{:S(2)}) collective-permute-start(f32[256,256]{0,1:T(8,128)S(1)} %broadcast_select_fusion.7), channel_id=1, source_target_pairs={{0,8},{2,10},{4,12},{6,14},{1,9},{3,11},{5,13},{7,15},{16,24},{18,... | collective-permute-start | bytes 786440 | tf_op jit(solution)/shard_map/ppermute | solution.py:404
  570.9 168.8 %collective-permute-start.8 = (f32[1536,256]{1,0:T(8,128)S(1)}, f32[1536,256]{1,0:T(8,128)}, u32[]{:S(2)}, u32[]{:S(2)}) collective-permute-start(f32[1536,256]{1,0:T(8,128)S(1)} %broadcast_select_fusion.3), channel_id=1, source_target_pairs={{0,12},{2,14},{5,1},{7,3},{24,20},{26,22},{29,25},{31,27}} | collective-permute-start | bytes 4718600 | tf_op jit(solution)/shard_map/ppermute | solution.py:422
  572.2 167.5 %collective-permute-start.9 = (f32[1536,256]{1,0:T(8,128)S(1)}, f32[1536,256]{1,0:T(8,128)}, u32[]{:S(2)}, u32[]{:S(2)}) collective-permute-start(f32[1536,256]{1,0:T(8,128)S(1)} %broadcast_select_fusion.3), channel_id=1, source_target_pairs={{0,8},{2,10},{5,13},{7,15},{24,16},{26,18},{29,21},{31,23}} | collective-permute-start | bytes 4718600 | tf_op jit(solution)/shard_map/ppermute | solution.py:422
  574.1 165.7 %collective-permute-start.10 = (f32[1536,256]{1,0:T(8,128)S(1)}, f32[1536,256]{1,0:T(8,128)}, u32[]{:S(2)}, u32[]{:S(2)}) collective-permute-start(f32[1536,256]{1,0:T(8,128)S(1)} %broadcast_select_fusion.3), channel_id=1, source_target_pairs={{0,4},{2,6},{5,9},{7,11},{24,28},{26,30},{29,17},{31,19}} | collective-permute-start | bytes 4718600 | tf_op jit(solution)/shard_map/ppermute | solution.py:422
  741.6 36.5 %collective-permute-start.11 = (f32[1536,256]{1,0:T(8,128)S(1)}, f32[1536,256]{1,0:T(8,128)}, u32[]{:S(2)}, u32[]{:S(2)}) collective-permute-start(f32[1536,256]{1,0:T(8,128)S(1)} %select_select_fusion), channel_id=1, source_target_pairs={{0,2},{2,0},{4,6},{6,4},{8,10},{10,8},{12,14},{14,12},{1,3},{3,1},... | collective-permute-start | bytes 4718600 | tf_op jit(solution)/shard_map/ppermute | solution.py:429
Sparse Core Ops, SparseCore 0:
  19.2 226.5 all-gather.1

commit v2 on v1

--- a/solution.py
+++ b/solution.py
@@ -38,21 +38,25 @@
     rows = update.shape[0]
     groups, width = chosen.shape
 
-    def body(chosen_ref, in_ref, out_ref):
-        out_ref[0, 0] = in_ref[...]
+    def body(chosen_ref, *refs):
+        for d in range(groups):
+            refs[groups + d][0] = refs[d][...]
+
+    def source(d):
+        return pl.BlockSpec((rows, BLK), lambda u, s: (0, s[d * width + u]))
 
     return pl.pallas_call(
         body,
         grid_spec=pltpu.PrefetchScalarGridSpec(
             num_scalar_prefetch=1,
-            grid=(groups, width),
-            in_specs=[pl.BlockSpec((rows, BLK), lambda g, u, s: (0, s[g * width + u]))],
-            out_specs=pl.BlockSpec((1, 1, rows, BLK), lambda g, u, s: (g, u, 0, 0)),
-        ),
-        out_shape=jax.ShapeDtypeStruct((groups, width, rows, BLK), F32),
+            grid=(width,),
+            in_specs=[source(d) for d in range(groups)],
+            out_specs=[pl.BlockSpec((1, rows, BLK), lambda u, s: (u, 0, 0))] * groups,
+        ),
+        out_shape=[jax.ShapeDtypeStruct((width, rows, BLK), F32)] * groups,
         compiler_params=params(),
         cost_estimate=cost(0, 8 * groups * width * rows * BLK),
-    )(chosen.reshape(-1), update)
+    )(chosen.reshape(-1), *([update] * groups))
 
 
 def pick_rows(own, other, block, mine):
@@ -85,68 +89,125 @@
     )(block, mine, own, other)
 
 
-def schur_rows(own, other, columns, panel_blocks, child, block, mine, places):
-    slots = child.shape[0]
+def schur_rows(own, other, arrived, panels, half, item_slot, sources, places, origins, slots, col_count):
+    groups = len(arrived)
     depth = own.shape[1]
-    _, col_count, width, rows, _ = columns.shape
-    wide = col_count * width * BLK
+    width, rows, _ = arrived[0].shape
+    child_blocks = rows // BLK
+    tall = 2 if child_blocks % 2 == 0 else 1
+    steps = child_blocks // tall
     per_child = col_count * width
-
-    def body(child_ref, block_ref, mine_ref, place_ref, own_ref, other_ref, col_ref, *rest):
-        b_refs = rest[: 2 * per_child]
-        out_ref, hi_ref, lo_ref = rest[2 * per_child :]
-        s = pl.program_id(0)
-
-        @pl.when(s == 0)
-        def _():
-            for k in range(2 * per_child):
-                at = pl.ds((k % per_child) * BLK, BLK)
-                hi, lo = split(b_refs[k][0])
-                hi_ref[k // per_child, at, :] = hi
-                lo_ref[k // per_child, at, :] = lo
-
-        c = child_ref[s]
-        rows_f32 = jnp.where(mine_ref[s] == 1, own_ref[...], other_ref[...])
-        a_hi, a_lo = split(rows_f32)
-        both = dot_nt(jnp.concatenate([a_hi, a_lo], axis=0), hi_ref[c])
-        total = both[:BLK] + both[BLK:] + dot_nt(a_hi, lo_ref[c])
-        for q in range(col_count):
-            for u in range(width):
-                k = q * width + u
-                out_ref[0, q, u] = col_ref[0, q, u] - total[:, k * BLK : (k + 1) * BLK]
-
-    row_spec = pl.BlockSpec((BLK, depth), lambda s, c, b, m, p: (b[s], 0))
-    b_specs = [
-        pl.BlockSpec((1, BLK, depth), functools.partial(lambda k, s, c, b, m, p: (p[k], 0, 0), k))
-        for k in range(2 * per_child)
-    ]
+    wide = per_child * BLK
+    count = len(panels)
+    piece = next(w for w in (512, 384, 256, 128) if wide % w == 0)
+
+    def body(half_ref, slot_ref, source_ref, place_ref, origin_ref, own_ref, other_ref, *rest):
+        in_refs = rest[:groups]
+        panel_refs = rest[groups : groups + count]
+        out_ref, staged, hi_ref, lo_ref, total_ref, result, load_sem, store_sem = rest[groups + count :]
+        c = pl.program_id(0)
+        step = c * steps + pl.program_id(1)
+
+        @pl.when(step == 0)
+        def _():
+            @pl.loop(0, 2 * per_child)
+            def _(k):
+                for a in range(count):
+
+                    @pl.when(source_ref[k] == a)
+                    def _():
+                        pltpu.make_async_copy(
+                            panel_refs[a].at[place_ref[k]], staged.at[k], load_sem.at[k]
+                        ).start()
+
+            @pl.loop(0, 2 * per_child)
+            def _(k):
+                pltpu.make_async_copy(panel_refs[0].at[0], staged.at[k], load_sem.at[k]).wait()
+                hi, lo = split(staged[k])
+                hi_ref[k] = hi
+                lo_ref[k] = lo
+
+        a_hi, a_lo = split(jnp.where(c == half_ref[0], own_ref[...], other_ref[...]))
+        stacked = jnp.concatenate([a_hi, a_lo], axis=0)
+        high = tall * BLK
+        at_once = piece // BLK
+        for n in range(0, per_child, at_once):
+            at = pl.ds(c * per_child + n, at_once)
+            both = dot_nt(stacked, hi_ref[at].reshape(piece, depth))
+            total = both[:high] + both[high:] + dot_nt(a_hi, lo_ref[at].reshape(piece, depth))
+            for k in range(at_once):
+                total_ref[n + k] = total[:, k * BLK : (k + 1) * BLK]
+
+        buffer = step % 2
+
+        def store(m, at_step):
+            item = at_step * tall + m
+            return pltpu.make_async_copy(
+                result.at[at_step % 2, m], out_ref.at[slot_ref[item]], store_sem.at[at_step % 2, m]
+            )
+
+        @pl.when(step >= 2)
+        def _():
+            for m in range(tall):
+                store(m, step - 2).wait()
+
+        for d in range(groups):
+
+            @pl.when(origin_ref[d] // col_count == c)
+            def _():
+                q = origin_ref[d] % col_count
+                for u in range(width):
+                    for m in range(tall):
+                        at = slice(m * BLK, (m + 1) * BLK)
+                        result[buffer, m, q, u] = in_refs[d][u, at, :] - total_ref[q * width + u, at, :]
+
+        for m in range(tall):
+            store(m, step).start()
+
+        @pl.when(step == 2 * steps - 1)
+        def _():
+            for m in range(tall):
+                if steps > 0:
+                    store(m, step - 1).wait()
+                store(m, step).wait()
+
+    def stay(c, i, mine):
+        return jnp.where(c == mine, i, jnp.where(c < mine, 0, steps - 1))
+
+    def arrival(d):
+        return pl.BlockSpec(
+            (width, tall * BLK, BLK),
+            lambda c, i, h, t, s, p, o: (0, stay(c, i, o[d] // col_count), 0),
+        )
+
     return pl.pallas_call(
         body,
         grid_spec=pltpu.PrefetchScalarGridSpec(
-            num_scalar_prefetch=4,
-            grid=(slots,),
+            num_scalar_prefetch=5,
+            grid=(2, steps),
             in_specs=[
-                row_spec,
-                row_spec,
-                pl.BlockSpec(
-                    (1, col_count, width, BLK, BLK), lambda s, c, b, m, p: (c[s], 0, 0, b[s], 0)
-                ),
+                pl.BlockSpec((tall * BLK, depth), lambda c, i, h, t, s, p, o: (stay(c, i, h[0]), 0)),
+                pl.BlockSpec((tall * BLK, depth), lambda c, i, h, t, s, p, o: (stay(c, i, 1 - h[0]), 0)),
             ]
-            + b_specs,
-            out_specs=pl.BlockSpec(
-                (1, col_count, width, BLK, BLK), lambda s, c, b, m, p: (s, 0, 0, 0, 0)
-            ),
+            + [arrival(d) for d in range(groups)]
+            + [pl.BlockSpec(memory_space=pl.ANY)] * count,
+            out_specs=pl.BlockSpec(memory_space=pl.ANY),
             scratch_shapes=[
-                pltpu.VMEM((2, wide, depth), BF16),
-                pltpu.VMEM((2, wide, depth), BF16),
+                pltpu.VMEM((2 * per_child, BLK, depth), F32),
+                pltpu.VMEM((2 * per_child, BLK, depth), BF16),
+                pltpu.VMEM((2 * per_child, BLK, depth), BF16),
+                pltpu.VMEM((per_child, tall * BLK, BLK), F32),
+                pltpu.VMEM((2, tall, col_count, width, BLK, BLK), F32),
+                pltpu.SemaphoreType.DMA((2 * per_child,)),
+                pltpu.SemaphoreType.DMA((2, tall)),
             ],
         ),
         out_shape=jax.ShapeDtypeStruct((slots, col_count, width, BLK, BLK), F32),
         compiler_params=params(),
         cost_estimate=cost(
-            6 * slots * BLK * wide * depth, slots * BLK * (2 * depth + 2 * wide) * 4 + 8 * wide * depth
-        ),
-    )(child, block, mine, places, own, other, columns, *([panel_blocks] * (2 * per_child)))
+            12 * rows * wide * depth, 8 * rows * (depth + 2 * wide) + 8 * wide * depth
+        ),
+    )(half.reshape(1), item_slot, sources, places, origins, own, other, *arrived, *panels)
 
 
 def first_panel(root, part, row_slot, row_valid, col_place):
@@ -186,7 +247,7 @@
     )(row_slot, row_valid, col_place, root, part, part)
 
 
-def finish(root, parts, own_rows, columns, row_slot, row_valid, col_place, flags):
+def advance(root, parts, own_rows, columns, row_slot, row_valid, col_place, flags):
     rows, cols = root.shape
     row_blocks = rows // BLK
     count = len(parts)
@@ -259,6 +320,47 @@
         compiler_params=params(),
         cost_estimate=cost(6 * rows * cols * RP, 8 * rows * cols + 4 * sum(p.size for p in parts)),
     )(row_slot, row_valid, col_place, flags, root, *parts, *parts, own_rows, columns)
+
+
+def deliver(root, part, row_slot, row_valid, col_place):
+    rows, cols = root.shape
+    row_blocks = rows // BLK
+    _, col_count, width, _, _ = part.shape
+
+    def body(slot_ref, valid_ref, place_ref, root_ref, a0_ref, a1_ref, out_ref):
+        r = pl.program_id(0)
+        out_ref[...] = root_ref[...]
+        for c, a_ref in enumerate((a0_ref, a1_ref)):
+
+            @pl.when(valid_ref[c * row_blocks + r] == 1)
+            def _():
+                for q in range(col_count):
+                    for u in range(width):
+                        col = place_ref[c, q * width + u]
+
+                        @pl.when(col >= 0)
+                        def _():
+                            at = pl.ds(pl.multiple_of(col * BLK, BLK), BLK)
+                            out_ref[:, at] += a_ref[0, q, u]
+
+    def arrived(c):
+        return pl.BlockSpec(
+            (1, col_count, width, BLK, BLK), lambda r, s, v, p: (s[c * row_blocks + r], 0, 0, 0, 0)
+        )
+
+    whole = pl.BlockSpec((BLK, cols), lambda r, s, v, p: (r, 0))
+    return pl.pallas_call(
+        body,
+        grid_spec=pltpu.PrefetchScalarGridSpec(
+            num_scalar_prefetch=3,
+            grid=(row_blocks,),
+            in_specs=[whole, arrived(0), arrived(1)],
+            out_specs=whole,
+        ),
+        out_shape=jax.ShapeDtypeStruct((rows, cols), F32),
+        compiler_params=params(),
+        cost_estimate=cost(0, 8 * rows * cols + 4 * part.size),
+    )(row_slot, row_valid, col_place, root, part, part)
 
 
 def shards(child_update, child_panel, root_front, index_map):
@@ -279,8 +381,9 @@
     cap_col = max(1, col_blocks // group_count)
     cap_row = max(1, 2 * child_blocks // row_count)
     cap_pick = cap_row * ratio
-    width = 2 if cap_col % 2 == 0 else 1
-    chunks = cap_col // width
+    widths = [cap_col] if cap_col <= 2 else [2, cap_col - 2]
+    spans = [(sum(widths[:j]), w) for j, w in enumerate(widths)]
+    band = 2 if row_count % 2 == 0 else 1
     iota = functools.partial(jnp.arange, dtype=jnp.int32)
     own_panel = child_panel[0]
     other_panel = lax.ppermute(own_panel, "half", [(0, 1), (1, 0)])
@@ -325,35 +428,22 @@
         ),
         axis=1,
     )
-    send_item = jnp.sum(
-        jnp.where(
-            (own_owner * cap_row + own_row_rank)[None, :] == iota(row_count * cap_row)[:, None],
-            iota(items),
-            0,
-        ),
-        axis=1,
-    )
-
-    def to_child(item):
-        child = item // child_blocks
-        return child, item % child_blocks, (child == half).astype(jnp.int32)
-
-    slot_of = (iota(row_count)[:, None] * cap_pick + pick_rank).reshape(
-        row_count, 2, child_blocks
-    )
-    slot_of = slot_of.transpose(1, 0, 2).reshape(2, col_count, col_blocks)
+    item_slot = own_owner * cap_row + own_row_rank
+
+    spread_z, spread_x = iota(row_count) // band - prow // band, (iota(row_count) - prow) % band
+    source = jnp.where(
+        spread_z == 0,
+        spread_x,
+        band * (2 * jnp.abs(spread_z) - 1 + (spread_z > 0)) + spread_x,
+    )
+    code = (source[:, None] * cap_pick + pick_rank).reshape(row_count, 2, child_blocks)
+    slot_of = code.transpose(1, 0, 2).reshape(2, col_count, col_blocks)
     match = col_key[:, :, None, :] == (group * cap_col + iota(cap_col))[:, None]
     place = jnp.sum(jnp.where(match, slot_of[:, :, None, :], 0), axis=-1)
     col_local = (
         jnp.sum(jnp.where(match, by_col[:, :, None, :] - group * group_cols + 1, 0), axis=-1) - 1
     )
 
-    def chunked(table):
-        table = table.reshape(2, col_count, chunks, width).transpose(2, 0, 1, 3)
-        return table.reshape(chunks, 2, col_count * width)
-
-    place = chunked(place)
-    col_local = chunked(col_local)
     row_slot = (iota(row_count)[:, None] * cap_row + row_rank).reshape(row_count, 2, child_blocks)
     row_match = by_row[..., None] == prow * row_blocks + iota(row_blocks)
     row_slot = jnp.sum(
@@ -362,60 +452,92 @@
     row_valid = (row_slot > 0).astype(jnp.int32).reshape(-1)
     row_slot = jnp.maximum(row_slot - 1, 0).reshape(-1)
 
-    _, pick_block, pick_mine = to_child(pick_item)
-    picked = pick_rows(own_panel, other_panel, pick_block, pick_mine)
-    panel_blocks = lax.all_gather(picked, "prow", axis=0, tiled=True)
-
-    columns = []
-    for j in range(chunks):
-        packed = pack_columns(child_update[0], chosen[:, j * width : (j + 1) * width])
-        got = lax.all_to_all(packed, ("half", "pcol"), split_axis=0, concat_axis=0, tiled=True)
-        columns.append(got.reshape(2, col_count, width, rows_dev, BLK))
-
-    send_child, send_block, send_mine = to_child(send_item)
-    parts = []
-    for j in range(chunks):
+    pick_mine = (pick_item // child_blocks == half).astype(jnp.int32)
+    picked = pick_rows(own_panel, other_panel, pick_item % child_blocks, pick_mine)
+
+    def across(value, rows_in):
+        return [
+            lax.ppermute(value, "prow", [(r, r - r % band + (r % band - o) % band) for r in rows_in])
+            for o in range(1, band)
+        ]
+
+    rows_all = list(range(row_count))
+    bands = row_count // band
+    panels = [picked] + across(picked, rows_all)
+    up = down = picked
+    for k in range(1, bands):
+        up = lax.ppermute(
+            up, "prow", [(r, r + band) for r in rows_all if k - 1 <= r // band < bands - 1]
+        )
+        down = lax.ppermute(
+            down, "prow", [(r, r - band) for r in rows_all if 0 < r // band <= bands - k]
+        )
+        panels += [up] + across(up, [r for r in rows_all if r // band >= k])
+        panels += [down] + across(down, [r for r in rows_all if r // band < bands - k])
+
+    device = lambda g, r: ((g // col_count) * row_count + r) * col_count + g % col_count
+    everyone = ("half", "prow", "pcol")
+    distance = (group + iota(group_count)) % group_count
+    origins = (group - iota(group_count)) % group_count
+    arrived = []
+    for start, width in spans:
+        packed = pack_columns(child_update[0], chosen[distance, start : start + width])
+        got = [packed[0]]
+        for d in range(1, group_count):
+            pairs = [
+                (device(g, r), device((g + d) % group_count, r))
+                for g in range(group_count)
+                for r in range(row_count)
+            ]
+            got.append(lax.ppermute(packed[d], everyone, pairs))
+        arrived.append(got)
+
+    parts, col_places = [], []
+    for (start, width), got in zip(spans, arrived):
+        codes = place[:, :, start : start + width].reshape(-1)
+        col_places.append(col_local[:, :, start : start + width].reshape(2, -1))
         outgoing = schur_rows(
             own_panel,
             other_panel,
-            columns[j],
-            panel_blocks,
-            send_child,
-            send_block,
-            send_mine,
-            place[j].reshape(-1),
+            got,
+            panels,
+            half,
+            item_slot,
+            codes // cap_pick,
+            codes % cap_pick,
+            origins,
+            row_count * cap_row,
+            col_count,
         )
         parts.append(lax.all_to_all(outgoing, "prow", split_axis=0, concat_axis=0, tiled=True))
 
-    raw = first_panel(root_front, parts[0], row_slot, row_valid, col_local[0])
+    raw = first_panel(root_front, parts[0], row_slot, row_valid, col_places[0])
 
     def to_groups(value):
-        span = 1
-        while span < col_count:
-            got = lax.ppermute(value, "pcol", [(i, i + span) for i in range(min(span, col_count - span))])
-            value = jnp.where((pcol >= span) & (pcol < 2 * span), got, value)
-            span *= 2
-        got = lax.ppermute(value, "half", [(0, 1)])
-        return jnp.where(half == 1, got, value)
-
-    pivot = to_groups(raw[:RP])
-    span = 1
-    while span < row_count:
-        got = lax.ppermute(pivot, "prow", [(i, i + span) for i in range(min(span, row_count - span))])
-        pivot = jnp.where((prow >= span) & (prow < 2 * span), got, pivot)
-        span *= 2
+        total = jnp.where(group == 0, value, 0.0)
+        for g in range(1, group_count):
+            pairs = [(device(0, r), device(g, r)) for r in range(row_count)]
+            total = total + lax.ppermute(value, everyone, pairs)
+        return total
+
+    corner = raw[:RP]
+    first = jnp.where(group == 0, corner, 0.0)
+    for g in range(1, group_count):
+        first = first + lax.ppermute(corner, everyone, [(device(0, 0), device(g, 0))])
+    pivot = jnp.where(prow == 0, first, 0.0)
+    for r in range(1, row_count):
+        pivot = pivot + lax.ppermute(first, "prow", [(0, r)])
     factor = jnp.linalg.cholesky(pivot)
     inverse = lax.linalg.triangular_solve(
         factor, jnp.eye(RP, dtype=F32), left_side=True, lower=True
     )
     raw_rows = to_groups(raw)
-    bands = row_count // ratio
-    device = lambda g, r: ((g // col_count) * row_count + r) * col_count + g % col_count
-    shift = (prow // ratio - group) % bands
+    groups_of = row_count // ratio
+    shift = (prow // ratio - group) % groups_of
     tile = jnp.where(shift == 0, raw_rows, 0.0)
-    for k in range(1, bands):
+    for k in range(1, groups_of):
         pairs = [
-            (device(g, g * ratio + o), device(g, ((g + k) % bands) * ratio + o))
+            (device(g, g * ratio + o), device(g, ((g + k) % groups_of) * ratio + o))
             for g in range(group_count)
             for o in range(ratio)
         ]
@@ -442,8 +564,12 @@
     top = jnp.where(prow == 0, factor, solved[:RP])
     own_rows = jnp.concatenate([top, solved[RP:]], axis=0)
     flags = jnp.stack([(prow == 0), (group == 0)]).astype(jnp.int32)
-    col_all = col_local.transpose(1, 0, 2).reshape(2, -1)
-    return finish(root_front, parts, own_rows, lower_cols, row_slot, row_valid, col_all, flags)
+    root = advance(
+        root_front, parts[:1], own_rows, lower_cols, row_slot, row_valid, col_places[0], flags
+    )
+    for part, col_place in zip(parts[1:], col_places[1:]):
+        root = deliver(root, part, row_slot, row_valid, col_place)
+    return root
 
 
 def solution(mesh):

time: 825 us -> 916 us (1.11)
  the two profiles are of different devices: /device:TPU:24 before, /device:TPU:22 now
where the time goes in v2:
time: 916 us; the launch traced here: 914 us
  waiting for transfers between devices  564 us (62%)
  Pallas kernels  127 us (14%)
  starting transfers between devices  113 us (12%)
  other arithmetic  72.1 us (8%)
  local copies, waits for them, and re-layouts  26.6 us (3%)
  matrix products  9.54 us (1%)
    ppermute x7, waiting for transfers between devices, shards(): pivot = pivot + lax.ppermute(first, 'prow', [(0, r)])  185 us
    ppermute x6, waiting for transfers between devices, shards(): got.append(lax.ppermute(packed[d], everyone, pairs))  180 us
    ppermute x7, waiting for transfers between devices, across(): lax.ppermute(value, 'prow', [(r, r - r % band + (r % band - o) % band) fo...  102 us
    ppermute x3, waiting for transfers between devices, shards(): lax.ppermute(up, 'prow', [(r, r + band) for r in rows_all if k - 1 <= r /...  50.4 us
    pallas_call x2, Pallas kernels, schur_rows(): pl.pallas_call(body, grid_spec=pltpu.PrefetchScalarGridSpec(num_scalar_pr...  50.2 us
    ppermute x3, waiting for transfers between devices, shards(): got = lax.ppermute(raw_rows, ('half', 'prow', 'pcol'), pairs)  37 us
    another operation x7, other arithmetic, shards(): factor = jnp.linalg.cholesky(pivot)  34.6 us
    all_to_all x2, starting transfers between devices, shards(): lax.all_to_all(outgoing, 'prow', split_axis=0, concat_axis=0, tiled=True)  29.6 us
  transfers between devices with their start and end apart: 39, of which 13 were waited for; matrix products, arithmetic and copies ran while one was open for 11% of the time, Pallas kernels for 9%

profile of v2, /device:TPU:22, one launch (start us, length us, event | category | flops | bytes accessed | tf_op | source)
XLA Modules:
  0.0 914.1 jit_solution(616220288243624873)
XLA Ops:
  3.0 4.5 collective-permute-done.other_ref
  7.5 5.0 shard_map.47.rest_4_
  12.5 3.4 collective-permute-start.5
  15.8 2.5 collective-permute-start.7
  18.8 43.4 %collective-permute-done.5.rest_6_ = f32[4,128,1024]{2,1,0:T(8,128)} collective-permute-done((f32[4,128,1024]{2,1,0:T(8,128)}, f32[4,128,1024]{2,1,0:T(8,128)}, u32[]{:S(2)}, u32[]{:S(2)}) %collective-permute-start.5) | collective-permute-done | bytes 2097184 | tf_op jit(solution)/shard_map/ppermute | solution.py:469
  62.2 3.5 collective-permute-start.9
  65.7 5.0 collective-permute-start.11
  73.1 4.5 shard_map.46
  78.8 22.7 %collective-permute-done.1.rest_1_ = f32[2,1024,128]{2,1,0:T(8,128)S(1)} collective-permute-done((f32[2,1024,128]{2,1,0:T(8,128)}, f32[2,1024,128]{2,1,0:T(8,128)S(1)}, u32[]{:S(2)}, u32[]{:S(2)}) %collective-permute-start.1) | collective-permute-done | bytes 1048608 | tf_op jit(solution)/shard_map/ppermute | solution.py:492
  101.5 2.6 collective-permute-start.6
  104.1 7.1 collective-permute-done.9.rest_10_
  111.1 4.9 collective-permute-start.13
  116.1 2.0 collective-permute-start.15
  118.6 24.2 %collective-permute-done.3.rest_3_ = f32[2,1024,128]{2,1,0:T(8,128)S(1)} collective-permute-done((f32[2,1024,128]{2,1,0:T(8,128)}, f32[2,1024,128]{2,1,0:T(8,128)S(1)}, u32[]{:S(2)}, u32[]{:S(2)}) %collective-permute-start.3) | collective-permute-done | bytes 1048608 | tf_op jit(solution)/shard_map/ppermute | solution.py:492
  142.8 2.4 collective-permute-start.8
  145.3 1.4 copy-done.2
  146.6 3.4 collective-permute-start.10
  150.0 21.7 %collective-permute-done.6.rest_7_ = f32[4,128,1024]{2,1,0:T(8,128)} collective-permute-done((f32[4,128,1024]{2,1,0:T(8,128)}, f32[4,128,1024]{2,1,0:T(8,128)}, u32[]{:S(2)}, u32[]{:S(2)}) %collective-permute-start.6) | collective-permute-done | bytes 2097184 | tf_op jit(solution)/shard_map/ppermute | solution.py:460
  171.8 2.0 collective-permute-start.12
  173.8 2.0 collective-permute-start.14
  175.7 2.0 collective-permute-start.16
  180.2 36.5 %collective-permute-done.8.rest_9_ = f32[4,128,1024]{2,1,0:T(8,128)} collective-permute-done((f32[4,128,1024]{2,1,0:T(8,128)}, f32[4,128,1024]{2,1,0:T(8,128)}, u32[]{:S(2)}, u32[]{:S(2)}) %collective-permute-start.8) | collective-permute-done | bytes 2097184 | tf_op jit(solution)/shard_map/ppermute | solution.py:460
  216.7 43.9 %collective-permute-done.10.rest_11_ = f32[4,128,1024]{2,1,0:T(8,128)S(1)} collective-permute-done((f32[4,128,1024]{2,1,0:T(8,128)}, f32[4,128,1024]{2,1,0:T(8,128)S(1)}, u32[]{:S(2)}, u32[]{:S(2)}) %collective-permute-start.10) | collective-permute-done | bytes 2097184 | tf_op jit(solution)/shard_map/ppermute | solution.py:460
  260.6 1.3 copy-done.3
  261.9 16.5 %shard_map.48 = f32[16,2,2,128,128]{4,3,2,1,0:T(8,128)} custom-call(s32[1]{0:T(128)} %bitcast.6.half_ref, s32[16]{0:T(128)} %fusion.34.slot_ref, s32[8]{0:T(128)} %get-tuple-element.79.source_ref, s32[8]{0:T(128)} %get-tuple-element.78.place_ref, s32[4]{0:T(128)} %and_select_fusion.6.origin_ref, f32[1024,1024]{1,0:T(8,128)} %bitcast.84, ...), custom_call_target="tpu_custom_call" | custom-call | flops 6442450944 | bytes 20971520 | tf_op jit(solution)/shard_map/pallas_call | solution.py:183
  278.4 23.5 %all-to-all-start = ((f32[16,2,2,128,128]{4,3,2,1,0:T(8,128)}), f32[16,2,2,128,128]{4,3,2,1,0:T(8,128)}, u32[]{:S(2)}, u32[]{:S(2)}) async-start(f32[16,2,2,128,128]{4,3,2,1,0:T(8,128)} %shard_map.48), calls=%async_computation | async-start | bytes 8388608 | tf_op jit(solution)/shard_map/all_to_all | solution.py:512
  301.9 7.2 while.3
  309.7 11.0 %shard_map.51 = (f32[6,1024,128]{2,1,0:T(8,128)}, f32[6,1024,128]{2,1,0:T(8,128)}, f32[6,1024,128]{2,1,0:T(8,128)}, f32[6,1024,128]{2,1,0:T(8,128)}) custom-call(s32[24]{0:T(128)} %reshape.357.chosen_ref, f32[1024,4096]{1,0:T(8,128)} %bitcast.78, f32[1024,4096]{1,0:T(8,128)} %bitcast.79, f32[1024,4096]{1,0:T(8,128)} %bitcast.80, f32[1024,4096]{1,0:T(8,128)} %bitcast.81), custom_call_target="tpu_custom_call" | custom-call | bytes 25165824 | tf_op jit(solution)/shard_map/pallas_call | solution.py:48
  321.3 1.5 collective-permute-start.36
  323.5 68.5 %collective-permute-done.34.rest_1_ = f32[6,1024,128]{2,1,0:T(8,128)S(1)} collective-permute-done((f32[6,1024,128]{2,1,0:T(8,128)}, f32[6,1024,128]{2,1,0:T(8,128)S(1)}, u32[]{:S(2)}, u32[]{:S(2)}) %collective-permute-start.34) | collective-permute-done | bytes 3145760 | tf_op jit(solution)/shard_map/ppermute | solution.py:492
  392.0 64.8 %collective-permute-done.36.rest_3_ = f32[6,1024,128]{2,1,0:T(8,128)} collective-permute-done((f32[6,1024,128]{2,1,0:T(8,128)}, f32[6,1024,128]{2,1,0:T(8,128)}, u32[]{:S(2)}, u32[]{:S(2)}) %collective-permute-start.36) | collective-permute-done | bytes 3145760 | tf_op jit(solution)/shard_map/ppermute | solution.py:492
  456.8 33.7 %shard_map.52 = f32[16,2,6,128,128]{4,3,2,1,0:T(8,128)} custom-call(s32[1]{0:T(128)} %bitcast.6.half_ref, s32[16]{0:T(128)} %fusion.34.slot_ref, s32[24]{0:T(128)} %get-tuple-element.77.source_ref, s32[24]{0:T(128)} %get-tuple-element.76.place_ref, s32[4]{0:T(128)} %and_select_fusion.6.origin_ref, f32[1024,1024]{1,0:T(8,128)} %bitcast.85, ...), custom_call_target="tpu_custom_call" | custom-call | flops 19327352832 | bytes 46137344 | tf_op jit(solution)/shard_map/pallas_call | solution.py:183
  490.6 6.1 all-to-all-start.1
  498.8 9.4 %shard_map.49 = f32[1536,256]{1,0:T(8,128)} custom-call(s32[24]{0:T(128)} %max.8.slot_ref, s32[24]{0:T(128)} %reshape.396.valid_ref, s32[2,4]{1,0:T(2,128)} %reshape.351.place_ref, f32[1536,3072]{1,0:T(8,128)} %root_ref.3, f32[16,2,2,128,128]{4,3,2,1,0:T(8,128)} %all-to-all-done.a0_ref.a1_ref.rest_0_.rest_1_, ...), custom_call_target="tpu_custom_call" | custom-call | bytes 7340032 | tf_op jit(solution)/shard_map/pallas_call | solution.py:236
  508.2 1.4 collective-permute-start.27
  509.6 1.8 collective-permute-start.28
  511.4 1.8 collective-permute-start.29
  513.2 1.7 slice.99
  514.9 1.4 collective-permute-start.17
  517.0 1.4 collective-permute-start.19
  520.3 1.4 collective-permute-start.20
  521.7 1.4 collective-permute-start.21
  525.8 5.1 collective-permute-done.27
  530.8 1.3 collective-permute-start.24
  533.5 2.8 add_add_fusion
  536.3 1.8 collective-permute-start.30
  538.2 1.8 collective-permute-start.31
  540.0 184.5 %collective-permute-done.24 = f32[256,256]{1,0:T(8,128)S(1)} collective-permute-done((f32[256,256]{1,0:T(8,128)S(1)}, f32[256,256]{1,0:T(8,128)S(1)}, u32[]{:S(2)}, u32[]{:S(2)}) %collective-permute-start.24) | collective-permute-done | bytes 262176 | tf_op jit(solution)/shard_map/ppermute | solution.py:529
  724.5 1.5 collective-permute-start.32
  727.3 11.7 %cholesky.49 = f32[128,128]{1,0:T(8,128)S(1)} custom-call(f32[128,128]{1,0:T(8,128)S(1)} %cholesky.115), custom_call_target="Cholesky" | custom-call | tf_op jit(solution)/shard_map/jit(cholesky)/cholesky | solution.py:530
  739.1 9.8 %custom-call.14 = f32[1,128,128]{1,2,0:T(8,128)S(1)} custom-call(f32[1,128,128]{2,1,0:T(8,128)S(1)} %get-tuple-element.68), custom_call_target="InvertDiagBlocksLowerTriangular" | custom-call | tf_op jit(solution)/shard_map/jit(cholesky)/cholesky | solution.py:530
  749.4 11.7 %cholesky.103 = f32[128,128]{1,0:T(8,128)S(1)} custom-call(f32[128,128]{1,0:T(8,128)S(1)} %slice_subtract_fusion), custom_call_target="Cholesky" | custom-call | tf_op jit(solution)/shard_map/jit(cholesky)/cholesky | solution.py:530
  764.4 37.0 %collective-permute-done.32 = f32[1536,256]{1,0:T(8,128)} collective-permute-done((f32[1536,256]{1,0:T(8,128)S(1)}, f32[1536,256]{1,0:T(8,128)}, u32[]{:S(2)}, u32[]{:S(2)}) %collective-permute-start.32) | collective-permute-done | bytes 1572896 | tf_op jit(solution)/shard_map/ppermute | solution.py:544
  801.3 1.8 select_select_fusion
  803.2 23.9 %collective-permute-start.33 = (f32[1536,256]{1,0:T(8,128)S(1)}, f32[1536,256]{1,0:T(8,128)}, u32[]{:S(2)}, u32[]{:S(2)}) collective-permute-start(f32[1536,256]{1,0:T(8,128)S(1)} %select_select_fusion), channel_id=1, source_target_pairs={{0,2},{2,0},{4,6},{6,4},{8,10},{10,8},{12,14},{14,12},{1,3},{3,1},... | collective-permute-start | bytes 4718600 | tf_op jit(solution)/shard_map/ppermute | solution.py:551
  827.1 6.7 while.2
  827.7 2.8 bitcast_dynamic-update-slice_fusion.2
  831.1 2.7 bitcast_dynamic-update-slice_fusion.2
  833.9 21.1 %custom-call.15 = f32[2,128,128]{1,2,0:T(8,128)} custom-call(f32[2,128,128]{2,1,0:T(8,128)} %get-tuple-element.28), custom_call_target="InvertDiagBlocksLowerTriangular" | custom-call | tf_op jit(solution)/shard_map/triangular_solve | solution.py:531
  858.4 1.4 fusion.6
  861.2 1.6 broadcast_select_fusion.1
  862.8 4.3 fusion.rest_3_
  867.1 24.8 %shard_map.50.root_ref = f32[1536,3072]{1,0:T(8,128)} custom-call(s32[24]{0:T(128)} %max.8.slot_ref, s32[24]{0:T(128)} %reshape.396.valid_ref, s32[2,4]{1,0:T(2,128)} %reshape.351.place_ref, s32[2]{0:T(128)} %add_convert_fusion.flag_ref, f32[1536,3072]{1,0:T(8,128)} %root_ref.3, f32[16,2,2,128,128]{4,3,2,1,0:T(8,128)} %all-to-all-done.a0_ref.a1_ref.rest_0_.rest_1_, ...), custom_call_target="tpu_custom_call" | custom-call | flops 7247757312 | bytes 41943040 | tf_op jit(solution)/shard_map/pallas_call | solution.py:304
  891.9 22.2 %shard_map.53 = f32[1536,3072]{1,0:T(8,128)} custom-call(s32[24]{0:T(128)} %max.8.slot_ref, s32[24]{0:T(128)} %reshape.396.valid_ref, s32[2,12]{1,0:T(2,128)} %reshape.350.place_ref, f32[1536,3072]{1,0:T(8,128)} %shard_map.50.root_ref, f32[16,2,6,128,128]{4,3,2,1,0:T(8,128)} %all-to-all-done.1.a0_ref.a1_ref, f32[16,2,6,128,128]{4,3,2,1,0:T(8,128)} %all-to-all-done.1.a0_ref.a1_ref), custom_call_target="tpu_custom_call" | custom-call | bytes 50331648 | tf_op jit(solution)/shard_map/pallas_call | solution.py:352
  (174 shorter events, 37.8 us)
Async XLA Ops:
  0.0 7.5 collective-permute-start
  3.0 15.3 %copy-start.9 = (s32[2,64]{1,0:T(2,128)S(1)}, s32[2,64]{1,0:T(2,128)}, u32[]{:S(2)}) copy-start(s32[2,64]{1,0:T(2,128)} %param.7) | copy-start | bytes 1540
  3.0 68.0 %copy-start.10 = (s32[2]{0:T(128)S(1)}, s32[2]{0:T(128)}, u32[]{:S(2)}) copy-start(s32[2]{0:T(128)} %constant.278) | copy-start | bytes 28
  12.5 49.8 %collective-permute-start.5 = (f32[4,128,1024]{2,1,0:T(8,128)}, f32[4,128,1024]{2,1,0:T(8,128)}, u32[]{:S(2)}, u32[]{:S(2)}) collective-permute-start(f32[4,128,1024]{2,1,0:T(8,128)} %shard_map.47.rest_4_), channel_id=1, source_target_pairs={{0,4},{2,6},{4,8},{6,10},{8,12},{10,14},{1,5},{3,7},{5,9},{7,11},{... | collective-permute-start | bytes 6291464 | tf_op jit(solution)/shard_map/ppermute | solution.py:469
  15.8 49.9 %collective-permute-start.7 = (f32[4,128,1024]{2,1,0:T(8,128)}, f32[4,128,1024]{2,1,0:T(8,128)}, u32[]{:S(2)}, u32[]{:S(2)}) collective-permute-start(f32[4,128,1024]{2,1,0:T(8,128)} %shard_map.47.rest_4_), channel_id=1, source_target_pairs={{4,0},{6,2},{8,4},{10,6},{12,8},{14,10},{5,1},{7,3},{9,5},{11,7},{... | collective-permute-start | bytes 6291464 | tf_op jit(solution)/shard_map/ppermute | solution.py:472
  62.2 48.9 %collective-permute-start.9 = (f32[4,128,1024]{2,1,0:T(8,128)}, f32[4,128,1024]{2,1,0:T(8,128)}, u32[]{:S(2)}, u32[]{:S(2)}) collective-permute-start(f32[4,128,1024]{2,1,0:T(8,128)} %collective-permute-done.5.rest_6_), channel_id=1, source_target_pairs={{4,8},{6,10},{8,12},{10,14},{5,9},{7,11},{9,13},{11,15},{20,24},{2... | collective-permute-start | bytes 6291464 | tf_op jit(solution)/shard_map/ppermute | solution.py:469
  65.7 50.4 %collective-permute-start.11 = (f32[4,128,1024]{2,1,0:T(8,128)}, f32[4,128,1024]{2,1,0:T(8,128)}, u32[]{:S(2)}, u32[]{:S(2)}) collective-permute-start(f32[4,128,1024]{2,1,0:T(8,128)} %collective-permute-done.7.rest_8_), channel_id=1, source_target_pairs={{4,0},{6,2},{8,4},{10,6},{5,1},{7,3},{9,5},{11,7},{20,16},{22,18},... | collective-permute-start | bytes 6291464 | tf_op jit(solution)/shard_map/ppermute | solution.py:472
  73.1 5.1 copy-start.1
  77.6 23.9 %collective-permute-start.1 = (f32[2,1024,128]{2,1,0:T(8,128)}, f32[2,1024,128]{2,1,0:T(8,128)S(1)}, u32[]{:S(2)}, u32[]{:S(2)}) collective-permute-start(f32[2,1024,128]{2,1,0:T(8,128)} %get-tuple-element.14), channel_id=1, source_target_pairs={{0,1},{2,3},{4,5},{6,7},{8,9},{10,11},{12,13},{14,15},{1,16},{3,18... | collective-permute-start | bytes 3145736 | tf_op jit(solution)/shard_map/ppermute | solution.py:492
  77.6 40.5 %collective-permute-start.2 = (f32[2,1024,128]{2,1,0:T(8,128)}, f32[2,1024,128]{2,1,0:T(8,128)S(1)}, u32[]{:S(2)}, u32[]{:S(2)}) collective-permute-start(f32[2,1024,128]{2,1,0:T(8,128)} %get-tuple-element.15), channel_id=1, source_target_pairs={{0,16},{2,18},{4,20},{6,22},{8,24},{10,26},{12,28},{14,30},{1,17},... | collective-permute-start | bytes 3145736 | tf_op jit(solution)/shard_map/ppermute | solution.py:492
  78.2 67.0 %collective-permute-start.4 = (f32[4,128,1024]{2,1,0:T(8,128)S(1)}, f32[4,128,1024]{2,1,0:T(8,128)S(1)}, u32[]{:S(2)}, u32[]{:S(2)}) collective-permute-start(f32[4,128,1024]{2,1,0:T(8,128)S(1)} %copy-done.1), channel_id=1, source_target_pairs={{0,2},{2,0},{4,6},{6,4},{8,10},{10,8},{12,14},{14,12},{1,3},{3,1},... | collective-permute-start | bytes 6291464 | tf_op jit(solution)/shard_map/ppermute | solution.py:460
  101.5 159.1 %copy-start.5 = (f32[2,1024,128]{2,1,0:T(8,128)}, f32[2,1024,128]{2,1,0:T(8,128)S(1)}, u32[]{:S(2)}) copy-start(f32[2,1024,128]{2,1,0:T(8,128)S(1)} %collective-permute-done.1.rest_1_) | copy-start | bytes 3145732
  101.5 70.3 %collective-permute-start.6 = (f32[4,128,1024]{2,1,0:T(8,128)}, f32[4,128,1024]{2,1,0:T(8,128)}, u32[]{:S(2)}, u32[]{:S(2)}) collective-permute-start(f32[4,128,1024]{2,1,0:T(8,128)} %collective-permute-done.5.rest_6_), channel_id=1, source_target_pairs={{4,6},{6,4},{8,10},{10,8},{12,14},{14,12},{5,7},{7,5},{9,11},{11,9... | collective-permute-start | bytes 6291464 | tf_op jit(solution)/shard_map/ppermute | solution.py:460
  111.1 62.6 %collective-permute-start.13 = (f32[4,128,1024]{2,1,0:T(8,128)}, f32[4,128,1024]{2,1,0:T(8,128)}, u32[]{:S(2)}, u32[]{:S(2)}) collective-permute-start(f32[4,128,1024]{2,1,0:T(8,128)} %collective-permute-done.9.rest_10_), channel_id=1, source_target_pairs={{8,12},{10,14},{9,13},{11,15},{24,28},{26,30},{25,29},{27,31}} | collective-permute-start | bytes 6291464 | tf_op jit(solution)/shard_map/ppermute | solution.py:469
  116.1 59.7 %collective-permute-start.15 = (f32[4,128,1024]{2,1,0:T(8,128)}, f32[4,128,1024]{2,1,0:T(8,128)}, u32[]{:S(2)}, u32[]{:S(2)}) collective-permute-start(f32[4,128,1024]{2,1,0:T(8,128)} %collective-permute-done.11.rest_12_), channel_id=1, source_target_pairs={{4,0},{6,2},{5,1},{7,3},{20,16},{22,18},{21,17},{23,19}} | collective-permute-start | bytes 6291464 | tf_op jit(solution)/shard_map/ppermute | solution.py:472
  118.1 31.9 %copy-start.6 = (f32[2,1024,128]{2,1,0:T(8,128)}, f32[2,1024,128]{2,1,0:T(8,128)S(1)}, u32[]{:S(2)}) copy-start(f32[2,1024,128]{2,1,0:T(8,128)S(1)} %collective-permute-done.2.rest_2_) | copy-start | bytes 3145732
  118.1 24.7 %collective-permute-start.3 = (f32[2,1024,128]{2,1,0:T(8,128)}, f32[2,1024,128]{2,1,0:T(8,128)S(1)}, u32[]{:S(2)}, u32[]{:S(2)}) collective-permute-start(f32[2,1024,128]{2,1,0:T(8,128)} %get-tuple-element.16), channel_id=1, source_target_pairs={{0,17},{2,19},{4,21},{6,23},{8,25},{10,27},{12,29},{14,31},{1,0},{... | collective-permute-start | bytes 3145736 | tf_op jit(solution)/shard_map/ppermute | solution.py:492
  142.8 29.0 %copy-start.7 = (f32[2,1024,128]{2,1,0:T(8,128)}, f32[2,1024,128]{2,1,0:T(8,128)S(1)}, u32[]{:S(2)}) copy-start(f32[2,1024,128]{2,1,0:T(8,128)S(1)} %collective-permute-done.3.rest_3_) | copy-start | bytes 3145732
  142.8 73.9 %collective-permute-start.8 = (f32[4,128,1024]{2,1,0:T(8,128)}, f32[4,128,1024]{2,1,0:T(8,128)}, u32[]{:S(2)}, u32[]{:S(2)}) collective-permute-start(f32[4,128,1024]{2,1,0:T(8,128)} %collective-permute-done.7.rest_8_), channel_id=1, source_target_pairs={{0,2},{2,0},{4,6},{6,4},{8,10},{10,8},{1,3},{3,1},{5,7},{7,5},{9,1... | collective-permute-start | bytes 6291464 | tf_op jit(solution)/shard_map/ppermute | solution.py:460
  145.3 1.4 copy-start.2
  146.6 113.9 %collective-permute-start.10 = (f32[4,128,1024]{2,1,0:T(8,128)}, f32[4,128,1024]{2,1,0:T(8,128)S(1)}, u32[]{:S(2)}, u32[]{:S(2)}) collective-permute-start(f32[4,128,1024]{2,1,0:T(8,128)} %collective-permute-done.9.rest_10_), channel_id=1, source_target_pairs={{8,10},{10,8},{12,14},{14,12},{9,11},{11,9},{13,15},{15,13},{24,26... | collective-permute-start | bytes 6291464 | tf_op jit(solution)/shard_map/ppermute | solution.py:460
  171.8 88.8 %collective-permute-start.12 = (f32[4,128,1024]{2,1,0:T(8,128)}, f32[4,128,1024]{2,1,0:T(8,128)}, u32[]{:S(2)}, u32[]{:S(2)}) collective-permute-start(f32[4,128,1024]{2,1,0:T(8,128)} %collective-permute-done.11.rest_12_), channel_id=1, source_target_pairs={{0,2},{2,0},{4,6},{6,4},{1,3},{3,1},{5,7},{7,5},{16,18},{18,16},{2... | collective-permute-start | bytes 6291464 | tf_op jit(solution)/shard_map/ppermute | solution.py:460
  173.8 86.8 %collective-permute-start.14 = (f32[4,128,1024]{2,1,0:T(8,128)}, f32[4,128,1024]{2,1,0:T(8,128)}, u32[]{:S(2)}, u32[]{:S(2)}) collective-permute-start(f32[4,128,1024]{2,1,0:T(8,128)} %collective-permute-done.13.rest_14_), channel_id=1, source_target_pairs={{12,14},{14,12},{13,15},{15,13},{28,30},{30,28},{29,31},{31,29}} | collective-permute-start | bytes 6291464 | tf_op jit(solution)/shard_map/ppermute | solution.py:460
  175.7 84.9 %collective-permute-start.16 = (f32[4,128,1024]{2,1,0:T(8,128)}, f32[4,128,1024]{2,1,0:T(8,128)}, u32[]{:S(2)}, u32[]{:S(2)}) collective-permute-start(f32[4,128,1024]{2,1,0:T(8,128)} %collective-permute-done.15.rest_16_), channel_id=1, source_target_pairs={{0,2},{2,0},{1,3},{3,1},{16,18},{18,16},{17,19},{19,17}} | collective-permute-start | bytes 6291464 | tf_op jit(solution)/shard_map/ppermute | solution.py:460
  260.6 1.3 copy-start.3
  278.4 212.2 %all-to-all-start = ((f32[16,2,2,128,128]{4,3,2,1,0:T(8,128)}), f32[16,2,2,128,128]{4,3,2,1,0:T(8,128)}, u32[]{:S(2)}, u32[]{:S(2)}) async-start(f32[16,2,2,128,128]{4,3,2,1,0:T(8,128)} %shard_map.48), calls=%async_computation | async-start | bytes 8388608 | tf_op jit(solution)/shard_map/all_to_all | solution.py:512
  320.7 71.2 %collective-permute-start.34 = (f32[6,1024,128]{2,1,0:T(8,128)}, f32[6,1024,128]{2,1,0:T(8,128)S(1)}, u32[]{:S(2)}, u32[]{:S(2)}) collective-permute-start(f32[6,1024,128]{2,1,0:T(8,128)} %get-tuple-element.18), channel_id=1, source_target_pairs={{0,1},{2,3},{4,5},{6,7},{8,9},{10,11},{12,13},{14,15},{1,16},{3,18... | collective-permute-start | bytes 9437192 | tf_op jit(solution)/shard_map/ppermute | solution.py:492
  320.7 71.2 %collective-permute-start.35 = (f32[6,1024,128]{2,1,0:T(8,128)}, f32[6,1024,128]{2,1,0:T(8,128)}, u32[]{:S(2)}, u32[]{:S(2)}) collective-permute-start(f32[6,1024,128]{2,1,0:T(8,128)} %get-tuple-element.19), channel_id=1, source_target_pairs={{0,16},{2,18},{4,20},{6,22},{8,24},{10,26},{12,28},{14,30},{1,17},... | collective-permute-start | bytes 9437192 | tf_op jit(solution)/shard_map/ppermute | solution.py:492
  321.3 135.5 %collective-permute-start.36 = (f32[6,1024,128]{2,1,0:T(8,128)}, f32[6,1024,128]{2,1,0:T(8,128)}, u32[]{:S(2)}, u32[]{:S(2)}) collective-permute-start(f32[6,1024,128]{2,1,0:T(8,128)} %get-tuple-element.20), channel_id=1, source_target_pairs={{0,17},{2,19},{4,21},{6,23},{8,25},{10,27},{12,29},{14,31},{1,0},{... | collective-permute-start | bytes 9437192 | tf_op jit(solution)/shard_map/ppermute | solution.py:492
  392.0 64.9 %copy-start.11 = (f32[6,1024,128]{2,1,0:T(8,128)}, f32[6,1024,128]{2,1,0:T(8,128)S(1)}, u32[]{:S(2)}) copy-start(f32[6,1024,128]{2,1,0:T(8,128)S(1)} %collective-permute-done.34.rest_1_) | copy-start | bytes 9437188
  490.6 401.3 %all-to-all-start.1 = ((f32[16,2,6,128,128]{4,3,2,1,0:T(8,128)}), f32[16,2,6,128,128]{4,3,2,1,0:T(8,128)}, u32[]{:S(2)}, u32[]{:S(2)}) async-start(f32[16,2,6,128,128]{4,3,2,1,0:T(8,128)} %shard_map.52), calls=%async_computation.1 | async-start | bytes 25165824 | tf_op jit(solution)/shard_map/all_to_all | solution.py:512
  508.2 25.3 %copy-start = (f32[1536,256]{1,0:T(8,128)S(1)}, f32[1536,256]{1,0:T(8,128)}, u32[]{:S(2)}) copy-start(f32[1536,256]{1,0:T(8,128)} %shard_map.49) | copy-start | bytes 4718596
  508.2 22.6 %collective-permute-start.27 = (f32[1536,256]{1,0:T(8,128)}, f32[1536,256]{1,0:T(8,128)S(1)}, u32[]{:S(2)}, u32[]{:S(2)}) collective-permute-start(f32[1536,256]{1,0:T(8,128)} %shard_map.49), channel_id=1, source_target_pairs={{0,1},{2,3},{4,5},{6,7},{8,9},{10,11},{12,13},{14,15}} | collective-permute-start | bytes 4718600 | tf_op jit(solution)/shard_map/ppermute | solution.py:520
  509.6 22.5 %collective-permute-start.28 = (f32[1536,256]{1,0:T(8,128)}, f32[1536,256]{1,0:T(8,128)}, u32[]{:S(2)}, u32[]{:S(2)}) collective-permute-start(f32[1536,256]{1,0:T(8,128)} %shard_map.49), channel_id=1, source_target_pairs={{0,16},{2,18},{4,20},{6,22},{8,24},{10,26},{12,28},{14,30}} | collective-permute-start | bytes 4718600 | tf_op jit(solution)/shard_map/ppermute | solution.py:520
  511.4 21.4 %collective-permute-start.29 = (f32[1536,256]{1,0:T(8,128)}, f32[1536,256]{1,0:T(8,128)}, u32[]{:S(2)}, u32[]{:S(2)}) collective-permute-start(f32[1536,256]{1,0:T(8,128)} %shard_map.49), channel_id=1, source_target_pairs={{0,17},{2,19},{4,21},{6,23},{8,25},{10,27},{12,29},{14,31}} | collective-permute-start | bytes 4718600 | tf_op jit(solution)/shard_map/ppermute | solution.py:520
  514.9 2.0 collective-permute-start.17
  516.3 2.1 collective-permute-start.18
  517.0 2.1 collective-permute-start.19
  518.3 0.7 copy-start.8
  520.3 4.1 collective-permute-start.20
  521.7 3.4 collective-permute-start.21
  524.4 11.9 %collective-permute-start.22 = (f32[256,256]{1,0:T(8,128)S(1)}, f32[256,256]{1,0:T(8,128)S(1)}, u32[]{:S(2)}, u32[]{:S(2)}) collective-permute-start(f32[256,256]{1,0:T(8,128)S(1)} %add_add_fusion.2), channel_id=1, source_target_pairs={{0,6},{1,7},{16,22},{17,23}} | collective-permute-start | bytes 786440 | tf_op jit(solution)/shard_map/ppermute | solution.py:529
  525.1 13.1 %collective-permute-start.23 = (f32[256,256]{1,0:T(8,128)S(1)}, f32[256,256]{1,0:T(8,128)S(1)}, u32[]{:S(2)}, u32[]{:S(2)}) collective-permute-start(f32[256,256]{1,0:T(8,128)S(1)} %add_add_fusion.2), channel_id=1, source_target_pairs={{0,8},{1,9},{16,24},{17,25}} | collective-permute-start | bytes 786440 | tf_op jit(solution)/shard_map/ppermute | solution.py:529
  530.8 2.0 copy-start.4
  530.8 193.6 %collective-permute-start.24 = (f32[256,256]{1,0:T(8,128)S(1)}, f32[256,256]{1,0:T(8,128)S(1)}, u32[]{:S(2)}, u32[]{:S(2)}) collective-permute-start(f32[256,256]{1,0:T(8,128)S(1)} %add_add_fusion.2), channel_id=1, source_target_pairs={{0,10},{1,11},{16,26},{17,27}} | collective-permute-start | bytes 786440 | tf_op jit(solution)/shard_map/ppermute | solution.py:529
  532.1 193.8 %collective-permute-start.25 = (f32[256,256]{1,0:T(8,128)S(1)}, f32[256,256]{1,0:T(8,128)S(1)}, u32[]{:S(2)}, u32[]{:S(2)}) collective-permute-start(f32[256,256]{1,0:T(8,128)S(1)} %add_add_fusion.2), channel_id=1, source_target_pairs={{0,12},{1,13},{16,28},{17,29}} | collective-permute-start | bytes 786440 | tf_op jit(solution)/shard_map/ppermute | solution.py:529
  532.9 193.1 %collective-permute-start.26 = (f32[256,256]{1,0:T(8,128)S(1)}, f32[256,256]{1,0:T(8,128)S(1)}, u32[]{:S(2)}, u32[]{:S(2)}) collective-permute-start(f32[256,256]{1,0:T(8,128)S(1)} %add_add_fusion.2), channel_id=1, source_target_pairs={{0,14},{1,15},{16,30},{17,31}} | collective-permute-start | bytes 786440 | tf_op jit(solution)/shard_map/ppermute | solution.py:529
  536.3 228.0 %collective-permute-start.30 = (f32[1536,256]{1,0:T(8,128)S(1)}, f32[1536,256]{1,0:T(8,128)}, u32[]{:S(2)}, u32[]{:S(2)}) collective-permute-start(f32[1536,256]{1,0:T(8,128)S(1)} %add_add_fusion), channel_id=1, source_target_pairs={{0,12},{2,14},{5,1},{7,3},{24,20},{26,22},{29,25},{31,27}} | collective-permute-start | bytes 4718600 | tf_op jit(solution)/shard_map/ppermute | solution.py:544
  538.2 226.2 %collective-permute-start.31 = (f32[1536,256]{1,0:T(8,128)S(1)}, f32[1536,256]{1,0:T(8,128)}, u32[]{:S(2)}, u32[]{:S(2)}) collective-permute-start(f32[1536,256]{1,0:T(8,128)S(1)} %add_add_fusion), channel_id=1, source_target_pairs={{0,8},{2,10},{5,13},{7,15},{24,16},{26,18},{29,21},{31,23}} | collective-permute-start | bytes 4718600 | tf_op jit(solution)/shard_map/ppermute | solution.py:544
  724.5 76.9 %collective-permute-start.32 = (f32[1536,256]{1,0:T(8,128)S(1)}, f32[1536,256]{1,0:T(8,128)}, u32[]{:S(2)}, u32[]{:S(2)}) collective-permute-start(f32[1536,256]{1,0:T(8,128)S(1)} %add_add_fusion), channel_id=1, source_target_pairs={{0,4},{2,6},{5,9},{7,11},{24,28},{26,30},{29,17},{31,19}} | collective-permute-start | bytes 4718600 | tf_op jit(solution)/shard_map/ppermute | solution.py:544
  803.2 58.0 %collective-permute-start.33 = (f32[1536,256]{1,0:T(8,128)S(1)}, f32[1536,256]{1,0:T(8,128)}, u32[]{:S(2)}, u32[]{:S(2)}) collective-permute-start(f32[1536,256]{1,0:T(8,128)S(1)} %select_select_fusion), channel_id=1, source_target_pairs={{0,2},{2,0},{4,6},{6,4},{8,10},{10,8},{12,14},{14,12},{1,3},{3,1},... | collective-permute-start | bytes 4718600 | tf_op jit(solution)/shard_map/ppermute | solution.py:551

commit v3 on v2

--- a/solution.py
+++ b/solution.py
@@ -89,22 +89,21 @@
     )(block, mine, own, other)
 
 
-def schur_rows(own, other, arrived, panels, half, item_slot, sources, places, origins, slots, col_count):
+def schur_rows(own, other, arrived, panels, half, item_slot, places, origins, slots, col_count, span):
     groups = len(arrived)
     depth = own.shape[1]
-    width, rows, _ = arrived[0].shape
+    first, width = span
+    rows = arrived[0].shape[1]
     child_blocks = rows // BLK
     tall = 2 if child_blocks % 2 == 0 else 1
     steps = child_blocks // tall
     per_child = col_count * width
     wide = per_child * BLK
-    count = len(panels)
     piece = next(w for w in (512, 384, 256, 128) if wide % w == 0)
 
-    def body(half_ref, slot_ref, source_ref, place_ref, origin_ref, own_ref, other_ref, *rest):
+    def body(half_ref, slot_ref, place_ref, origin_ref, own_ref, other_ref, *rest):
         in_refs = rest[:groups]
-        panel_refs = rest[groups : groups + count]
-        out_ref, staged, hi_ref, lo_ref, total_ref, result, load_sem, store_sem = rest[groups + count :]
+        panel_ref, out_ref, staged, hi_ref, lo_ref, total_ref, result, load_sem, store_sem = rest[groups:]
         c = pl.program_id(0)
         step = c * steps + pl.program_id(1)
 
@@ -112,17 +111,11 @@
         def _():
             @pl.loop(0, 2 * per_child)
             def _(k):
-                for a in range(count):
-
-                    @pl.when(source_ref[k] == a)
-                    def _():
-                        pltpu.make_async_copy(
-                            panel_refs[a].at[place_ref[k]], staged.at[k], load_sem.at[k]
-                        ).start()
+                pltpu.make_async_copy(panel_ref.at[place_ref[k]], staged.at[k], load_sem.at[k]).start()
 
             @pl.loop(0, 2 * per_child)
             def _(k):
-                pltpu.make_async_copy(panel_refs[0].at[0], staged.at[k], load_sem.at[k]).wait()
+                pltpu.make_async_copy(panel_ref.at[place_ref[k]], staged.at[k], load_sem.at[k]).wait()
                 hi, lo = split(staged[k])
                 hi_ref[k] = hi
                 lo_ref[k] = lo
@@ -177,20 +170,20 @@
     def arrival(d):
         return pl.BlockSpec(
             (width, tall * BLK, BLK),
-            lambda c, i, h, t, s, p, o: (0, stay(c, i, o[d] // col_count), 0),
+            lambda c, i, h, t, p, o: (first // width, stay(c, i, o[d] // col_count), 0),
         )
 
     return pl.pallas_call(
         body,
         grid_spec=pltpu.PrefetchScalarGridSpec(
-            num_scalar_prefetch=5,
+            num_scalar_prefetch=4,
             grid=(2, steps),
             in_specs=[
-                pl.BlockSpec((tall * BLK, depth), lambda c, i, h, t, s, p, o: (stay(c, i, h[0]), 0)),
-                pl.BlockSpec((tall * BLK, depth), lambda c, i, h, t, s, p, o: (stay(c, i, 1 - h[0]), 0)),
+                pl.BlockSpec((tall * BLK, depth), lambda c, i, h, t, p, o: (stay(c, i, h[0]), 0)),
+                pl.BlockSpec((tall * BLK, depth), lambda c, i, h, t, p, o: (stay(c, i, 1 - h[0]), 0)),
             ]
             + [arrival(d) for d in range(groups)]
-            + [pl.BlockSpec(memory_space=pl.ANY)] * count,
+            + [pl.BlockSpec(memory_space=pl.ANY)],
             out_specs=pl.BlockSpec(memory_space=pl.ANY),
             scratch_shapes=[
                 pltpu.VMEM((2 * per_child, BLK, depth), F32),
@@ -207,47 +200,50 @@
         cost_estimate=cost(
             12 * rows * wide * depth, 8 * rows * (depth + 2 * wide) + 8 * wide * depth
         ),
-    )(half.reshape(1), item_slot, sources, places, origins, own, other, *arrived, *panels)
-
-
-def first_panel(root, part, row_slot, row_valid, col_place):
+    )(half.reshape(1), item_slot, places, origins, own, other, *arrived, panels)
+
+
+def first_panel(root, parts, row_slot, row_valid, col_places):
     row_blocks = root.shape[0] // BLK
-    _, col_count, width, _, _ = part.shape
-
-    def body(slot_ref, valid_ref, place_ref, root_ref, a0_ref, a1_ref, out_ref):
+    count = len(parts)
+    _, col_count, width, _, _ = parts[0].shape
+
+    def body(slot_ref, valid_ref, place_ref, root_ref, *rest):
+        a_refs, out_ref = rest[:-1], rest[-1]
         r = pl.program_id(0)
         out_ref[...] = root_ref[...]
-        for c, a_ref in enumerate((a0_ref, a1_ref)):
-            for q in range(col_count):
-                for u in range(width):
-                    col = place_ref[c, q * width + u]
-                    ok = (valid_ref[c * row_blocks + r] == 1) & (col >= 0) & (col < RP // BLK)
-
-                    @pl.when(ok)
-                    def _():
-                        at = pl.ds(pl.multiple_of(col * BLK, BLK), BLK)
-                        out_ref[:, at] += a_ref[0, q, u]
+        for c in range(2):
+            for k in range(count * col_count * width):
+                j, q, u = k // (col_count * width), k // width % col_count, k % width
+                col = place_ref[c, k]
+                ok = (valid_ref[c * row_blocks + r] == 1) & (col >= 0) & (col < RP // BLK)
+
+                @pl.when(ok)
+                def _():
+                    at = pl.ds(pl.multiple_of(col * BLK, BLK), BLK)
+                    out_ref[:, at] += a_refs[c * count + j][0, q, u]
 
     def arrived(c):
         return pl.BlockSpec(
             (1, col_count, width, BLK, BLK), lambda r, s, v, p: (s[c * row_blocks + r], 0, 0, 0, 0)
         )
 
+    panel = pl.BlockSpec((BLK, RP), lambda r, s, v, p: (r, 0))
     return pl.pallas_call(
         body,
         grid_spec=pltpu.PrefetchScalarGridSpec(
             num_scalar_prefetch=3,
             grid=(row_blocks,),
-            in_specs=[pl.BlockSpec((BLK, RP), lambda r, s, v, p: (r, 0)), arrived(0), arrived(1)],
-            out_specs=pl.BlockSpec((BLK, RP), lambda r, s, v, p: (r, 0)),
+            in_specs=[panel] + [arrived(0)] * count + [arrived(1)] * count,
+            out_specs=panel,
         ),
         out_shape=jax.ShapeDtypeStruct((root.shape[0], RP), F32),
         compiler_params=params(),
-        cost_estimate=cost(0, 8 * root.shape[0] * RP + 4 * part.size),
-    )(row_slot, row_valid, col_place, root, part, part)
-
-
-def advance(root, parts, own_rows, columns, row_slot, row_valid, col_place, flags):
+        cost_estimate=cost(0, 8 * root.shape[0] * RP + 4 * sum(p.size for p in parts)),
+    )(row_slot, row_valid, jnp.concatenate(col_places, axis=1), root, *parts, *parts)
+
+
+def advance(root, parts, own_rows, columns, row_slot, row_valid, col_places, flags):
     rows, cols = root.shape
     row_blocks = rows // BLK
     count = len(parts)
@@ -319,7 +315,17 @@
         out_shape=jax.ShapeDtypeStruct((rows, cols), F32),
         compiler_params=params(),
         cost_estimate=cost(6 * rows * cols * RP, 8 * rows * cols + 4 * sum(p.size for p in parts)),
-    )(row_slot, row_valid, col_place, flags, root, *parts, *parts, own_rows, columns)
+    )(
+        row_slot,
+        row_valid,
+        jnp.concatenate(col_places, axis=1),
+        flags,
+        root,
+        *parts,
+        *parts,
+        own_rows,
+        columns,
+    )
 
 
 def deliver(root, part, row_slot, row_valid, col_place):
@@ -381,29 +387,47 @@
     cap_col = max(1, col_blocks // group_count)
     cap_row = max(1, 2 * child_blocks // row_count)
     cap_pick = cap_row * ratio
-    widths = [cap_col] if cap_col <= 2 else [2, cap_col - 2]
-    spans = [(sum(widths[:j]), w) for j, w in enumerate(widths)]
-    band = 2 if row_count % 2 == 0 else 1
+    even = col_blocks == group_count * cap_col and 2 * child_blocks == row_count * cap_row
+    halves = 2 if even and cap_pick % 2 == 0 and cap_col % 2 == 0 else 1
+    half_col, half_pick = cap_col // halves, cap_pick // halves
+    width = half_col // 2 if half_col % 2 == 0 else half_col
     iota = functools.partial(jnp.arange, dtype=jnp.int32)
     own_panel = child_panel[0]
     other_panel = lax.ppermute(own_panel, "half", [(0, 1), (1, 0)])
 
     by_col = index_map.reshape(2, col_count, col_blocks)
-    col_group = by_col // group_cols
-    before = (by_col[..., None, :] < by_col[..., :, None]) & (
-        col_group[..., None, :] == col_group[..., :, None]
-    )
-    col_rank = jnp.sum(before.astype(jnp.int32), axis=-1)
-    col_key = col_group * cap_col + col_rank
+    by_row = index_map.reshape(2, row_count, child_blocks)
+    key = by_row // group_cols
+    if halves == 2:
+        in_group = key[..., None] == iota(group_count)
+        named = jnp.sum(in_group.astype(jnp.int32), axis=2)
+        leading = jnp.sum((in_group & (by_row[..., None] < RP // BLK)).astype(jnp.int32), axis=2)
+        least = jnp.maximum(jnp.maximum(half_pick - named[1], leading[0]), 0)
+        most = jnp.minimum(jnp.minimum(named[0], half_pick - leading[1]), half_pick)
+        least = least.reshape(col_count, row_count // col_count, group_count)
+        room = most.reshape(least.shape) - least
+        rest = half_col - jnp.sum(least, axis=1, keepdims=True)
+        taken = least + jnp.clip(rest - (jnp.cumsum(room, axis=1) - room), 0, room)
+        taken = taken.reshape(row_count, group_count)
+        taken = jnp.stack([taken, half_pick - taken])
+        ahead = (by_row[..., None, :] < by_row[..., :, None]) & (key[..., None, :] == key[..., :, None])
+        place_in = jnp.sum(ahead.astype(jnp.int32), axis=-1)
+        limit = jnp.sum(jnp.where(in_group, taken[:, :, None, :], 0), axis=-1)
+        key = 2 * key + (place_in >= limit).astype(jnp.int32)
+
+    col_key = key.reshape(2, col_count, col_blocks)
+    before = (col_key[..., None, :] == col_key[..., :, None]) & (
+        iota(col_blocks)[None, :] < iota(col_blocks)[:, None]
+    )
+    col_key = col_key * half_col + jnp.sum(before.astype(jnp.int32), axis=-1)
     own_key = lax.dynamic_index_in_dim(
         col_key.reshape(group_count, col_blocks), group, 0, keepdims=False
     )
     chosen = jnp.sum(
         jnp.where(own_key[None, :] == iota(group_count * cap_col)[:, None], iota(col_blocks), 0),
         axis=1,
-    ).reshape(group_count, cap_col)
-
-    by_row = index_map.reshape(2, row_count, child_blocks)
+    ).reshape(group_count, halves, half_col)
+
     joint = by_row.transpose(1, 0, 2).reshape(row_count, 2 * child_blocks)
     items = 2 * child_blocks
     earlier = iota(items)[None, :] < iota(items)[:, None]
@@ -411,32 +435,21 @@
     row_rank = jnp.sum(
         ((owner[:, None, :] == owner[:, :, None]) & earlier).astype(jnp.int32), axis=-1
     )
-    joint_group = joint // group_cols
+    joint_key = key.transpose(1, 0, 2).reshape(row_count, items)
     pick_rank = jnp.sum(
-        ((joint_group[:, None, :] == joint_group[:, :, None]) & earlier).astype(jnp.int32), axis=-1
+        ((joint_key[:, None, :] == joint_key[:, :, None]) & earlier).astype(jnp.int32), axis=-1
     )
     here = lax.dynamic_index_in_dim
     own_owner = here(owner, prow, 0, keepdims=False)
     own_row_rank = here(row_rank, prow, 0, keepdims=False)
-    own_pick_group = here(joint_group, prow, 0, keepdims=False)
-    own_pick_rank = here(pick_rank, prow, 0, keepdims=False)
+    own_pick = here(joint_key * half_pick + pick_rank, prow, 0, keepdims=False)
     pick_item = jnp.sum(
-        jnp.where(
-            (own_pick_group[None, :] == group) & (own_pick_rank[None, :] == iota(cap_pick)[:, None]),
-            iota(items),
-            0,
-        ),
+        jnp.where(own_pick[None, :] == (group * cap_pick + iota(cap_pick))[:, None], iota(items), 0),
         axis=1,
     )
     item_slot = own_owner * cap_row + own_row_rank
 
-    spread_z, spread_x = iota(row_count) // band - prow // band, (iota(row_count) - prow) % band
-    source = jnp.where(
-        spread_z == 0,
-        spread_x,
-        band * (2 * jnp.abs(spread_z) - 1 + (spread_z > 0)) + spread_x,
-    )
-    code = (source[:, None] * cap_pick + pick_rank).reshape(row_count, 2, child_blocks)
+    code = (iota(row_count)[:, None] * half_pick + pick_rank).reshape(row_count, 2, child_blocks)
     slot_of = code.transpose(1, 0, 2).reshape(2, col_count, col_blocks)
     match = col_key[:, :, None, :] == (group * cap_col + iota(cap_col))[:, None]
     place = jnp.sum(jnp.where(match, slot_of[:, :, None, :], 0), axis=-1)
@@ -453,35 +466,22 @@
     row_slot = jnp.maximum(row_slot - 1, 0).reshape(-1)
 
     pick_mine = (pick_item // child_blocks == half).astype(jnp.int32)
-    picked = pick_rows(own_panel, other_panel, pick_item % child_blocks, pick_mine)
-
-    def across(value, rows_in):
-        return [
-            lax.ppermute(value, "prow", [(r, r - r % band + (r % band - o) % band) for r in rows_in])
-            for o in range(1, band)
-        ]
-
-    rows_all = list(range(row_count))
-    bands = row_count // band
-    panels = [picked] + across(picked, rows_all)
-    up = down = picked
-    for k in range(1, bands):
-        up = lax.ppermute(
-            up, "prow", [(r, r + band) for r in rows_all if k - 1 <= r // band < bands - 1]
-        )
-        down = lax.ppermute(
-            down, "prow", [(r, r - band) for r in rows_all if 0 < r // band <= bands - k]
-        )
-        panels += [up] + across(up, [r for r in rows_all if r // band >= k])
-        panels += [down] + across(down, [r for r in rows_all if r // band < bands - k])
+    panels = []
+    for h in range(halves):
+        at = slice(h * half_pick, (h + 1) * half_pick)
+        picked = pick_rows(own_panel, other_panel, pick_item[at] % child_blocks, pick_mine[at])
+        panels.append(lax.all_gather(picked, "prow", axis=0, tiled=True))
 
     device = lambda g, r: ((g // col_count) * row_count + r) * col_count + g % col_count
     everyone = ("half", "prow", "pcol")
     distance = (group + iota(group_count)) % group_count
     origins = (group - iota(group_count)) % group_count
     arrived = []
-    for start, width in spans:
-        packed = pack_columns(child_update[0], chosen[distance, start : start + width])
+    for h in range(halves):
+        picks = chosen[distance, h]
+        if arrived:
+            picks, arrived[-1] = lax.optimization_barrier((picks, arrived[-1]))
+        packed = pack_columns(child_update[0], picks)
         got = [packed[0]]
         for d in range(1, group_count):
             pairs = [
@@ -493,25 +493,27 @@
         arrived.append(got)
 
     parts, col_places = [], []
-    for (start, width), got in zip(spans, arrived):
-        codes = place[:, :, start : start + width].reshape(-1)
-        col_places.append(col_local[:, :, start : start + width].reshape(2, -1))
-        outgoing = schur_rows(
-            own_panel,
-            other_panel,
-            got,
-            panels,
-            half,
-            item_slot,
-            codes // cap_pick,
-            codes % cap_pick,
-            origins,
-            row_count * cap_row,
-            col_count,
-        )
-        parts.append(lax.all_to_all(outgoing, "prow", split_axis=0, concat_axis=0, tiled=True))
-
-    raw = first_panel(root_front, parts[0], row_slot, row_valid, col_places[0])
+    for h in range(halves):
+        for first in range(0, half_col, width):
+            at = slice(h * half_col + first, h * half_col + first + width)
+            col_places.append(col_local[:, :, at].reshape(2, -1))
+            outgoing = schur_rows(
+                own_panel,
+                other_panel,
+                arrived[h],
+                panels[h],
+                half,
+                item_slot,
+                place[:, :, at].reshape(-1),
+                origins,
+                row_count * cap_row,
+                col_count,
+                (first, width),
+            )
+            parts.append(lax.all_to_all(outgoing, "prow", split_axis=0, concat_axis=0, tiled=True))
+
+    early = max(1, len(parts) // halves)
+    raw = first_panel(root_front, parts[:early], row_slot, row_valid, col_places[:early])
 
     def to_groups(value):
         total = jnp.where(group == 0, value, 0.0)
@@ -564,10 +566,11 @@
     top = jnp.where(prow == 0, factor, solved[:RP])
     own_rows = jnp.concatenate([top, solved[RP:]], axis=0)
     flags = jnp.stack([(prow == 0), (group == 0)]).astype(jnp.int32)
+    late = max(1, len(parts) - 1)
     root = advance(
-        root_front, parts[:1], own_rows, lower_cols, row_slot, row_valid, col_places[0], flags
-    )
-    for part, col_place in zip(parts[1:], col_places[1:]):
+        root_front, parts[:late], own_rows, lower_cols, row_slot, row_valid, col_places[:late], flags
+    )
+    for part, col_place in zip(parts[late:], col_places[late:]):
         root = deliver(root, part, row_slot, row_valid, col_place)
     return root
 

time: 916 us -> 815 us (0.89)
  the two profiles are of different devices: /device:TPU:22 before, /device:TPU:0 now
where the time goes in v3:
time: 815 us; the launch traced here: 810 us
  waiting for transfers between devices  486 us (60%)
  Pallas kernels  145 us (18%)
  other arithmetic  71.9 us (9%)
  starting transfers between devices  63.2 us (8%)
  local copies, waits for them, and re-layouts  19.2 us (2%)
  between operations  15.2 us (2%)
  matrix products  9.56 us (1%)
    all_to_all x4, waiting for transfers between devices, shards(): lax.all_to_all(outgoing, 'prow', split_axis=0, concat_axis=0, tiled=True)  205 us
    ppermute x6, waiting for transfers between devices, shards(): got.append(lax.ppermute(packed[d], everyone, pairs))  179 us
    ppermute x7, waiting for transfers between devices, shards(): pivot = pivot + lax.ppermute(first, 'prow', [(0, r)])  67.3 us
    pallas_call x4, Pallas kernels, schur_rows(): pl.pallas_call(body, grid_spec=pltpu.PrefetchScalarGridSpec(num_scalar_pr...  65.8 us
    another operation x7, other arithmetic, shards(): factor = jnp.linalg.cholesky(pivot)  34.6 us
    pallas_call x1, Pallas kernels, advance(): pl.pallas_call(body, grid_spec=pltpu.PrefetchScalarGridSpec(num_scalar_pr...  27.8 us
    another operation x3, other arithmetic, shards(): lax.linalg.triangular_solve(factor, jnp.eye(RP, dtype=F32), left_side=Tru...  21.8 us
    all_gather x2, waiting for transfers between devices, shards(): panels.append(lax.all_gather(picked, 'prow', axis=0, tiled=True))  20.5 us
  transfers between devices with their start and end apart: 30, of which 13 were waited for; matrix products, arithmetic and copies ran while one was open for 12% of the time, Pallas kernels for 15%

profile of v3, /device:TPU:0, one launch (start us, length us, event | category | flops | bytes accessed | tf_op | source)
XLA Modules:
  0.0 810.4 jit_solution(8225165466432394257)
XLA Ops:
  7.0 0.8 eq.173
  11.7 2.5 collective-permute-done.other_ref
  14.1 3.2 shard_map.47
  19.6 7.7 shard_map.46
  27.3 2.9 collective-permute-start.1
  33.6 43.0 %collective-permute-done.1.rest_1_ = f32[4,1024,128]{2,1,0:T(8,128)S(1)} collective-permute-done((f32[4,1024,128]{2,1,0:T(8,128)}, f32[4,1024,128]{2,1,0:T(8,128)S(1)}, u32[]{:S(2)}, u32[]{:S(2)}) %collective-permute-start.1) | collective-permute-done | bytes 2097184 | tf_op jit(solution)/shard_map/ppermute | solution.py:492
  76.5 44.9 %collective-permute-done.3.rest_3_ = f32[4,1024,128]{2,1,0:T(8,128)} collective-permute-done((f32[4,1024,128]{2,1,0:T(8,128)}, f32[4,1024,128]{2,1,0:T(8,128)}, u32[]{:S(2)}, u32[]{:S(2)}) %collective-permute-start.3) | collective-permute-done | bytes 2097184 | tf_op jit(solution)/shard_map/ppermute | solution.py:492
  121.4 3.1 shard_map.51
  124.5 20.5 %all-gather.3.cloned.1.call-done.rest_4_ = f32[16,128,1024]{2,1,0:T(8,128)} async-done(((f32[2,128,1024]{2,1,0:T(8,128)}), f32[16,128,1024]{2,1,0:T(8,128)}) %all-gather.3.cloned.1.call-update) | async-done | bytes 8388624 | tf_op jit(solution)/shard_map/all_gather | solution.py:473
  145.0 16.6 %shard_map.48 = f32[16,2,2,128,128]{4,3,2,1,0:T(8,128)} custom-call(s32[1]{0:T(128)} %bitcast.6.half_ref, s32[16]{0:T(128)} %fusion.39.slot_ref, s32[8]{0:T(128)} %reshape.438.place_ref, s32[4]{0:T(128)} %and_select_fusion.4.origin_ref, f32[1024,1024]{1,0:T(8,128)} %bitcast.78, f32[1024,1024]{1,0:T(8,128)} %collective-permute-done.other_ref, ...), custom_call_target="tpu_custom_call" | custom-call | flops 6442450944 | bytes 20971520 | tf_op jit(solution)/shard_map/pallas_call | solution.py:176
  161.7 4.6 all-to-all-start
  166.9 16.5 %shard_map.49 = f32[16,2,2,128,128]{4,3,2,1,0:T(8,128)} custom-call(s32[1]{0:T(128)} %bitcast.6.half_ref, s32[16]{0:T(128)} %fusion.39.slot_ref, s32[8]{0:T(128)} %reshape.441.place_ref, s32[4]{0:T(128)} %and_select_fusion.4.origin_ref, f32[1024,1024]{1,0:T(8,128)} %bitcast.79, f32[1024,1024]{1,0:T(8,128)} %collective-permute-done.other_ref, ...), custom_call_target="tpu_custom_call" | custom-call | flops 6442450944 | bytes 20971520 | tf_op jit(solution)/shard_map/pallas_call | solution.py:176
  183.3 154.5 %all-to-all-done.rest_0_.rest_2_.rest_3_ = f32[16,2,2,128,128]{4,3,2,1,0:T(8,128)} async-done(((f32[16,2,2,128,128]{4,3,2,1,0:T(8,128)}), f32[16,2,2,128,128]{4,3,2,1,0:T(8,128)}, u32[]{:S(2)}, u32[]{:S(2)}) %all-to-all-start) | async-done | bytes 4194336 | tf_op jit(solution)/shard_map/all_to_all | solution.py:513
  337.8 4.6 all-to-all-start.1
  343.0 7.7 shard_map.50
  350.7 1.5 collective-permute-start.4
  353.1 45.7 %collective-permute-done.4.rest_1_ = f32[4,1024,128]{2,1,0:T(8,128)S(1)} collective-permute-done((f32[4,1024,128]{2,1,0:T(8,128)}, f32[4,1024,128]{2,1,0:T(8,128)S(1)}, u32[]{:S(2)}, u32[]{:S(2)}) %collective-permute-start.4) | collective-permute-done | bytes 2097184 | tf_op jit(solution)/shard_map/ppermute | solution.py:492
  398.8 45.1 %collective-permute-done.6.rest_3_ = f32[4,1024,128]{2,1,0:T(8,128)} collective-permute-done((f32[4,1024,128]{2,1,0:T(8,128)}, f32[4,1024,128]{2,1,0:T(8,128)}, u32[]{:S(2)}, u32[]{:S(2)}) %collective-permute-start.6) | collective-permute-done | bytes 2097184 | tf_op jit(solution)/shard_map/ppermute | solution.py:492
  443.9 16.4 %shard_map.52 = f32[16,2,2,128,128]{4,3,2,1,0:T(8,128)} custom-call(s32[1]{0:T(128)} %bitcast.6.half_ref, s32[16]{0:T(128)} %fusion.39.slot_ref, s32[8]{0:T(128)} %reshape.442.place_ref, s32[4]{0:T(128)} %and_select_fusion.4.origin_ref, f32[1024,1024]{1,0:T(8,128)} %bitcast.80, f32[1024,1024]{1,0:T(8,128)} %collective-permute-done.other_ref, ...), custom_call_target="tpu_custom_call" | custom-call | flops 6442450944 | bytes 20971520 | tf_op jit(solution)/shard_map/pallas_call | solution.py:176
  460.3 5.9 all-to-all-start.2
  468.6 10.8 %shard_map.53 = f32[1536,256]{1,0:T(8,128)} custom-call(s32[24]{0:T(128)} %max.46.slot_ref, s32[24]{0:T(128)} %reshape.464.valid_ref, s32[2,8]{1,0:T(2,128)} %pad_add_fusion.2.place_ref, f32[1536,3072]{1,0:T(8,128)} %root_ref.3, f32[16,2,2,128,128]{4,3,2,1,0:T(8,128)} %all-to-all-done.rest_0_.rest_2_.rest_3_, ...), custom_call_target="tpu_custom_call" | custom-call | bytes 11534336 | tf_op jit(solution)/shard_map/pallas_call | solution.py:232
  479.4 1.4 collective-permute-start.19
  480.8 2.4 collective-permute-start.18
  483.3 2.4 collective-permute-start.17
  485.7 1.7 slice.145
  487.4 1.3 collective-permute-start.8
  489.3 1.3 collective-permute-start.7
  490.6 2.0 collective-permute-start.9
  492.6 16.4 %shard_map.55 = f32[16,2,2,128,128]{4,3,2,1,0:T(8,128)} custom-call(s32[1]{0:T(128)} %bitcast.6.half_ref, s32[16]{0:T(128)} %fusion.39.slot_ref, s32[8]{0:T(128)} %reshape.444.place_ref, s32[4]{0:T(128)} %and_select_fusion.4.origin_ref, f32[1024,1024]{1,0:T(8,128)} %bitcast.81, f32[1024,1024]{1,0:T(8,128)} %collective-permute-done.other_ref, ...), custom_call_target="tpu_custom_call" | custom-call | flops 6442450944 | bytes 20971520 | tf_op jit(solution)/shard_map/pallas_call | solution.py:176
  509.0 50.7 %all-to-all-done.2.rest_2_.rest_5_ = f32[16,2,2,128,128]{4,3,2,1,0:T(8,128)} async-done(((f32[16,2,2,128,128]{4,3,2,1,0:T(8,128)}), f32[16,2,2,128,128]{4,3,2,1,0:T(8,128)}, u32[]{:S(2)}, u32[]{:S(2)}) %all-to-all-start.2) | async-done | bytes 4194336 | tf_op jit(solution)/shard_map/all_to_all | solution.py:513
  559.7 4.6 all-to-all-start.3
  565.1 1.2 add_add_fusion.2
  566.2 7.3 collective-permute-start.16
  573.5 2.0 collective-permute-start.15
  577.5 61.9 %collective-permute-done.16 = f32[256,256]{1,0:T(8,128)} collective-permute-done((f32[256,256]{1,0:T(8,128)S(1)}, f32[256,256]{1,0:T(8,128)}, u32[]{:S(2)}, u32[]{:S(2)}) %collective-permute-start.16) | collective-permute-done | bytes 262176 | tf_op jit(solution)/shard_map/ppermute | solution.py:531
  639.4 1.3 collective-permute-start.14
  640.7 4.3 collective-permute-done.15
  645.0 1.3 collective-permute-start.13
  646.3 1.3 collective-permute-start.12
  647.7 1.3 collective-permute-start.11
  649.0 1.5 collective-permute-start.10
  650.5 2.8 add_add_fusion
  653.3 2.4 collective-permute-start.22
  656.2 6.4 collective-permute-start.21
  662.7 2.5 collective-permute-start.20
  665.7 1.2 add_add_fusion.1
  667.0 11.7 %cholesky.49 = f32[128,128]{1,0:T(8,128)S(1)} custom-call(f32[128,128]{1,0:T(8,128)S(1)} %cholesky.115), custom_call_target="Cholesky" | custom-call | tf_op jit(solution)/shard_map/jit(cholesky)/cholesky | solution.py:532
  678.8 9.8 %custom-call.14 = f32[1,128,128]{1,2,0:T(8,128)S(1)} custom-call(f32[1,128,128]{2,1,0:T(8,128)S(1)} %get-tuple-element.64), custom_call_target="InvertDiagBlocksLowerTriangular" | custom-call | tf_op jit(solution)/shard_map/jit(cholesky)/cholesky | solution.py:532
  689.1 11.7 %cholesky.103 = f32[128,128]{1,0:T(8,128)S(1)} custom-call(f32[128,128]{1,0:T(8,128)S(1)} %slice_subtract_fusion), custom_call_target="Cholesky" | custom-call | tf_op jit(solution)/shard_map/jit(cholesky)/cholesky | solution.py:532
  703.4 0.7 fusion.5
  704.2 12.1 %collective-permute-done.20 = f32[1536,256]{1,0:T(8,128)} collective-permute-done((f32[1536,256]{1,0:T(8,128)S(1)}, f32[1536,256]{1,0:T(8,128)}, u32[]{:S(2)}, u32[]{:S(2)}) %collective-permute-start.20) | collective-permute-done | bytes 1572896 | tf_op jit(solution)/shard_map/ppermute | solution.py:546
  716.8 7.1 while.1
  717.6 2.9 bitcast_dynamic-update-slice_fusion.2
  721.1 2.8 bitcast_dynamic-update-slice_fusion.2
  723.9 21.1 %custom-call.15 = f32[2,128,128]{1,2,0:T(8,128)} custom-call(f32[2,128,128]{2,1,0:T(8,128)} %get-tuple-element.38), custom_call_target="InvertDiagBlocksLowerTriangular" | custom-call | tf_op jit(solution)/shard_map/triangular_solve | solution.py:533
  745.0 1.1 fusion.7
  746.1 1.1 convolution_subtract_fusion
  747.2 1.1 fusion.10
  748.3 1.4 fusion.6
  749.9 1.2 pad_maximum_fusion.rest_6_
  751.1 1.6 broadcast_select_fusion.1
  752.8 4.3 fusion.rest_7_
  757.1 27.8 %shard_map.54.root_ref = f32[1536,3072]{1,0:T(8,128)} custom-call(s32[24]{0:T(128)} %max.46.slot_ref, s32[24]{0:T(128)} %reshape.464.valid_ref, s32[2,12]{1,0:T(2,128)} %pad_add_fusion.1.place_ref, s32[2]{0:T(128)} %add_convert_fusion.flag_ref, f32[1536,3072]{1,0:T(8,128)} %root_ref.3, f32[16,2,2,128,128]{4,3,2,1,0:T(8,128)} %all-to-all-done.rest_0_.rest_2_.rest_3_, ...), custom_call_target="tpu_custom_call" | custom-call | flops 7247757312 | bytes 50331648 | tf_op jit(solution)/shard_map/pallas_call | solution.py:300
  784.9 18.7 %shard_map.56 = f32[1536,3072]{1,0:T(8,128)} custom-call(s32[24]{0:T(128)} %max.46.slot_ref, s32[24]{0:T(128)} %reshape.464.valid_ref, s32[2,4]{1,0:T(2,128)} %reshape.433.place_ref, f32[1536,3072]{1,0:T(8,128)} %shard_map.54.root_ref, f32[16,2,2,128,128]{4,3,2,1,0:T(8,128)} %all-to-all-done.3.a0_ref.a1_ref, f32[16,2,2,128,128]{4,3,2,1,0:T(8,128)} %all-to-all-done.3.a0_ref.a1_ref), custom_call_target="tpu_custom_call" | custom-call | bytes 41943040 | tf_op jit(solution)/shard_map/pallas_call | solution.py:358
  (150 shorter events, 22.6 us)
Async XLA Ops:
  6.5 138.5 %all-gather.3.cloned.1.call-start = ((), (), s32[]{:S(2)}) async-start(), calls=%async_computation.4 | async-start | bytes 9437184 | tf_op jit(solution)/shard_map/all_gather | solution.py:473
  6.5 7.6 collective-permute-start
  14.1 3.3 copy-start.6
  17.3 426.6 %all-gather.5.cloned.1.call-start = ((), (), s32[]{:S(2)}) async-start(), calls=%async_computation.5 | async-start | bytes 9437184 | tf_op jit(solution)/shard_map/all_gather | solution.py:473
  27.3 49.2 %collective-permute-start.1 = (f32[4,1024,128]{2,1,0:T(8,128)}, f32[4,1024,128]{2,1,0:T(8,128)S(1)}, u32[]{:S(2)}, u32[]{:S(2)}) collective-permute-start(f32[4,1024,128]{2,1,0:T(8,128)} %get-tuple-element.19), channel_id=1, source_target_pairs={{0,1},{2,3},{4,5},{6,7},{8,9},{10,11},{12,13},{14,15},{1,16},{3,18... | collective-permute-start | bytes 6291464 | tf_op jit(solution)/shard_map/ppermute | solution.py:492
  30.2 46.3 %collective-permute-start.2 = (f32[4,1024,128]{2,1,0:T(8,128)}, f32[4,1024,128]{2,1,0:T(8,128)}, u32[]{:S(2)}, u32[]{:S(2)}) collective-permute-start(f32[4,1024,128]{2,1,0:T(8,128)} %get-tuple-element.20), channel_id=1, source_target_pairs={{0,16},{2,18},{4,20},{6,22},{8,24},{10,26},{12,28},{14,30},{1,17},... | collective-permute-start | bytes 6291464 | tf_op jit(solution)/shard_map/ppermute | solution.py:492
  30.2 91.2 %collective-permute-start.3 = (f32[4,1024,128]{2,1,0:T(8,128)}, f32[4,1024,128]{2,1,0:T(8,128)}, u32[]{:S(2)}, u32[]{:S(2)}) collective-permute-start(f32[4,1024,128]{2,1,0:T(8,128)} %get-tuple-element.21), channel_id=1, source_target_pairs={{0,17},{2,19},{4,21},{6,23},{8,25},{10,27},{12,29},{14,31},{1,0},{... | collective-permute-start | bytes 6291464 | tf_op jit(solution)/shard_map/ppermute | solution.py:492
  76.5 48.0 %copy-start.2 = (f32[4,1024,128]{2,1,0:T(8,128)}, f32[4,1024,128]{2,1,0:T(8,128)S(1)}, u32[]{:S(2)}) copy-start(f32[4,1024,128]{2,1,0:T(8,128)S(1)} %collective-permute-done.1.rest_1_) | copy-start | bytes 6291460
  161.7 176.2 %all-to-all-start = ((f32[16,2,2,128,128]{4,3,2,1,0:T(8,128)}), f32[16,2,2,128,128]{4,3,2,1,0:T(8,128)}, u32[]{:S(2)}, u32[]{:S(2)}) async-start(f32[16,2,2,128,128]{4,3,2,1,0:T(8,128)} %shard_map.48), calls=%async_computation | async-start | bytes 8388608 | tf_op jit(solution)/shard_map/all_to_all | solution.py:513
  337.8 122.5 %all-to-all-start.1 = ((f32[16,2,2,128,128]{4,3,2,1,0:T(8,128)}), f32[16,2,2,128,128]{4,3,2,1,0:T(8,128)}, u32[]{:S(2)}, u32[]{:S(2)}) async-start(f32[16,2,2,128,128]{4,3,2,1,0:T(8,128)} %shard_map.49), calls=%async_computation.1 | async-start | bytes 8388608 | tf_op jit(solution)/shard_map/all_to_all | solution.py:513
  350.7 48.1 %collective-permute-start.4 = (f32[4,1024,128]{2,1,0:T(8,128)}, f32[4,1024,128]{2,1,0:T(8,128)S(1)}, u32[]{:S(2)}, u32[]{:S(2)}) collective-permute-start(f32[4,1024,128]{2,1,0:T(8,128)} %get-tuple-element.28), channel_id=1, source_target_pairs={{0,1},{2,3},{4,5},{6,7},{8,9},{10,11},{12,13},{14,15},{1,16},{3,18... | collective-permute-start | bytes 6291464 | tf_op jit(solution)/shard_map/ppermute | solution.py:492
  352.2 46.6 %collective-permute-start.5 = (f32[4,1024,128]{2,1,0:T(8,128)}, f32[4,1024,128]{2,1,0:T(8,128)}, u32[]{:S(2)}, u32[]{:S(2)}) collective-permute-start(f32[4,1024,128]{2,1,0:T(8,128)} %get-tuple-element.29), channel_id=1, source_target_pairs={{0,16},{2,18},{4,20},{6,22},{8,24},{10,26},{12,28},{14,30},{1,17},... | collective-permute-start | bytes 6291464 | tf_op jit(solution)/shard_map/ppermute | solution.py:492
  352.2 91.7 %collective-permute-start.6 = (f32[4,1024,128]{2,1,0:T(8,128)}, f32[4,1024,128]{2,1,0:T(8,128)}, u32[]{:S(2)}, u32[]{:S(2)}) collective-permute-start(f32[4,1024,128]{2,1,0:T(8,128)} %get-tuple-element.30), channel_id=1, source_target_pairs={{0,17},{2,19},{4,21},{6,23},{8,25},{10,27},{12,29},{14,31},{1,0},{... | collective-permute-start | bytes 6291464 | tf_op jit(solution)/shard_map/ppermute | solution.py:492
  398.8 45.1 %copy-start.1 = (f32[4,1024,128]{2,1,0:T(8,128)}, f32[4,1024,128]{2,1,0:T(8,128)S(1)}, u32[]{:S(2)}) copy-start(f32[4,1024,128]{2,1,0:T(8,128)S(1)} %collective-permute-done.4.rest_1_) | copy-start | bytes 6291460
  460.3 99.4 %all-to-all-start.2 = ((f32[16,2,2,128,128]{4,3,2,1,0:T(8,128)}), f32[16,2,2,128,128]{4,3,2,1,0:T(8,128)}, u32[]{:S(2)}, u32[]{:S(2)}) async-start(f32[16,2,2,128,128]{4,3,2,1,0:T(8,128)} %shard_map.52), calls=%async_computation.2 | async-start | bytes 8388608 | tf_op jit(solution)/shard_map/all_to_all | solution.py:513
  479.4 166.9 %collective-permute-start.19 = (f32[1536,256]{1,0:T(8,128)}, f32[1536,256]{1,0:T(8,128)S(1)}, u32[]{:S(2)}, u32[]{:S(2)}) collective-permute-start(f32[1536,256]{1,0:T(8,128)} %shard_map.53), channel_id=1, source_target_pairs={{0,17},{2,19},{4,21},{6,23},{8,25},{10,27},{12,29},{14,31}} | collective-permute-start | bytes 4718600 | tf_op jit(solution)/shard_map/ppermute | solution.py:522
  480.8 166.8 %collective-permute-start.18 = (f32[1536,256]{1,0:T(8,128)}, f32[1536,256]{1,0:T(8,128)}, u32[]{:S(2)}, u32[]{:S(2)}) collective-permute-start(f32[1536,256]{1,0:T(8,128)} %shard_map.53), channel_id=1, source_target_pairs={{0,16},{2,18},{4,20},{6,22},{8,24},{10,26},{12,28},{14,30}} | collective-permute-start | bytes 4718600 | tf_op jit(solution)/shard_map/ppermute | solution.py:522
  483.3 165.7 %collective-permute-start.17 = (f32[1536,256]{1,0:T(8,128)}, f32[1536,256]{1,0:T(8,128)}, u32[]{:S(2)}, u32[]{:S(2)}) collective-permute-start(f32[1536,256]{1,0:T(8,128)} %shard_map.53), channel_id=1, source_target_pairs={{0,1},{2,3},{4,5},{6,7},{8,9},{10,11},{12,13},{14,15}} | collective-permute-start | bytes 4718600 | tf_op jit(solution)/shard_map/ppermute | solution.py:522
  487.4 3.2 collective-permute-start.8
  489.3 75.0 %collective-permute-start.7 = (f32[256,256]{1,0:T(8,128)}, f32[256,256]{1,0:T(8,128)S(1)}, u32[]{:S(2)}, u32[]{:S(2)}) collective-permute-start(f32[256,256]{1,0:T(8,128)} %slice.145), channel_id=1, source_target_pairs={{0,1}} | collective-permute-start | bytes 786440 | tf_op jit(solution)/shard_map/ppermute | solution.py:528
  490.6 2.0 copy-start.4
  490.6 74.4 %collective-permute-start.9 = (f32[256,256]{1,0:T(8,128)}, f32[256,256]{1,0:T(8,128)}, u32[]{:S(2)}, u32[]{:S(2)}) collective-permute-start(f32[256,256]{1,0:T(8,128)} %slice.145), channel_id=1, source_target_pairs={{0,17}} | collective-permute-start | bytes 786440 | tf_op jit(solution)/shard_map/ppermute | solution.py:528
  509.0 56.0 %copy-start = (f32[1536,256]{1,0:T(8,128)S(1)}, f32[1536,256]{1,0:T(8,128)}, u32[]{:S(2)}) copy-start(f32[1536,256]{1,0:T(8,128)} %shard_map.53) | copy-start | bytes 4718596
  559.7 225.2 %all-to-all-start.3 = ((f32[16,2,2,128,128]{4,3,2,1,0:T(8,128)}), f32[16,2,2,128,128]{4,3,2,1,0:T(8,128)}, u32[]{:S(2)}, u32[]{:S(2)}) async-start(f32[16,2,2,128,128]{4,3,2,1,0:T(8,128)} %shard_map.55), calls=%async_computation.3 | async-start | bytes 8388608 | tf_op jit(solution)/shard_map/all_to_all | solution.py:513
  564.3 0.7 copy-start.5
  566.2 73.2 %collective-permute-start.16 = (f32[256,256]{1,0:T(8,128)S(1)}, f32[256,256]{1,0:T(8,128)}, u32[]{:S(2)}, u32[]{:S(2)}) collective-permute-start(f32[256,256]{1,0:T(8,128)S(1)} %add_add_fusion.2), channel_id=1, source_target_pairs={{0,14},{1,15},{16,30},{17,31}} | collective-permute-start | bytes 786440 | tf_op jit(solution)/shard_map/ppermute | solution.py:531
  573.5 71.5 %collective-permute-start.15 = (f32[256,256]{1,0:T(8,128)S(1)}, f32[256,256]{1,0:T(8,128)}, u32[]{:S(2)}, u32[]{:S(2)}) collective-permute-start(f32[256,256]{1,0:T(8,128)S(1)} %add_add_fusion.2), channel_id=1, source_target_pairs={{0,12},{1,13},{16,28},{17,29}} | collective-permute-start | bytes 786440 | tf_op jit(solution)/shard_map/ppermute | solution.py:531
  639.4 13.9 %collective-permute-start.14 = (f32[256,256]{1,0:T(8,128)S(1)}, f32[256,256]{1,0:T(8,128)S(1)}, u32[]{:S(2)}, u32[]{:S(2)}) collective-permute-start(f32[256,256]{1,0:T(8,128)S(1)} %add_add_fusion.2), channel_id=1, source_target_pairs={{0,10},{1,11},{16,26},{17,27}} | collective-permute-start | bytes 786440 | tf_op jit(solution)/shard_map/ppermute | solution.py:531
  645.0 11.2 %collective-permute-start.13 = (f32[256,256]{1,0:T(8,128)S(1)}, f32[256,256]{1,0:T(8,128)S(1)}, u32[]{:S(2)}, u32[]{:S(2)}) collective-permute-start(f32[256,256]{1,0:T(8,128)S(1)} %add_add_fusion.2), channel_id=1, source_target_pairs={{0,8},{1,9},{16,24},{17,25}} | collective-permute-start | bytes 786440 | tf_op jit(solution)/shard_map/ppermute | solution.py:531
  646.3 2.7 copy-start.3
  646.3 16.3 %collective-permute-start.12 = (f32[256,256]{1,0:T(8,128)S(1)}, f32[256,256]{1,0:T(8,128)S(1)}, u32[]{:S(2)}, u32[]{:S(2)}) collective-permute-start(f32[256,256]{1,0:T(8,128)S(1)} %add_add_fusion.2), channel_id=1, source_target_pairs={{0,6},{1,7},{16,22},{17,23}} | collective-permute-start | bytes 786440 | tf_op jit(solution)/shard_map/ppermute | solution.py:531
  647.7 18.0 %collective-permute-start.11 = (f32[256,256]{1,0:T(8,128)S(1)}, f32[256,256]{1,0:T(8,128)S(1)}, u32[]{:S(2)}, u32[]{:S(2)}) collective-permute-start(f32[256,256]{1,0:T(8,128)S(1)} %add_add_fusion.2), channel_id=1, source_target_pairs={{0,4},{1,5},{16,20},{17,21}} | collective-permute-start | bytes 786440 | tf_op jit(solution)/shard_map/ppermute | solution.py:531
  649.0 16.7 %collective-permute-start.10 = (f32[256,256]{1,0:T(8,128)S(1)}, f32[256,256]{1,0:T(8,128)S(1)}, u32[]{:S(2)}, u32[]{:S(2)}) collective-permute-start(f32[256,256]{1,0:T(8,128)S(1)} %add_add_fusion.2), channel_id=1, source_target_pairs={{0,2},{1,3},{16,18},{17,19}} | collective-permute-start | bytes 786440 | tf_op jit(solution)/shard_map/ppermute | solution.py:531
  653.3 50.9 %collective-permute-start.22 = (f32[1536,256]{1,0:T(8,128)S(1)}, f32[1536,256]{1,0:T(8,128)}, u32[]{:S(2)}, u32[]{:S(2)}) collective-permute-start(f32[1536,256]{1,0:T(8,128)S(1)} %add_add_fusion), channel_id=1, source_target_pairs={{0,4},{2,6},{5,9},{7,11},{24,28},{26,30},{29,17},{31,19}} | collective-permute-start | bytes 4718600 | tf_op jit(solution)/shard_map/ppermute | solution.py:546
  656.2 47.9 %collective-permute-start.21 = (f32[1536,256]{1,0:T(8,128)S(1)}, f32[1536,256]{1,0:T(8,128)}, u32[]{:S(2)}, u32[]{:S(2)}) collective-permute-start(f32[1536,256]{1,0:T(8,128)S(1)} %add_add_fusion), channel_id=1, source_target_pairs={{0,8},{2,10},{5,13},{7,15},{24,16},{26,18},{29,21},{31,23}} | collective-permute-start | bytes 4718600 | tf_op jit(solution)/shard_map/ppermute | solution.py:546
  662.7 53.5 %collective-permute-start.20 = (f32[1536,256]{1,0:T(8,128)S(1)}, f32[1536,256]{1,0:T(8,128)}, u32[]{:S(2)}, u32[]{:S(2)}) collective-permute-start(f32[1536,256]{1,0:T(8,128)S(1)} %add_add_fusion), channel_id=1, source_target_pairs={{0,12},{2,14},{5,1},{7,3},{24,20},{26,22},{29,25},{31,27}} | collective-permute-start | bytes 4718600 | tf_op jit(solution)/shard_map/ppermute | solution.py:546
  716.6 34.5 %collective-permute-start.23 = (f32[1536,256]{1,0:T(8,128)S(1)}, f32[1536,256]{1,0:T(8,128)}, u32[]{:S(2)}, u32[]{:S(2)}) collective-permute-start(f32[1536,256]{1,0:T(8,128)S(1)} %select_select_fusion), channel_id=1, source_target_pairs={{0,2},{2,0},{4,6},{6,4},{8,10},{10,8},{12,14},{14,12},{1,3},{3,1},... | collective-permute-start | bytes 4718600 | tf_op jit(solution)/shard_map/ppermute | solution.py:553
Sparse Core Ops, SparseCore 0:
  17.5 127.5 all-gather.2
  147.1 206.1 all-gather.4

commit v4 on v3

--- a/solution.py
+++ b/solution.py
@@ -241,6 +241,42 @@
         compiler_params=params(),
         cost_estimate=cost(0, 8 * root.shape[0] * RP + 4 * sum(p.size for p in parts)),
     )(row_slot, row_valid, jnp.concatenate(col_places, axis=1), root, *parts, *parts)
+
+
+def pivot_part(root, outgoing, row_child, row_place, col_places, flag):
+    count = len(outgoing)
+    cap_row = row_child.shape[0]
+    _, col_count, width, _, _ = outgoing[0].shape
+
+    def body(child_ref, row_ref, place_ref, flag_ref, root_ref, *rest):
+        a_refs, out_ref = rest[:-1], rest[-1]
+        out_ref[...] = jnp.where(flag_ref[0] == 1, root_ref[...], 0.0)
+        for w in range(cap_row):
+            row = row_ref[w]
+            for k in range(count * col_count * width):
+                j, q, u = k // (col_count * width), k // width % col_count, k % width
+                col = place_ref[child_ref[w], k]
+
+                @pl.when((row >= 0) & (row < RP // BLK) & (col >= 0) & (col < RP // BLK))
+                def _():
+                    at_row = pl.ds(pl.multiple_of(row * BLK, BLK), BLK)
+                    at_col = pl.ds(pl.multiple_of(col * BLK, BLK), BLK)
+                    out_ref[at_row, at_col] += a_refs[j][w, q, u]
+
+    corner = pl.BlockSpec((RP, RP), lambda i, c, r, p, f: (0, 0))
+    leading = pl.BlockSpec((cap_row, col_count, width, BLK, BLK), lambda i, c, r, p, f: (0,) * 5)
+    return pl.pallas_call(
+        body,
+        grid_spec=pltpu.PrefetchScalarGridSpec(
+            num_scalar_prefetch=4,
+            grid=(1,),
+            in_specs=[corner] + [leading] * count,
+            out_specs=corner,
+        ),
+        out_shape=jax.ShapeDtypeStruct((RP, RP), F32),
+        compiler_params=params(),
+        cost_estimate=cost(0, 8 * RP * RP + 4 * count * cap_row * col_count * width * BLK * BLK),
+    )(row_child, row_place, jnp.concatenate(col_places, axis=1), flag.reshape(1), root, *outgoing)
 
 
 def advance(root, parts, own_rows, columns, row_slot, row_valid, col_places, flags):
@@ -466,84 +502,103 @@
     row_slot = jnp.maximum(row_slot - 1, 0).reshape(-1)
 
     pick_mine = (pick_item // child_blocks == half).astype(jnp.int32)
-    panels = []
+    picked = []
     for h in range(halves):
         at = slice(h * half_pick, (h + 1) * half_pick)
-        picked = pick_rows(own_panel, other_panel, pick_item[at] % child_blocks, pick_mine[at])
-        panels.append(lax.all_gather(picked, "prow", axis=0, tiled=True))
+        picked.append(pick_rows(own_panel, other_panel, pick_item[at] % child_blocks, pick_mine[at]))
 
     device = lambda g, r: ((g // col_count) * row_count + r) * col_count + g % col_count
     everyone = ("half", "prow", "pcol")
     distance = (group + iota(group_count)) % group_count
     origins = (group - iota(group_count)) % group_count
     arrived = []
+    packed = [pack_columns(child_update[0], chosen[distance, h]) for h in range(halves)]
+    origins, picked[1:], packed[1:] = lax.optimization_barrier((origins, picked[1:], packed[1:]))
+    panels = [lax.all_gather(value, "prow", axis=0, tiled=True) for value in picked]
     for h in range(halves):
-        picks = chosen[distance, h]
         if arrived:
-            picks, arrived[-1] = lax.optimization_barrier((picks, arrived[-1]))
-        packed = pack_columns(child_update[0], picks)
-        got = [packed[0]]
+            packed[h], arrived[-1] = lax.optimization_barrier((packed[h], arrived[-1]))
+        got = [packed[h][0]]
         for d in range(1, group_count):
             pairs = [
                 (device(g, r), device((g + d) % group_count, r))
                 for g in range(group_count)
                 for r in range(row_count)
             ]
-            got.append(lax.ppermute(packed[d], everyone, pairs))
+            got.append(lax.ppermute(packed[h][d], everyone, pairs))
         arrived.append(got)
 
-    parts, col_places = [], []
+    outgoing, parts, col_places = [], [], []
     for h in range(halves):
         for first in range(0, half_col, width):
             at = slice(h * half_col + first, h * half_col + first + width)
             col_places.append(col_local[:, :, at].reshape(2, -1))
-            outgoing = schur_rows(
-                own_panel,
-                other_panel,
-                arrived[h],
-                panels[h],
-                half,
-                item_slot,
-                place[:, :, at].reshape(-1),
-                origins,
-                row_count * cap_row,
-                col_count,
-                (first, width),
+            if len(outgoing) == 1:
+                origins, outgoing[0], arrived = lax.optimization_barrier(
+                    (origins, outgoing[0], arrived)
+                )
+            elif outgoing:
+                origins, outgoing[-1] = lax.optimization_barrier((origins, outgoing[-1]))
+            outgoing.append(
+                schur_rows(
+                    own_panel,
+                    other_panel,
+                    arrived[h],
+                    panels[h],
+                    half,
+                    item_slot,
+                    place[:, :, at].reshape(-1),
+                    origins,
+                    row_count * cap_row,
+                    col_count,
+                    (first, width),
+                )
             )
-            parts.append(lax.all_to_all(outgoing, "prow", split_axis=0, concat_axis=0, tiled=True))
-
+            parts.append(
+                lax.all_to_all(outgoing[-1], "prow", split_axis=0, concat_axis=0, tiled=True)
+            )
     early = max(1, len(parts) // halves)
-    raw = first_panel(root_front, parts[:early], row_slot, row_valid, col_places[:early])
-
-    def to_groups(value):
-        total = jnp.where(group == 0, value, 0.0)
-        for g in range(1, group_count):
-            pairs = [(device(0, r), device(g, r)) for r in range(row_count)]
-            total = total + lax.ppermute(value, everyone, pairs)
-        return total
-
-    corner = raw[:RP]
-    first = jnp.where(group == 0, corner, 0.0)
-    for g in range(1, group_count):
-        first = first + lax.ppermute(corner, everyone, [(device(0, 0), device(g, 0))])
-    pivot = jnp.where(prow == 0, first, 0.0)
-    for r in range(1, row_count):
-        pivot = pivot + lax.ppermute(first, "prow", [(0, r)])
+
+    to_first = (own_owner == 0)[None, :] & (own_row_rank[None, :] == iota(cap_row)[:, None])
+    own_joint = here(joint, prow, 0, keepdims=False)
+    row_child = jnp.sum(jnp.where(to_first, iota(items) // child_blocks, 0), axis=1)
+    row_place = jnp.sum(jnp.where(to_first, own_joint + 1, 0), axis=1) - 1
+    pivot = pivot_part(
+        root_front,
+        outgoing[:early],
+        row_child,
+        row_place,
+        col_places[:early],
+        ((prow == 0) & (group == 0)).astype(jnp.int32),
+    )
+    step = 1
+    while step < row_count:
+        pivot = pivot + lax.ppermute(pivot, "prow", [(r, r ^ step) for r in range(row_count)])
+        step *= 2
+    pivot, parts[0] = lax.optimization_barrier((pivot, parts[0]))
     factor = jnp.linalg.cholesky(pivot)
     inverse = lax.linalg.triangular_solve(
         factor, jnp.eye(RP, dtype=F32), left_side=True, lower=True
     )
-    raw_rows = to_groups(raw)
+
+    raw = first_panel(root_front, parts[:early], row_slot, row_valid, col_places[:early])
+    solved = lax.dot_general(raw, inverse, NT, precision=HIGHEST, preferred_element_type=F32)
+    top = jnp.where(prow == 0, factor, solved[:RP])
+    solved = jnp.concatenate([top, solved[RP:]], axis=0)
+    own_rows = jnp.where(group == 0, solved, 0.0)
+    for g in range(1, group_count):
+        pairs = [(device(0, r), device(g, r)) for r in range(row_count)]
+        own_rows = own_rows + lax.ppermute(solved, everyone, pairs)
     groups_of = row_count // ratio
     shift = (prow // ratio - group) % groups_of
-    tile = jnp.where(shift == 0, raw_rows, 0.0)
+    tile = jnp.where(shift == 0, own_rows, 0.0)
     for k in range(1, groups_of):
         pairs = [
             (device(g, g * ratio + o), device(g, ((g + k) % groups_of) * ratio + o))
             for g in range(group_count)
             for o in range(ratio)
         ]
-        got = lax.ppermute(raw_rows, ("half", "prow", "pcol"), pairs)
+        got = lax.ppermute(own_rows, everyone, pairs)
         tile = jnp.where(shift == k, got, tile)
     tiles = [tile]
     for o in range(1, ratio):
@@ -558,13 +613,7 @@
         for k in range(1, ratio):
             value = jnp.where((offset - k) % ratio == o, tiles[k], value)
         ordered.append(value)
-    raw_cols = jnp.concatenate(ordered, axis=0)
-    solved = lax.dot_general(raw_rows, inverse, NT, precision=HIGHEST, preferred_element_type=F32)
-    lower_cols = lax.dot_general(
-        raw_cols, inverse, NT, precision=HIGHEST, preferred_element_type=F32
-    )
-    top = jnp.where(prow == 0, factor, solved[:RP])
-    own_rows = jnp.concatenate([top, solved[RP:]], axis=0)
+    lower_cols = jnp.concatenate(ordered, axis=0)
     flags = jnp.stack([(prow == 0), (group == 0)]).astype(jnp.int32)
     late = max(1, len(parts) - 1)
     root = advance(

time: 815 us -> 865 us (1.061)
  waiting for transfers between devices: 486 us -> 550 us
  starting transfers between devices: 63.2 us -> 50.2 us
    ppermute x22 -> x15, waiting for transfers between devices: 258 us -> 358 us  [the longest x6 167 us: shards(): got.append(lax.ppermute(packed[h][d], everyone, pairs))]
    all_to_all x4, waiting for transfers between devices: 205 us -> 132 us  [shards(): lax.all_to_all(outgoing[-1], 'prow', split_axis=0, concat_axis=0, tiled=T...]
    ppermute x1, waiting for transfers between devices: 0.01 us -> 24.4 us  [shards(): tiles.append(lax.ppermute(tile, 'prow', pairs))]
    ppermute x22 -> x15, starting transfers between devices: 43 us -> 29.2 us  [the longest x3 9.35 us: shards(): own_rows = own_rows + lax.ppermute(solved, everyone, pairs)]
    all_gather x2, waiting for transfers between devices: 20.5 us -> 33.9 us  [shards(): lax.all_gather(value, 'prow', axis=0, tiled=True)]
  transfers between devices with their start and end apart: 30 -> 23, of which waited for: 13 -> 17; matrix products, arithmetic and copies ran while one was open for 12% -> 10% of each run, Pallas kernels for 15% -> 15%
where the time goes in v4:
time: 865 us; the launch traced here: 854 us
  waiting for transfers between devices  550 us (64%)
  Pallas kernels  149 us (17%)
  other arithmetic  69.6 us (8%)
  starting transfers between devices  50.2 us (6%)
  local copies, waits for them, and re-layouts  15.7 us (2%)
  between operations  15.2 us (2%)
    ppermute x6, waiting for transfers between devices, shards(): got.append(lax.ppermute(packed[h][d], everyone, pairs))  167 us
    all_to_all x4, waiting for transfers between devices, shards(): lax.all_to_all(outgoing[-1], 'prow', split_axis=0, concat_axis=0, tiled=T...  132 us
    ppermute x3, waiting for transfers between devices, shards(): got = lax.ppermute(own_rows, everyone, pairs)  93.4 us
    ppermute x3, waiting for transfers between devices, shards(): lax.ppermute(pivot, 'prow', [(r, r ^ step) for r in range(row_count)])  89.8 us
    pallas_call x4, Pallas kernels, schur_rows(): pl.pallas_call(body, grid_spec=pltpu.PrefetchScalarGridSpec(num_scalar_pr...  65.8 us
    another operation x7, other arithmetic, shards(): factor = jnp.linalg.cholesky(pivot)  34.7 us
    all_gather x2, waiting for transfers between devices, shards(): lax.all_gather(value, 'prow', axis=0, tiled=True)  33.9 us
    pallas_call x1, Pallas kernels, advance(): pl.pallas_call(body, grid_spec=pltpu.PrefetchScalarGridSpec(num_scalar_pr...  28 us
  transfers between devices with their start and end apart: 23, of which 17 were waited for; matrix products, arithmetic and copies ran while one was open for 10% of the time, Pallas kernels for 15%

profile of v4, /device:TPU:0, one launch (start us, length us, event | category | flops | bytes accessed | tf_op | source)
XLA Modules:
  0.0 854.3 jit_solution(16031149414097255816)
XLA Ops:
  7.0 0.8 eq.190
  8.6 0.7 reduce_window_sum.13
  12.1 2.0 collective-permute-done.other_ref
  14.1 3.2 shard_map.49
  19.7 7.7 shard_map.48
  27.4 2.9 collective-permute-start.1
  31.8 7.7 shard_map.47
  40.2 0.7 reshape.444.place_ref
  41.9 3.1 shard_map.46
  45.0 31.6 %collective-permute-done.1.rest_1_ = f32[4,1024,128]{2,1,0:T(8,128)S(1)} collective-permute-done((f32[4,1024,128]{2,1,0:T(8,128)}, f32[4,1024,128]{2,1,0:T(8,128)S(1)}, u32[]{:S(2)}, u32[]{:S(2)}) %collective-permute-start.1) | collective-permute-done | bytes 2097184 | tf_op jit(solution)/shard_map/ppermute | solution.py:528
  76.6 44.9 %collective-permute-done.3.rest_3_ = f32[4,1024,128]{2,1,0:T(8,128)} collective-permute-done((f32[4,1024,128]{2,1,0:T(8,128)}, f32[4,1024,128]{2,1,0:T(8,128)}, u32[]{:S(2)}, u32[]{:S(2)}) %collective-permute-start.3) | collective-permute-done | bytes 2097184 | tf_op jit(solution)/shard_map/ppermute | solution.py:528
  121.5 23.6 %all-gather.3.cloned.1.call-done.rest_4_ = f32[16,128,1024]{2,1,0:T(8,128)} async-done(((f32[2,128,1024]{2,1,0:T(8,128)}), f32[16,128,1024]{2,1,0:T(8,128)}) %all-gather.3.cloned.1.call-update) | async-done | bytes 8388624 | tf_op jit(solution)/shard_map/all_gather | solution.py:517
  145.0 16.6 %shard_map.50.rest_0_ = f32[16,2,2,128,128]{4,3,2,1,0:T(8,128)} custom-call(s32[1]{0:T(128)} %bitcast.15.half_ref, s32[16]{0:T(128)} %bitcast_add_fusion.1.slot_ref, s32[8]{0:T(128)} %reshape.444.place_ref, s32[4]{0:T(128)} %and_select_fusion.4.origin_ref, f32[1024,1024]{1,0:T(8,128)} %bitcast.83, f32[1024,1024]{1,0:T(8,128)} %collective-permute-done.other_ref, ...), custom_call_target="tpu_custom_call" | custom-call | flops 6442450944 | bytes 20971520 | tf_op jit(solution)/shard_map/pallas_call | solution.py:176
  161.7 4.6 all-to-all-start
  166.3 1.5 collective-permute-start.4
  168.7 45.8 %collective-permute-done.4.rest_1_ = f32[4,1024,128]{2,1,0:T(8,128)S(1)} collective-permute-done((f32[4,1024,128]{2,1,0:T(8,128)}, f32[4,1024,128]{2,1,0:T(8,128)S(1)}, u32[]{:S(2)}, u32[]{:S(2)}) %collective-permute-start.4) | collective-permute-done | bytes 2097184 | tf_op jit(solution)/shard_map/ppermute | solution.py:528
  214.4 45.1 %collective-permute-done.6.rest_3_ = f32[4,1024,128]{2,1,0:T(8,128)} collective-permute-done((f32[4,1024,128]{2,1,0:T(8,128)}, f32[4,1024,128]{2,1,0:T(8,128)}, u32[]{:S(2)}, u32[]{:S(2)}) %collective-permute-start.6) | collective-permute-done | bytes 2097184 | tf_op jit(solution)/shard_map/ppermute | solution.py:528
  259.5 16.4 %shard_map.51.rest_1_ = f32[16,2,2,128,128]{4,3,2,1,0:T(8,128)} custom-call(s32[1]{0:T(128)} %bitcast.15.half_ref, s32[16]{0:T(128)} %bitcast_add_fusion.1.slot_ref, s32[8]{0:T(128)} %reshape.446.place_ref, s32[4]{0:T(128)} %and_select_fusion.4.origin_ref, f32[1024,1024]{1,0:T(8,128)} %bitcast.84, f32[1024,1024]{1,0:T(8,128)} %collective-permute-done.other_ref, ...), custom_call_target="tpu_custom_call" | custom-call | flops 6442450944 | bytes 20971520 | tf_op jit(solution)/shard_map/pallas_call | solution.py:176
  275.9 61.9 %all-to-all-done.rest_0_.rest_2_.rest_3_ = f32[16,2,2,128,128]{4,3,2,1,0:T(8,128)} async-done(((f32[16,2,2,128,128]{4,3,2,1,0:T(8,128)}), f32[16,2,2,128,128]{4,3,2,1,0:T(8,128)}, u32[]{:S(2)}, u32[]{:S(2)}) %all-to-all-start) | async-done | bytes 4194336 | tf_op jit(solution)/shard_map/all_to_all | solution.py:558
  337.8 4.6 all-to-all-start.1
  343.1 10.3 %all-gather.5.cloned.1.call-done.rest_4_ = f32[16,128,1024]{2,1,0:T(8,128)} async-done(((f32[2,128,1024]{2,1,0:T(8,128)}), f32[16,128,1024]{2,1,0:T(8,128)}) %all-gather.5.cloned.1.call-update) | async-done | bytes 8388624 | tf_op jit(solution)/shard_map/all_gather | solution.py:517
  353.4 16.4 %shard_map.53 = f32[16,2,2,128,128]{4,3,2,1,0:T(8,128)} custom-call(s32[1]{0:T(128)} %bitcast.15.half_ref, s32[16]{0:T(128)} %bitcast_add_fusion.1.slot_ref, s32[8]{0:T(128)} %reshape.447.place_ref, s32[4]{0:T(128)} %and_select_fusion.4.origin_ref, f32[1024,1024]{1,0:T(8,128)} %bitcast.85, f32[1024,1024]{1,0:T(8,128)} %collective-permute-done.other_ref, ...), custom_call_target="tpu_custom_call" | custom-call | flops 6442450944 | bytes 20971520 | tf_op jit(solution)/shard_map/pallas_call | solution.py:176
  369.8 70.0 %all-to-all-done.1.rest_1_.rest_3_.rest_4_ = f32[16,2,2,128,128]{4,3,2,1,0:T(8,128)} async-done(((f32[16,2,2,128,128]{4,3,2,1,0:T(8,128)}), f32[16,2,2,128,128]{4,3,2,1,0:T(8,128)}, u32[]{:S(2)}, u32[]{:S(2)}) %all-to-all-start.1) | async-done | bytes 4194336 | tf_op jit(solution)/shard_map/all_to_all | solution.py:558
  439.8 4.6 all-to-all-start.2
  444.7 0.7 pad_add_fusion.2.place_ref
  445.3 0.7 select_reduce_fusion.6
  446.6 3.1 shard_map.52
  449.7 1.1 copy.26
  450.8 1.9 collective-permute-start.7
  452.7 32.4 %collective-permute-done.7 = f32[256,256]{0,1:T(8,128)S(1)} collective-permute-done((f32[256,256]{0,1:T(8,128)S(1)}, f32[256,256]{0,1:T(8,128)S(1)}, u32[]{:S(2)}, u32[]{:S(2)}) %collective-permute-start.7) | collective-permute-done | bytes 262176 | tf_op jit(solution)/shard_map/ppermute | solution.py:576
  485.8 32.9 %collective-permute-done.8 = f32[256,256]{0,1:T(8,128)S(1)} collective-permute-done((f32[256,256]{0,1:T(8,128)S(1)}, f32[256,256]{0,1:T(8,128)S(1)}, u32[]{:S(2)}, u32[]{:S(2)}) %collective-permute-start.8) | collective-permute-done | bytes 262176 | tf_op jit(solution)/shard_map/ppermute | solution.py:576
  518.8 3.6 collective-permute-start.9
  524.3 24.5 %collective-permute-done.9 = f32[256,256]{0,1:T(8,128)S(1)} collective-permute-done((f32[256,256]{0,1:T(8,128)S(1)}, f32[256,256]{0,1:T(8,128)S(1)}, u32[]{:S(2)}, u32[]{:S(2)}) %collective-permute-start.9) | collective-permute-done | bytes 262176 | tf_op jit(solution)/shard_map/ppermute | solution.py:576
  549.1 11.7 %cholesky.50 = f32[128,128]{1,0:T(8,128)S(1)} custom-call(f32[128,128]{1,0:T(8,128)S(1)} %cholesky.118), custom_call_target="Cholesky" | custom-call | tf_op jit(solution)/shard_map/jit(cholesky)/cholesky | solution.py:579
  560.9 9.8 %custom-call.14 = f32[1,128,128]{1,2,0:T(8,128)S(1)} custom-call(f32[1,128,128]{2,1,0:T(8,128)S(1)} %get-tuple-element.114), custom_call_target="InvertDiagBlocksLowerTriangular" | custom-call | tf_op jit(solution)/shard_map/jit(cholesky)/cholesky | solution.py:579
  571.2 11.7 %cholesky.105 = f32[128,128]{1,0:T(8,128)S(1)} custom-call(f32[128,128]{1,0:T(8,128)S(1)} %convolution_subtract_fusion.1), custom_call_target="Cholesky" | custom-call | tf_op jit(solution)/shard_map/jit(cholesky)/cholesky | solution.py:579
  582.9 0.7 compare_reduce_fusion
  583.6 0.7 compare_reduce_fusion.1
  585.7 4.3 while.1
  586.6 1.4 bitcast_dynamic-update-slice_fusion.2
  588.6 1.4 bitcast_dynamic-update-slice_fusion.2
  590.0 19.7 %custom-call.15 = f32[2,128,128]{1,2,0:T(8,128)S(1)} custom-call(f32[2,128,128]{2,1,0:T(8,128)S(1)} %get-tuple-element.86), custom_call_target="InvertDiagBlocksLowerTriangular" | custom-call | tf_op jit(solution)/shard_map/triangular_solve | solution.py:580
  609.7 11.2 %shard_map.54 = f32[1536,256]{1,0:T(8,128)} custom-call(s32[24]{0:T(128)} %max.46.slot_ref, s32[24]{0:T(128)} %reshape.468.valid_ref, s32[2,8]{1,0:T(2,128)} %pad_add_fusion.2.place_ref, f32[1536,3072]{1,0:T(8,128)} %root_ref.5, f32[16,2,2,128,128]{4,3,2,1,0:T(8,128)} %all-to-all-done.rest_0_.rest_2_.rest_3_, ...), custom_call_target="tpu_custom_call" | custom-call | bytes 11534336 | tf_op jit(solution)/shard_map/pallas_call | solution.py:232
  621.7 2.8 fusion
  624.8 4.4 collective-permute-start.10
  629.3 2.4 collective-permute-start.11
  631.7 2.5 collective-permute-start.12
  634.2 16.4 %shard_map.56 = f32[16,2,2,128,128]{4,3,2,1,0:T(8,128)} custom-call(s32[1]{0:T(128)} %bitcast.15.half_ref, s32[16]{0:T(128)} %bitcast_add_fusion.1.slot_ref, s32[8]{0:T(128)} %reshape.448.place_ref, s32[4]{0:T(128)} %and_select_fusion.4.origin_ref, f32[1024,1024]{1,0:T(8,128)} %bitcast.86, f32[1024,1024]{1,0:T(8,128)} %collective-permute-done.other_ref, ...), custom_call_target="tpu_custom_call" | custom-call | flops 6442450944 | bytes 20971520 | tf_op jit(solution)/shard_map/pallas_call | solution.py:176
  650.6 4.6 all-to-all-start.3
  655.2 7.7 collective-permute-done.12
  662.9 2.8 add_add_fusion.rest_6_
  665.6 4.0 collective-permute-start.13
  669.6 2.5 collective-permute-start.14
  672.1 2.4 collective-permute-start.15
  674.5 59.7 %collective-permute-done.13 = f32[1536,256]{1,0:T(8,128)S(1)} collective-permute-done((f32[1536,256]{1,0:T(8,128)S(1)}, f32[1536,256]{1,0:T(8,128)S(1)}, u32[]{:S(2)}, u32[]{:S(2)}) %collective-permute-start.13) | collective-permute-done | bytes 1572896 | tf_op jit(solution)/shard_map/ppermute | solution.py:601
  734.2 16.9 %collective-permute-done.14 = f32[1536,256]{1,0:T(8,128)} collective-permute-done((f32[1536,256]{1,0:T(8,128)S(1)}, f32[1536,256]{1,0:T(8,128)}, u32[]{:S(2)}, u32[]{:S(2)}) %collective-permute-start.14) | collective-permute-done | bytes 1572896 | tf_op jit(solution)/shard_map/ppermute | solution.py:601
  751.1 16.9 %collective-permute-done.15 = f32[1536,256]{1,0:T(8,128)} collective-permute-done((f32[1536,256]{1,0:T(8,128)S(1)}, f32[1536,256]{1,0:T(8,128)}, u32[]{:S(2)}, u32[]{:S(2)}) %collective-permute-start.15) | collective-permute-done | bytes 1572896 | tf_op jit(solution)/shard_map/ppermute | solution.py:601
  768.3 2.2 collective-permute-start.16
  770.6 0.7 reshape.434.place_ref
  772.5 24.4 %collective-permute-done.16 = f32[1536,256]{1,0:T(8,128)} collective-permute-done((f32[1536,256]{1,0:T(8,128)S(1)}, f32[1536,256]{1,0:T(8,128)}, u32[]{:S(2)}, u32[]{:S(2)}) %collective-permute-start.16) | collective-permute-done | bytes 1572896 | tf_op jit(solution)/shard_map/ppermute | solution.py:608
  796.9 1.6 broadcast_select_fusion.1
  798.5 1.8 pad_maximum_fusion.rest_7_
  800.3 28.0 %shard_map.55.root_ref = f32[1536,3072]{1,0:T(8,128)} custom-call(s32[24]{0:T(128)} %max.46.slot_ref, s32[24]{0:T(128)} %reshape.468.valid_ref, s32[2,12]{1,0:T(2,128)} %pad_add_fusion.1.place_ref, s32[2]{0:T(128)} %add_convert_fusion.flag_ref, f32[1536,3072]{1,0:T(8,128)} %root_ref.5, f32[16,2,2,128,128]{4,3,2,1,0:T(8,128)} %all-to-all-done.rest_0_.rest_2_.rest_3_, ...), custom_call_target="tpu_custom_call" | custom-call | flops 7247757312 | bytes 50331648 | tf_op jit(solution)/shard_map/pallas_call | solution.py:336
  828.3 19.1 %shard_map.57 = f32[1536,3072]{1,0:T(8,128)} custom-call(s32[24]{0:T(128)} %max.46.slot_ref, s32[24]{0:T(128)} %reshape.468.valid_ref, s32[2,4]{1,0:T(2,128)} %reshape.434.place_ref, f32[1536,3072]{1,0:T(8,128)} %shard_map.55.root_ref, f32[16,2,2,128,128]{4,3,2,1,0:T(8,128)} %all-to-all-done.3.a0_ref.a1_ref, f32[16,2,2,128,128]{4,3,2,1,0:T(8,128)} %all-to-all-done.3.a0_ref.a1_ref), custom_call_target="tpu_custom_call" | custom-call | bytes 41943040 | tf_op jit(solution)/shard_map/pallas_call | solution.py:394
  (137 shorter events, 19.5 us)
Async XLA Ops:
  6.5 138.5 %all-gather.3.cloned.1.call-start = ((), (), s32[]{:S(2)}) async-start(), calls=%async_computation.4 | async-start | bytes 9437184 | tf_op jit(solution)/shard_map/all_gather | solution.py:517
  6.5 7.6 collective-permute-start
  14.1 3.4 copy-start.4
  17.3 336.0 %all-gather.5.cloned.1.call-start = ((), (), s32[]{:S(2)}) async-start(), calls=%async_computation.5 | async-start | bytes 9437184 | tf_op jit(solution)/shard_map/all_gather | solution.py:517
  27.4 49.2 %collective-permute-start.1 = (f32[4,1024,128]{2,1,0:T(8,128)}, f32[4,1024,128]{2,1,0:T(8,128)S(1)}, u32[]{:S(2)}, u32[]{:S(2)}) collective-permute-start(f32[4,1024,128]{2,1,0:T(8,128)} %get-tuple-element.52), channel_id=1, source_target_pairs={{0,1},{2,3},{4,5},{6,7},{8,9},{10,11},{12,13},{14,15},{1,16},{3,18... | collective-permute-start | bytes 6291464 | tf_op jit(solution)/shard_map/ppermute | solution.py:528
  30.3 46.3 %collective-permute-start.2 = (f32[4,1024,128]{2,1,0:T(8,128)}, f32[4,1024,128]{2,1,0:T(8,128)}, u32[]{:S(2)}, u32[]{:S(2)}) collective-permute-start(f32[4,1024,128]{2,1,0:T(8,128)} %get-tuple-element.53), channel_id=1, source_target_pairs={{0,16},{2,18},{4,20},{6,22},{8,24},{10,26},{12,28},{14,30},{1,17},... | collective-permute-start | bytes 6291464 | tf_op jit(solution)/shard_map/ppermute | solution.py:528
  30.3 91.2 %collective-permute-start.3 = (f32[4,1024,128]{2,1,0:T(8,128)}, f32[4,1024,128]{2,1,0:T(8,128)}, u32[]{:S(2)}, u32[]{:S(2)}) collective-permute-start(f32[4,1024,128]{2,1,0:T(8,128)} %get-tuple-element.54), channel_id=1, source_target_pairs={{0,17},{2,19},{4,21},{6,23},{8,25},{10,27},{12,29},{14,31},{1,0},{... | collective-permute-start | bytes 6291464 | tf_op jit(solution)/shard_map/ppermute | solution.py:528
  76.6 68.5 %copy-start.2 = (f32[4,1024,128]{2,1,0:T(8,128)}, f32[4,1024,128]{2,1,0:T(8,128)S(1)}, u32[]{:S(2)}) copy-start(f32[4,1024,128]{2,1,0:T(8,128)S(1)} %collective-permute-done.1.rest_1_) | copy-start | bytes 6291460
  161.7 176.2 %all-to-all-start = ((f32[16,2,2,128,128]{4,3,2,1,0:T(8,128)}), f32[16,2,2,128,128]{4,3,2,1,0:T(8,128)}, u32[]{:S(2)}, u32[]{:S(2)}) async-start(f32[16,2,2,128,128]{4,3,2,1,0:T(8,128)} %shard_map.50.rest_0_), calls=%async_computation | async-start | bytes 8388608 | tf_op jit(solution)/shard_map/all_to_all | solution.py:558
  166.3 48.2 %collective-permute-start.4 = (f32[4,1024,128]{2,1,0:T(8,128)}, f32[4,1024,128]{2,1,0:T(8,128)S(1)}, u32[]{:S(2)}, u32[]{:S(2)}) collective-permute-start(f32[4,1024,128]{2,1,0:T(8,128)} %get-tuple-element.60), channel_id=1, source_target_pairs={{0,1},{2,3},{4,5},{6,7},{8,9},{10,11},{12,13},{14,15},{1,16},{3,18... | collective-permute-start | bytes 6291464 | tf_op jit(solution)/shard_map/ppermute | solution.py:528
  167.8 46.6 %collective-permute-start.5 = (f32[4,1024,128]{2,1,0:T(8,128)}, f32[4,1024,128]{2,1,0:T(8,128)}, u32[]{:S(2)}, u32[]{:S(2)}) collective-permute-start(f32[4,1024,128]{2,1,0:T(8,128)} %get-tuple-element.61), channel_id=1, source_target_pairs={{0,16},{2,18},{4,20},{6,22},{8,24},{10,26},{12,28},{14,30},{1,17},... | collective-permute-start | bytes 6291464 | tf_op jit(solution)/shard_map/ppermute | solution.py:528
  167.8 91.7 %collective-permute-start.6 = (f32[4,1024,128]{2,1,0:T(8,128)}, f32[4,1024,128]{2,1,0:T(8,128)}, u32[]{:S(2)}, u32[]{:S(2)}) collective-permute-start(f32[4,1024,128]{2,1,0:T(8,128)} %get-tuple-element.62), channel_id=1, source_target_pairs={{0,17},{2,19},{4,21},{6,23},{8,25},{10,27},{12,29},{14,31},{1,0},{... | collective-permute-start | bytes 6291464 | tf_op jit(solution)/shard_map/ppermute | solution.py:528
  214.4 61.5 %copy-start.1 = (f32[4,1024,128]{2,1,0:T(8,128)}, f32[4,1024,128]{2,1,0:T(8,128)S(1)}, u32[]{:S(2)}) copy-start(f32[4,1024,128]{2,1,0:T(8,128)S(1)} %collective-permute-done.4.rest_1_) | copy-start | bytes 6291460
  337.8 101.9 %all-to-all-start.1 = ((f32[16,2,2,128,128]{4,3,2,1,0:T(8,128)}), f32[16,2,2,128,128]{4,3,2,1,0:T(8,128)}, u32[]{:S(2)}, u32[]{:S(2)}) async-start(f32[16,2,2,128,128]{4,3,2,1,0:T(8,128)} %shard_map.51.rest_1_), calls=%async_computation.1 | async-start | bytes 8388608 | tf_op jit(solution)/shard_map/all_to_all | solution.py:558
  439.8 210.8 %all-to-all-start.2 = ((f32[16,2,2,128,128]{4,3,2,1,0:T(8,128)}), f32[16,2,2,128,128]{4,3,2,1,0:T(8,128)}, u32[]{:S(2)}, u32[]{:S(2)}) async-start(f32[16,2,2,128,128]{4,3,2,1,0:T(8,128)} %shard_map.53), calls=%async_computation.2 | async-start | bytes 8388608 | tf_op jit(solution)/shard_map/all_to_all | solution.py:558
  450.8 34.3 %collective-permute-start.7 = (f32[256,256]{0,1:T(8,128)S(1)}, f32[256,256]{0,1:T(8,128)S(1)}, u32[]{:S(2)}, u32[]{:S(2)}) collective-permute-start(f32[256,256]{0,1:T(8,128)S(1)} %copy.26), channel_id=1, source_target_pairs={{0,2},{2,0},{4,6},{6,4},{8,10},{10,8},{12,14},{14,12},{1,3},{3,1},... | collective-permute-start | bytes 786440 | tf_op jit(solution)/shard_map/ppermute | solution.py:576
  485.2 33.6 %collective-permute-start.8 = (f32[256,256]{0,1:T(8,128)S(1)}, f32[256,256]{0,1:T(8,128)S(1)}, u32[]{:S(2)}, u32[]{:S(2)}) collective-permute-start(f32[256,256]{0,1:T(8,128)S(1)} %add.312), channel_id=1, source_target_pairs={{0,4},{2,6},{4,0},{6,2},{8,12},{10,14},{12,8},{14,10},{1,5},{3,7},... | collective-permute-start | bytes 786440 | tf_op jit(solution)/shard_map/ppermute | solution.py:576
  518.8 30.0 %collective-permute-start.9 = (f32[256,256]{0,1:T(8,128)S(1)}, f32[256,256]{0,1:T(8,128)S(1)}, u32[]{:S(2)}, u32[]{:S(2)}) collective-permute-start(f32[256,256]{0,1:T(8,128)S(1)} %add.313), channel_id=1, source_target_pairs={{0,8},{2,10},{4,12},{6,14},{8,0},{10,2},{12,4},{14,6},{1,9},{3,11}... | collective-permute-start | bytes 786440 | tf_op jit(solution)/shard_map/ppermute | solution.py:576
  624.8 30.3 %collective-permute-start.10 = (f32[1536,256]{1,0:T(8,128)S(1)}, f32[1536,256]{1,0:T(8,128)}, u32[]{:S(2)}, u32[]{:S(2)}) collective-permute-start(f32[1536,256]{1,0:T(8,128)S(1)} %pad_maximum_fusion.1), channel_id=1, source_target_pairs={{0,1},{2,3},{4,5},{6,7},{8,9},{10,11},{12,13},{14,15}} | collective-permute-start | bytes 4718600 | tf_op jit(solution)/shard_map/ppermute | solution.py:591
  629.3 25.9 %collective-permute-start.11 = (f32[1536,256]{1,0:T(8,128)S(1)}, f32[1536,256]{1,0:T(8,128)}, u32[]{:S(2)}, u32[]{:S(2)}) collective-permute-start(f32[1536,256]{1,0:T(8,128)S(1)} %pad_maximum_fusion.1), channel_id=1, source_target_pairs={{0,16},{2,18},{4,20},{6,22},{8,24},{10,26},{12,28},{14,30}} | collective-permute-start | bytes 4718600 | tf_op jit(solution)/shard_map/ppermute | solution.py:591
  631.7 31.2 %collective-permute-start.12 = (f32[1536,256]{1,0:T(8,128)S(1)}, f32[1536,256]{1,0:T(8,128)}, u32[]{:S(2)}, u32[]{:S(2)}) collective-permute-start(f32[1536,256]{1,0:T(8,128)S(1)} %pad_maximum_fusion.1), channel_id=1, source_target_pairs={{0,17},{2,19},{4,21},{6,23},{8,25},{10,27},{12,29},{14,31}} | collective-permute-start | bytes 4718600 | tf_op jit(solution)/shard_map/ppermute | solution.py:591
  650.6 177.7 %all-to-all-start.3 = ((f32[16,2,2,128,128]{4,3,2,1,0:T(8,128)}), f32[16,2,2,128,128]{4,3,2,1,0:T(8,128)}, u32[]{:S(2)}, u32[]{:S(2)}) async-start(f32[16,2,2,128,128]{4,3,2,1,0:T(8,128)} %shard_map.56), calls=%async_computation.3 | async-start | bytes 8388608 | tf_op jit(solution)/shard_map/all_to_all | solution.py:558
  665.6 102.7 %copy-start = (f32[1536,256]{1,0:T(8,128)}, f32[1536,256]{1,0:T(8,128)S(1)}, u32[]{:S(2)}) copy-start(f32[1536,256]{1,0:T(8,128)S(1)} %add_add_fusion.rest_6_) | copy-start | bytes 4718596
  665.6 68.6 %collective-permute-start.13 = (f32[1536,256]{1,0:T(8,128)S(1)}, f32[1536,256]{1,0:T(8,128)S(1)}, u32[]{:S(2)}, u32[]{:S(2)}) collective-permute-start(f32[1536,256]{1,0:T(8,128)S(1)} %add_add_fusion.rest_6_), channel_id=1, source_target_pairs={{0,12},{2,14},{5,1},{7,3},{24,20},{26,22},{29,25},{31,27}} | collective-permute-start | bytes 4718600 | tf_op jit(solution)/shard_map/ppermute | solution.py:601
  669.6 81.5 %collective-permute-start.14 = (f32[1536,256]{1,0:T(8,128)S(1)}, f32[1536,256]{1,0:T(8,128)}, u32[]{:S(2)}, u32[]{:S(2)}) collective-permute-start(f32[1536,256]{1,0:T(8,128)S(1)} %add_add_fusion.rest_6_), channel_id=1, source_target_pairs={{0,8},{2,10},{5,13},{7,15},{24,16},{26,18},{29,21},{31,23}} | collective-permute-start | bytes 4718600 | tf_op jit(solution)/shard_map/ppermute | solution.py:601
  672.1 95.9 %collective-permute-start.15 = (f32[1536,256]{1,0:T(8,128)S(1)}, f32[1536,256]{1,0:T(8,128)}, u32[]{:S(2)}, u32[]{:S(2)}) collective-permute-start(f32[1536,256]{1,0:T(8,128)S(1)} %add_add_fusion.rest_6_), channel_id=1, source_target_pairs={{0,4},{2,6},{5,9},{7,11},{24,28},{26,30},{29,17},{31,19}} | collective-permute-start | bytes 4718600 | tf_op jit(solution)/shard_map/ppermute | solution.py:601
  734.2 16.9 %copy-start.3 = (f32[1536,256]{1,0:T(8,128)}, f32[1536,256]{1,0:T(8,128)S(1)}, u32[]{:S(2)}) copy-start(f32[1536,256]{1,0:T(8,128)S(1)} %collective-permute-done.13) | copy-start | bytes 4718596
  768.3 28.6 %collective-permute-start.16 = (f32[1536,256]{1,0:T(8,128)S(1)}, f32[1536,256]{1,0:T(8,128)}, u32[]{:S(2)}, u32[]{:S(2)}) collective-permute-start(f32[1536,256]{1,0:T(8,128)S(1)} %select_select_fusion), channel_id=1, source_target_pairs={{0,2},{2,0},{4,6},{6,4},{8,10},{10,8},{12,14},{14,12},{1,3},{3,1},... | collective-permute-start | bytes 4718600 | tf_op jit(solution)/shard_map/ppermute | solution.py:608
Sparse Core Ops, SparseCore 0:
  17.5 127.5 all-gather.2
  147.2 206.1 all-gather.4

commit v5 on v4

--- a/solution.py
+++ b/solution.py
@@ -285,10 +285,12 @@
     count = len(parts)
     _, col_count, width, _, _ = parts[0].shape
     step = next(w for w in (512, 384, 256) if cols % w == 0)
+    tall = 2 if row_blocks % 2 == 0 else 1
+    high = tall * BLK
 
     def body(slot_ref, valid_ref, place_ref, flag_ref, root_ref, *rest):
-        a_refs = rest[: 2 * count]
-        own_ref, col_ref, out_ref, hi_ref, lo_ref = rest[2 * count :]
+        a_refs = rest[: 2 * tall * count]
+        own_ref, col_ref, out_ref, hi_ref, lo_ref = rest[2 * tall * count :]
         r = pl.program_id(0)
 
         @pl.when(r == 0)
@@ -297,7 +299,7 @@
             hi_ref[...] = hi
             lo_ref[...] = lo
 
-        pivot_rows = (flag_ref[0] == 1) & (r < RP // BLK)
+        pivot_rows = (flag_ref[0] == 1) & (r * high < RP)
 
         @pl.when(pivot_rows)
         def _():
@@ -309,43 +311,47 @@
             stacked = jnp.concatenate([a_hi, a_lo], axis=0)
             for n in range(0, cols, step):
                 both = dot_nt(stacked, hi_ref[n : n + step, :])
-                total = both[:BLK] + both[BLK:] + dot_nt(a_hi, lo_ref[n : n + step, :])
+                total = both[:high] + both[high:] + dot_nt(a_hi, lo_ref[n : n + step, :])
                 out_ref[:, n : n + step] = root_ref[:, n : n + step] - total
 
         for c in range(2):
-            for j in range(count):
-                for q in range(col_count):
-                    for u in range(width):
-                        col = place_ref[c, (j * col_count + q) * width + u]
-
-                        @pl.when((valid_ref[c * row_blocks + r] == 1) & (col >= 0))
-                        def _():
-                            at = pl.ds(pl.multiple_of(col * BLK, BLK), BLK)
-                            out_ref[:, at] += a_refs[c * count + j][0, q, u]
+            for m in range(tall):
+
+                @pl.when(valid_ref[c * row_blocks + r * tall + m] == 1)
+                def _():
+                    for j in range(count):
+                        for q in range(col_count):
+                            for u in range(width):
+                                col = place_ref[c, (j * col_count + q) * width + u]
+                                a_ref = a_refs[(c * tall + m) * count + j]
+
+                                @pl.when(col >= 0)
+                                def _():
+                                    at = pl.ds(pl.multiple_of(col * BLK, BLK), BLK)
+                                    out_ref[m * BLK : (m + 1) * BLK, at] += a_ref[0, q, u]
 
         @pl.when(flag_ref[1] == 1)
         def _():
             out_ref[:, :RP] = own_ref[...]
 
-    def arrived(c):
+    def arrived(c, m):
         return pl.BlockSpec(
             (1, col_count, width, BLK, BLK),
-            lambda r, s, v, p, f: (s[c * row_blocks + r], 0, 0, 0, 0),
+            lambda r, s, v, p, f: (s[c * row_blocks + r * tall + m], 0, 0, 0, 0),
         )
 
     return pl.pallas_call(
         body,
         grid_spec=pltpu.PrefetchScalarGridSpec(
             num_scalar_prefetch=4,
-            grid=(row_blocks,),
-            in_specs=[pl.BlockSpec((BLK, cols), lambda r, s, v, p, f: (r, 0))]
-            + [arrived(0)] * count
-            + [arrived(1)] * count
+            grid=(row_blocks // tall,),
+            in_specs=[pl.BlockSpec((high, cols), lambda r, s, v, p, f: (r, 0))]
+            + [arrived(c, m) for c in range(2) for m in range(tall) for _ in range(count)]
             + [
-                pl.BlockSpec((BLK, RP), lambda r, s, v, p, f: (r, 0)),
+                pl.BlockSpec((high, RP), lambda r, s, v, p, f: (r, 0)),
                 pl.BlockSpec((cols, RP), lambda r, s, v, p, f: (0, 0)),
             ],
-            out_specs=pl.BlockSpec((BLK, cols), lambda r, s, v, p, f: (r, 0)),
+            out_specs=pl.BlockSpec((high, cols), lambda r, s, v, p, f: (r, 0)),
             scratch_shapes=[pltpu.VMEM((cols, RP), BF16), pltpu.VMEM((cols, RP), BF16)],
         ),
         out_shape=jax.ShapeDtypeStruct((rows, cols), F32),
@@ -357,8 +363,7 @@
         jnp.concatenate(col_places, axis=1),
         flags,
         root,
-        *parts,
-        *parts,
+        *(parts * (2 * tall)),
         own_rows,
         columns,
     )
@@ -517,7 +522,9 @@
     panels = [lax.all_gather(value, "prow", axis=0, tiled=True) for value in picked]
     for h in range(halves):
         if arrived:
-            packed[h], arrived[-1] = lax.optimization_barrier((packed[h], arrived[-1]))
+            packed[h], arrived[-1][col_count] = lax.optimization_barrier(
+                (packed[h], arrived[-1][col_count])
+            )
         got = [packed[h][0]]
         for d in range(1, group_count):
             pairs = [
@@ -528,58 +535,55 @@
             got.append(lax.ppermute(packed[h][d], everyone, pairs))
         arrived.append(got)
 
+    spans = [(h, first) for h in range(halves) for first in range(0, half_col, width)]
+    early = max(1, len(spans) // halves)
     outgoing, parts, col_places = [], [], []
-    for h in range(halves):
-        for first in range(0, half_col, width):
-            at = slice(h * half_col + first, h * half_col + first + width)
-            col_places.append(col_local[:, :, at].reshape(2, -1))
-            if len(outgoing) == 1:
-                origins, outgoing[0], arrived = lax.optimization_barrier(
-                    (origins, outgoing[0], arrived)
-                )
-            elif outgoing:
-                origins, outgoing[-1] = lax.optimization_barrier((origins, outgoing[-1]))
-            outgoing.append(
-                schur_rows(
-                    own_panel,
-                    other_panel,
-                    arrived[h],
-                    panels[h],
-                    half,
-                    item_slot,
-                    place[:, :, at].reshape(-1),
-                    origins,
-                    row_count * cap_row,
-                    col_count,
-                    (first, width),
-                )
-            )
-            parts.append(
-                lax.all_to_all(outgoing[-1], "prow", split_axis=0, concat_axis=0, tiled=True)
-            )
-    early = max(1, len(parts) // halves)
-
     to_first = (own_owner == 0)[None, :] & (own_row_rank[None, :] == iota(cap_row)[:, None])
     own_joint = here(joint, prow, 0, keepdims=False)
     row_child = jnp.sum(jnp.where(to_first, iota(items) // child_blocks, 0), axis=1)
     row_place = jnp.sum(jnp.where(to_first, own_joint + 1, 0), axis=1) - 1
-    pivot = pivot_part(
-        root_front,
-        outgoing[:early],
-        row_child,
-        row_place,
-        col_places[:early],
-        ((prow == 0) & (group == 0)).astype(jnp.int32),
-    )
-    step = 1
-    while step < row_count:
-        pivot = pivot + lax.ppermute(pivot, "prow", [(r, r ^ step) for r in range(row_count)])
-        step *= 2
-    pivot, parts[0] = lax.optimization_barrier((pivot, parts[0]))
-    factor = jnp.linalg.cholesky(pivot)
-    inverse = lax.linalg.triangular_solve(
-        factor, jnp.eye(RP, dtype=F32), left_side=True, lower=True
-    )
+    for h, first in spans:
+        at = slice(h * half_col + first, h * half_col + first + width)
+        col_places.append(col_local[:, :, at].reshape(2, -1))
+        if outgoing:
+            origins, outgoing[-1] = lax.optimization_barrier((origins, outgoing[-1]))
+        outgoing.append(
+            schur_rows(
+                own_panel,
+                other_panel,
+                arrived[h],
+                panels[h],
+                half,
+                item_slot,
+                place[:, :, at].reshape(-1),
+                origins,
+                row_count * cap_row,
+                col_count,
+                (first, width),
+            )
+        )
+        if len(outgoing) == early:
+            pivot = pivot_part(
+                root_front,
+                outgoing,
+                row_child,
+                row_place,
+                col_places,
+                ((prow == 0) & (group == 0)).astype(jnp.int32),
+            )
+            step = 1
+            while step < row_count:
+                pairs = [(r, r ^ step) for r in range(row_count)]
+                pivot = pivot + lax.ppermute(pivot, "prow", pairs)
+                step *= 2
+            factor = jnp.linalg.cholesky(pivot)
+            inverse = lax.linalg.triangular_solve(
+                factor, jnp.eye(RP, dtype=F32), left_side=True, lower=True
+            )
+            origins, inverse = lax.optimization_barrier((origins, inverse))
+    row_slot, outgoing[-1] = lax.optimization_barrier((row_slot, outgoing[-1]))
+    for value in outgoing:
+        parts.append(lax.all_to_all(value, "prow", split_axis=0, concat_axis=0, tiled=True))
 
     raw = first_panel(root_front, parts[:early], row_slot, row_valid, col_places[:early])
     solved = lax.dot_general(raw, inverse, NT, precision=HIGHEST, preferred_element_type=F32)

time: 865 us -> 849 us (0.982)
  waiting for transfers between devices: 550 us -> 536 us
    all_to_all x4, waiting for transfers between devices: 132 us -> 54 us  [shards(): lax.all_to_all(value, 'prow', split_axis=0, concat_axis=0, tiled=True)]
    ppermute x3, waiting for transfers between devices: 89.8 us -> 158 us  [shards(): pivot = pivot + lax.ppermute(pivot, 'prow', pairs)]
    ppermute x3, waiting for transfers between devices: 93.4 us -> 105 us  [shards(): got = lax.ppermute(own_rows, everyone, pairs)]
    all_gather x2, waiting for transfers between devices: 33.9 us -> 23.3 us  [shards(): lax.all_gather(value, 'prow', axis=0, tiled=True)]
    another operation x3 -> x4, other arithmetic: 19.7 us -> 19.7 us  [shards(): lax.linalg.triangular_solve(factor, jnp.eye(RP, dtype=F32), left_side=Tru...]
  transfers between devices with their start and end apart: 23 -> 23, of which waited for: 17 -> 14; matrix products, arithmetic and copies ran while one was open for 10% -> 11% of each run, Pallas kernels for 15% -> 15%
where the time goes in v5:
time: 849 us; the launch traced here: 838 us
  waiting for transfers between devices  536 us (63%)
  Pallas kernels  144 us (17%)
  other arithmetic  69.5 us (8%)
  starting transfers between devices  53.6 us (6%)
  local copies, waits for them, and re-layouts  15.4 us (2%)
  between operations  15.1 us (2%)
    ppermute x6, waiting for transfers between devices, shards(): got.append(lax.ppermute(packed[h][d], everyone, pairs))  168 us
    ppermute x3, waiting for transfers between devices, shards(): pivot = pivot + lax.ppermute(pivot, 'prow', pairs)  158 us
    ppermute x3, waiting for transfers between devices, shards(): got = lax.ppermute(own_rows, everyone, pairs)  105 us
    pallas_call x4, Pallas kernels, schur_rows(): pl.pallas_call(body, grid_spec=pltpu.PrefetchScalarGridSpec(num_scalar_pr...  65.8 us
    all_to_all x4, waiting for transfers between devices, shards(): lax.all_to_all(value, 'prow', split_axis=0, concat_axis=0, tiled=True)  54 us
    another operation x7, other arithmetic, shards(): factor = jnp.linalg.cholesky(pivot)  34.6 us
    ppermute x1, waiting for transfers between devices, shards(): tiles.append(lax.ppermute(tile, 'prow', pairs))  25.3 us
    pallas_call x1, Pallas kernels, advance(): pl.pallas_call(body, grid_spec=pltpu.PrefetchScalarGridSpec(num_scalar_pr...  24 us
  transfers between devices with their start and end apart: 23, of which 14 were waited for; matrix products, arithmetic and copies ran while one was open for 11% of the time, Pallas kernels for 15%

profile of v5, /device:TPU:0, one launch (start us, length us, event | category | flops | bytes accessed | tf_op | source)
XLA Modules:
  0.0 837.6 jit_solution(12476390005163480255)
XLA Ops:
  7.0 0.8 eq.190
  8.6 0.7 reduce_window_sum.13
  12.0 2.1 collective-permute-done.other_ref
  14.1 3.2 shard_map.49
  19.6 7.7 shard_map.48
  27.7 2.7 collective-permute-start.1
  31.6 7.7 shard_map.47
  41.7 3.1 shard_map.46
  44.8 31.9 %collective-permute-done.1.rest_1_ = f32[4,1024,128]{2,1,0:T(8,128)} collective-permute-done((f32[4,1024,128]{2,1,0:T(8,128)}, f32[4,1024,128]{2,1,0:T(8,128)}, u32[]{:S(2)}, u32[]{:S(2)}) %collective-permute-start.1) | collective-permute-done | bytes 2097184 | tf_op jit(solution)/shard_map/ppermute | solution.py:535
  76.7 45.1 %collective-permute-done.3.rest_3_ = f32[4,1024,128]{2,1,0:T(8,128)} collective-permute-done((f32[4,1024,128]{2,1,0:T(8,128)}, f32[4,1024,128]{2,1,0:T(8,128)}, u32[]{:S(2)}, u32[]{:S(2)}) %collective-permute-start.3) | collective-permute-done | bytes 2097184 | tf_op jit(solution)/shard_map/ppermute | solution.py:535
  121.8 23.3 %all-gather.3.cloned.1.call-done.rest_4_ = f32[16,128,1024]{2,1,0:T(8,128)} async-done(((f32[2,128,1024]{2,1,0:T(8,128)}), f32[16,128,1024]{2,1,0:T(8,128)}) %all-gather.3.cloned.1.call-update) | async-done | bytes 8388624 | tf_op jit(solution)/shard_map/all_gather | solution.py:522
  145.0 16.6 %shard_map.50.rest_0_ = f32[16,2,2,128,128]{4,3,2,1,0:T(8,128)} custom-call(s32[1]{0:T(128)} %bitcast.2.half_ref, s32[16]{0:T(128)} %get-tuple-element.87.slot_ref, s32[8]{0:T(128)} %reshape.436.place_ref, s32[4]{0:T(128)} %and_select_fusion.5.origin_ref, f32[1024,1024]{1,0:T(8,128)} %bitcast.83, f32[1024,1024]{1,0:T(8,128)} %collective-permute-done.other_ref, ...), custom_call_target="tpu_custom_call" | custom-call | flops 6442450944 | bytes 20971520 | tf_op jit(solution)/shard_map/pallas_call | solution.py:176
  161.7 4.6 all-to-all-start
  167.1 0.7 pad_add_fusion.1.place_ref
  167.8 0.7 select_reduce_fusion.6
  169.0 16.4 %shard_map.51.rest_1_ = f32[16,2,2,128,128]{4,3,2,1,0:T(8,128)} custom-call(s32[1]{0:T(128)} %bitcast.2.half_ref, s32[16]{0:T(128)} %get-tuple-element.87.slot_ref, s32[8]{0:T(128)} %reshape.442.place_ref, s32[4]{0:T(128)} %and_select_fusion.5.origin_ref, f32[1024,1024]{1,0:T(8,128)} %bitcast.84, f32[1024,1024]{1,0:T(8,128)} %collective-permute-done.other_ref, ...), custom_call_target="tpu_custom_call" | custom-call | flops 6442450944 | bytes 20971520 | tf_op jit(solution)/shard_map/pallas_call | solution.py:176
  185.4 3.1 shard_map.52
  188.6 1.1 copy.26
  189.7 1.9 collective-permute-start.4
  191.6 16.9 %collective-permute-done.4 = f32[256,256]{0,1:T(8,128)S(1)} collective-permute-done((f32[256,256]{0,1:T(8,128)S(1)}, f32[256,256]{0,1:T(8,128)S(1)}, u32[]{:S(2)}, u32[]{:S(2)}) %collective-permute-start.4) | collective-permute-done | bytes 262176 | tf_op jit(solution)/shard_map/ppermute | solution.py:577
  208.6 74.2 %collective-permute-done.5 = f32[256,256]{0,1:T(8,128)S(1)} collective-permute-done((f32[256,256]{0,1:T(8,128)S(1)}, f32[256,256]{0,1:T(8,128)S(1)}, u32[]{:S(2)}, u32[]{:S(2)}) %collective-permute-start.5) | collective-permute-done | bytes 262176 | tf_op jit(solution)/shard_map/ppermute | solution.py:577
  282.8 4.4 collective-permute-start.6
  287.3 67.3 %collective-permute-done.6 = f32[256,256]{0,1:T(8,128)S(1)} collective-permute-done((f32[256,256]{0,1:T(8,128)S(1)}, f32[256,256]{0,1:T(8,128)S(1)}, u32[]{:S(2)}, u32[]{:S(2)}) %collective-permute-start.6) | collective-permute-done | bytes 262176 | tf_op jit(solution)/shard_map/ppermute | solution.py:577
  354.8 11.7 %cholesky.50 = f32[128,128]{1,0:T(8,128)S(1)} custom-call(f32[128,128]{1,0:T(8,128)S(1)} %cholesky.118), custom_call_target="Cholesky" | custom-call | tf_op jit(solution)/shard_map/jit(cholesky)/cholesky | solution.py:579
  366.6 9.8 %custom-call.14 = f32[1,128,128]{1,2,0:T(8,128)S(1)} custom-call(f32[1,128,128]{2,1,0:T(8,128)S(1)} %get-tuple-element.100), custom_call_target="InvertDiagBlocksLowerTriangular" | custom-call | tf_op jit(solution)/shard_map/jit(cholesky)/cholesky | solution.py:579
  376.9 11.7 %cholesky.105 = f32[128,128]{1,0:T(8,128)S(1)} custom-call(f32[128,128]{1,0:T(8,128)S(1)} %slice_subtract_fusion), custom_call_target="Cholesky" | custom-call | tf_op jit(solution)/shard_map/jit(cholesky)/cholesky | solution.py:579
  389.3 0.7 compare_reduce_fusion.1
  391.3 4.2 while.1
  391.5 0.6 fusion.49
  392.1 1.3 bitcast_dynamic-update-slice_fusion.2
  394.1 1.3 bitcast_dynamic-update-slice_fusion.2
  395.5 19.7 %custom-call.15 = f32[2,128,128]{1,2,0:T(8,128)S(1)} custom-call(f32[2,128,128]{2,1,0:T(8,128)S(1)} %get-tuple-element.70), custom_call_target="InvertDiagBlocksLowerTriangular" | custom-call | tf_op jit(solution)/shard_map/triangular_solve | solution.py:580
  416.1 7.2 all-to-all-start.1
  423.3 1.5 collective-permute-start.7
  425.6 45.7 %collective-permute-done.7.rest_1_ = f32[4,1024,128]{2,1,0:T(8,128)S(1)} collective-permute-done((f32[4,1024,128]{2,1,0:T(8,128)}, f32[4,1024,128]{2,1,0:T(8,128)S(1)}, u32[]{:S(2)}, u32[]{:S(2)}) %collective-permute-start.7) | collective-permute-done | bytes 2097184 | tf_op jit(solution)/shard_map/ppermute | solution.py:535
  471.3 45.2 %collective-permute-done.9.rest_3_ = f32[4,1024,128]{2,1,0:T(8,128)} collective-permute-done((f32[4,1024,128]{2,1,0:T(8,128)}, f32[4,1024,128]{2,1,0:T(8,128)}, u32[]{:S(2)}, u32[]{:S(2)}) %collective-permute-start.9) | collective-permute-done | bytes 2097184 | tf_op jit(solution)/shard_map/ppermute | solution.py:535
  516.5 16.4 %shard_map.53 = f32[16,2,2,128,128]{4,3,2,1,0:T(8,128)} custom-call(s32[1]{0:T(128)} %bitcast.2.half_ref, s32[16]{0:T(128)} %get-tuple-element.87.slot_ref, s32[8]{0:T(128)} %reshape.443.place_ref, s32[4]{0:T(128)} %and_select_fusion.5.origin_ref, f32[1024,1024]{1,0:T(8,128)} %bitcast.85, f32[1024,1024]{1,0:T(8,128)} %collective-permute-done.other_ref, ...), custom_call_target="tpu_custom_call" | custom-call | flops 6442450944 | bytes 20971520 | tf_op jit(solution)/shard_map/pallas_call | solution.py:176
  532.8 6.0 all-to-all-start.2
  538.9 0.7 reshape.433.place_ref
  539.7 0.7 max.46.slot_ref
  540.9 16.4 %shard_map.54 = f32[16,2,2,128,128]{4,3,2,1,0:T(8,128)} custom-call(s32[1]{0:T(128)} %bitcast.2.half_ref, s32[16]{0:T(128)} %get-tuple-element.87.slot_ref, s32[8]{0:T(128)} %reshape.433.place_ref, s32[4]{0:T(128)} %and_select_fusion.5.origin_ref, f32[1024,1024]{1,0:T(8,128)} %bitcast.86, f32[1024,1024]{1,0:T(8,128)} %collective-permute-done.other_ref, ...), custom_call_target="tpu_custom_call" | custom-call | flops 6442450944 | bytes 20971520 | tf_op jit(solution)/shard_map/pallas_call | solution.py:176
  557.3 10.7 %shard_map.55 = f32[1536,256]{1,0:T(8,128)} custom-call(s32[24]{0:T(128)} %max.46.slot_ref, s32[24]{0:T(128)} %reshape.469.valid_ref, s32[2,8]{1,0:T(2,128)} %pad_add_fusion.1.place_ref, f32[1536,3072]{1,0:T(8,128)} %root_ref.5, f32[16,2,2,128,128]{4,3,2,1,0:T(8,128)} %all-to-all-done.rest_0_.rest_2_.rest_3_.rest_6_.rest_9_, ...), custom_call_target="tpu_custom_call" | custom-call | bytes 11534336 | tf_op jit(solution)/shard_map/pallas_call | solution.py:232
  568.0 2.8 fusion.41
  571.1 2.4 collective-permute-start.10
  573.5 2.4 collective-permute-start.11
  576.0 2.4 collective-permute-start.12
  578.4 54.0 %all-to-all-done.2.rest_2_.rest_5_.rest_8_.rest_11_ = f32[16,2,2,128,128]{4,3,2,1,0:T(8,128)} async-done(((f32[16,2,2,128,128]{4,3,2,1,0:T(8,128)}), f32[16,2,2,128,128]{4,3,2,1,0:T(8,128)}, u32[]{:S(2)}, u32[]{:S(2)}) %all-to-all-start.2) | async-done | bytes 4194336 | tf_op jit(solution)/shard_map/all_to_all | solution.py:586
  632.4 4.6 all-to-all-start.3
  637.0 2.8 add_add_fusion.rest_12_
  639.8 5.7 collective-permute-start.13
  645.5 2.5 collective-permute-start.14
  647.9 2.4 collective-permute-start.15
  650.4 71.1 %collective-permute-done.13 = f32[1536,256]{1,0:T(8,128)S(1)} collective-permute-done((f32[1536,256]{1,0:T(8,128)S(1)}, f32[1536,256]{1,0:T(8,128)S(1)}, u32[]{:S(2)}, u32[]{:S(2)}) %collective-permute-start.13) | collective-permute-done | bytes 1572896 | tf_op jit(solution)/shard_map/ppermute | solution.py:605
  721.5 16.9 %collective-permute-done.14 = f32[1536,256]{1,0:T(8,128)} collective-permute-done((f32[1536,256]{1,0:T(8,128)S(1)}, f32[1536,256]{1,0:T(8,128)}, u32[]{:S(2)}, u32[]{:S(2)}) %collective-permute-start.14) | collective-permute-done | bytes 1572896 | tf_op jit(solution)/shard_map/ppermute | solution.py:605
  738.3 16.9 %collective-permute-done.15 = f32[1536,256]{1,0:T(8,128)} collective-permute-done((f32[1536,256]{1,0:T(8,128)S(1)}, f32[1536,256]{1,0:T(8,128)}, u32[]{:S(2)}, u32[]{:S(2)}) %collective-permute-start.15) | collective-permute-done | bytes 1572896 | tf_op jit(solution)/shard_map/ppermute | solution.py:605
  755.6 1.7 collective-permute-start.16
  757.3 0.7 reshape.444.place_ref
  758.0 0.7 add_convert_fusion.flag_ref
  758.7 0.7 pad_add_fusion.2.place_ref
  759.3 25.3 %collective-permute-done.16 = f32[1536,256]{1,0:T(8,128)} collective-permute-done((f32[1536,256]{1,0:T(8,128)S(1)}, f32[1536,256]{1,0:T(8,128)}, u32[]{:S(2)}, u32[]{:S(2)}) %collective-permute-start.16) | collective-permute-done | bytes 1572896 | tf_op jit(solution)/shard_map/ppermute | solution.py:612
  784.6 1.6 broadcast_select_fusion.1
  786.2 1.9 pad_maximum_fusion.rest_13_
  788.1 24.0 %shard_map.56.root_ref = f32[1536,3072]{1,0:T(8,128)} custom-call(s32[24]{0:T(128)} %max.46.slot_ref, s32[24]{0:T(128)} %reshape.469.valid_ref, s32[2,12]{1,0:T(2,128)} %pad_add_fusion.2.place_ref, s32[2]{0:T(128)} %add_convert_fusion.flag_ref, f32[1536,3072]{1,0:T(8,128)} %root_ref.5, ...), custom_call_target="tpu_custom_call" | custom-call | flops 7247757312 | bytes 50331648 | tf_op jit(solution)/shard_map/pallas_call | solution.py:343
  812.2 18.7 %shard_map.57 = f32[1536,3072]{1,0:T(8,128)} custom-call(s32[24]{0:T(128)} %max.46.slot_ref, s32[24]{0:T(128)} %reshape.469.valid_ref, s32[2,4]{1,0:T(2,128)} %reshape.444.place_ref, f32[1536,3072]{1,0:T(8,128)} %shard_map.56.root_ref, f32[16,2,2,128,128]{4,3,2,1,0:T(8,128)} %all-to-all-done.3.a0_ref.a1_ref, f32[16,2,2,128,128]{4,3,2,1,0:T(8,128)} %all-to-all-done.3.a0_ref.a1_ref), custom_call_target="tpu_custom_call" | custom-call | bytes 41943040 | tf_op jit(solution)/shard_map/pallas_call | solution.py:399
  (137 shorter events, 17.1 us)
Async XLA Ops:
  6.5 138.5 %all-gather.3.cloned.1.call-start = ((), (), s32[]{:S(2)}) async-start(), calls=%async_computation.4 | async-start | bytes 9437184 | tf_op jit(solution)/shard_map/all_gather | solution.py:522
  6.5 7.6 collective-permute-start
  14.1 3.4 copy-start.4
  17.3 499.1 %all-gather.5.cloned.1.call-start = ((), (), s32[]{:S(2)}) async-start(), calls=%async_computation.5 | async-start | bytes 9437184 | tf_op jit(solution)/shard_map/all_gather | solution.py:522
  27.3 17.4 %collective-permute-start.2 = (f32[4,1024,128]{2,1,0:T(8,128)}, f32[4,1024,128]{2,1,0:T(8,128)S(1)}, u32[]{:S(2)}, u32[]{:S(2)}) collective-permute-start(f32[4,1024,128]{2,1,0:T(8,128)} %get-tuple-element.45), channel_id=1, source_target_pairs={{0,16},{2,18},{4,20},{6,22},{8,24},{10,26},{12,28},{14,30},{1,17},... | collective-permute-start | bytes 6291464 | tf_op jit(solution)/shard_map/ppermute | solution.py:535
  27.7 49.0 %collective-permute-start.1 = (f32[4,1024,128]{2,1,0:T(8,128)}, f32[4,1024,128]{2,1,0:T(8,128)}, u32[]{:S(2)}, u32[]{:S(2)}) collective-permute-start(f32[4,1024,128]{2,1,0:T(8,128)} %get-tuple-element.40), channel_id=1, source_target_pairs={{0,1},{2,3},{4,5},{6,7},{8,9},{10,11},{12,13},{14,15},{1,16},{3,18... | collective-permute-start | bytes 6291464 | tf_op jit(solution)/shard_map/ppermute | solution.py:535
  30.4 91.4 %collective-permute-start.3 = (f32[4,1024,128]{2,1,0:T(8,128)}, f32[4,1024,128]{2,1,0:T(8,128)}, u32[]{:S(2)}, u32[]{:S(2)}) collective-permute-start(f32[4,1024,128]{2,1,0:T(8,128)} %get-tuple-element.47), channel_id=1, source_target_pairs={{0,17},{2,19},{4,21},{6,23},{8,25},{10,27},{12,29},{14,31},{1,0},{... | collective-permute-start | bytes 6291464 | tf_op jit(solution)/shard_map/ppermute | solution.py:535
  44.8 100.3 %copy-start.1 = (f32[4,1024,128]{2,1,0:T(8,128)}, f32[4,1024,128]{2,1,0:T(8,128)S(1)}, u32[]{:S(2)}) copy-start(f32[4,1024,128]{2,1,0:T(8,128)S(1)} %collective-permute-done.2.rest_2_) | copy-start | bytes 6291460
  161.7 254.4 %all-to-all-start = ((f32[16,2,2,128,128]{4,3,2,1,0:T(8,128)}), f32[16,2,2,128,128]{4,3,2,1,0:T(8,128)}, u32[]{:S(2)}, u32[]{:S(2)}) async-start(f32[16,2,2,128,128]{4,3,2,1,0:T(8,128)} %shard_map.50.rest_0_), calls=%async_computation | async-start | bytes 8388608 | tf_op jit(solution)/shard_map/all_to_all | solution.py:586
  189.7 18.8 %collective-permute-start.4 = (f32[256,256]{0,1:T(8,128)S(1)}, f32[256,256]{0,1:T(8,128)S(1)}, u32[]{:S(2)}, u32[]{:S(2)}) collective-permute-start(f32[256,256]{0,1:T(8,128)S(1)} %copy.26), channel_id=1, source_target_pairs={{0,2},{2,0},{4,6},{6,4},{8,10},{10,8},{12,14},{14,12},{1,3},{3,1},... | collective-permute-start | bytes 786440 | tf_op jit(solution)/shard_map/ppermute | solution.py:577
  208.5 74.3 %collective-permute-start.5 = (f32[256,256]{0,1:T(8,128)S(1)}, f32[256,256]{0,1:T(8,128)S(1)}, u32[]{:S(2)}, u32[]{:S(2)}) collective-permute-start(f32[256,256]{0,1:T(8,128)S(1)} %add.312), channel_id=1, source_target_pairs={{0,4},{2,6},{4,0},{6,2},{8,12},{10,14},{12,8},{14,10},{1,5},{3,7},... | collective-permute-start | bytes 786440 | tf_op jit(solution)/shard_map/ppermute | solution.py:577
  282.8 71.7 %collective-permute-start.6 = (f32[256,256]{0,1:T(8,128)S(1)}, f32[256,256]{0,1:T(8,128)S(1)}, u32[]{:S(2)}, u32[]{:S(2)}) collective-permute-start(f32[256,256]{0,1:T(8,128)S(1)} %add.313), channel_id=1, source_target_pairs={{0,8},{2,10},{4,12},{6,14},{8,0},{10,2},{12,4},{14,6},{1,9},{3,11}... | collective-permute-start | bytes 786440 | tf_op jit(solution)/shard_map/ppermute | solution.py:577
  416.1 116.8 %all-to-all-start.1 = ((f32[16,2,2,128,128]{4,3,2,1,0:T(8,128)}), f32[16,2,2,128,128]{4,3,2,1,0:T(8,128)}, u32[]{:S(2)}, u32[]{:S(2)}) async-start(f32[16,2,2,128,128]{4,3,2,1,0:T(8,128)} %shard_map.51.rest_1_), calls=%async_computation.1 | async-start | bytes 8388608 | tf_op jit(solution)/shard_map/all_to_all | solution.py:586
  423.3 48.0 %collective-permute-start.7 = (f32[4,1024,128]{2,1,0:T(8,128)}, f32[4,1024,128]{2,1,0:T(8,128)S(1)}, u32[]{:S(2)}, u32[]{:S(2)}) collective-permute-start(f32[4,1024,128]{2,1,0:T(8,128)} %get-tuple-element.53), channel_id=1, source_target_pairs={{0,1},{2,3},{4,5},{6,7},{8,9},{10,11},{12,13},{14,15},{1,16},{3,18... | collective-permute-start | bytes 6291464 | tf_op jit(solution)/shard_map/ppermute | solution.py:535
  424.8 46.5 %collective-permute-start.8 = (f32[4,1024,128]{2,1,0:T(8,128)}, f32[4,1024,128]{2,1,0:T(8,128)}, u32[]{:S(2)}, u32[]{:S(2)}) collective-permute-start(f32[4,1024,128]{2,1,0:T(8,128)} %get-tuple-element.54), channel_id=1, source_target_pairs={{0,16},{2,18},{4,20},{6,22},{8,24},{10,26},{12,28},{14,30},{1,17},... | collective-permute-start | bytes 6291464 | tf_op jit(solution)/shard_map/ppermute | solution.py:535
  424.8 91.7 %collective-permute-start.9 = (f32[4,1024,128]{2,1,0:T(8,128)}, f32[4,1024,128]{2,1,0:T(8,128)}, u32[]{:S(2)}, u32[]{:S(2)}) collective-permute-start(f32[4,1024,128]{2,1,0:T(8,128)} %get-tuple-element.55), channel_id=1, source_target_pairs={{0,17},{2,19},{4,21},{6,23},{8,25},{10,27},{12,29},{14,31},{1,0},{... | collective-permute-start | bytes 6291464 | tf_op jit(solution)/shard_map/ppermute | solution.py:535
  471.3 45.2 %copy-start.2 = (f32[4,1024,128]{2,1,0:T(8,128)}, f32[4,1024,128]{2,1,0:T(8,128)S(1)}, u32[]{:S(2)}) copy-start(f32[4,1024,128]{2,1,0:T(8,128)S(1)} %collective-permute-done.7.rest_1_) | copy-start | bytes 6291460
  532.8 99.5 %all-to-all-start.2 = ((f32[16,2,2,128,128]{4,3,2,1,0:T(8,128)}), f32[16,2,2,128,128]{4,3,2,1,0:T(8,128)}, u32[]{:S(2)}, u32[]{:S(2)}) async-start(f32[16,2,2,128,128]{4,3,2,1,0:T(8,128)} %shard_map.53), calls=%async_computation.2 | async-start | bytes 8388608 | tf_op jit(solution)/shard_map/all_to_all | solution.py:586
  571.1 65.8 %collective-permute-start.10 = (f32[1536,256]{1,0:T(8,128)S(1)}, f32[1536,256]{1,0:T(8,128)}, u32[]{:S(2)}, u32[]{:S(2)}) collective-permute-start(f32[1536,256]{1,0:T(8,128)S(1)} %pad_maximum_fusion.1), channel_id=1, source_target_pairs={{0,1},{2,3},{4,5},{6,7},{8,9},{10,11},{12,13},{14,15}} | collective-permute-start | bytes 4718600 | tf_op jit(solution)/shard_map/ppermute | solution.py:595
  573.5 63.4 %collective-permute-start.11 = (f32[1536,256]{1,0:T(8,128)S(1)}, f32[1536,256]{1,0:T(8,128)}, u32[]{:S(2)}, u32[]{:S(2)}) collective-permute-start(f32[1536,256]{1,0:T(8,128)S(1)} %pad_maximum_fusion.1), channel_id=1, source_target_pairs={{0,16},{2,18},{4,20},{6,22},{8,24},{10,26},{12,28},{14,30}} | collective-permute-start | bytes 4718600 | tf_op jit(solution)/shard_map/ppermute | solution.py:595
  576.0 61.0 %collective-permute-start.12 = (f32[1536,256]{1,0:T(8,128)S(1)}, f32[1536,256]{1,0:T(8,128)}, u32[]{:S(2)}, u32[]{:S(2)}) collective-permute-start(f32[1536,256]{1,0:T(8,128)S(1)} %pad_maximum_fusion.1), channel_id=1, source_target_pairs={{0,17},{2,19},{4,21},{6,23},{8,25},{10,27},{12,29},{14,31}} | collective-permute-start | bytes 4718600 | tf_op jit(solution)/shard_map/ppermute | solution.py:595
  632.4 179.8 %all-to-all-start.3 = ((f32[16,2,2,128,128]{4,3,2,1,0:T(8,128)}), f32[16,2,2,128,128]{4,3,2,1,0:T(8,128)}, u32[]{:S(2)}, u32[]{:S(2)}) async-start(f32[16,2,2,128,128]{4,3,2,1,0:T(8,128)} %shard_map.54), calls=%async_computation.3 | async-start | bytes 8388608 | tf_op jit(solution)/shard_map/all_to_all | solution.py:586
  639.7 115.8 %copy-start = (f32[1536,256]{1,0:T(8,128)}, f32[1536,256]{1,0:T(8,128)S(1)}, u32[]{:S(2)}) copy-start(f32[1536,256]{1,0:T(8,128)S(1)} %add_add_fusion.rest_12_) | copy-start | bytes 4718596
  639.8 81.7 %collective-permute-start.13 = (f32[1536,256]{1,0:T(8,128)S(1)}, f32[1536,256]{1,0:T(8,128)S(1)}, u32[]{:S(2)}, u32[]{:S(2)}) collective-permute-start(f32[1536,256]{1,0:T(8,128)S(1)} %add_add_fusion.rest_12_), channel_id=1, source_target_pairs={{0,12},{2,14},{5,1},{7,3},{24,20},{26,22},{29,25},{31,27}} | collective-permute-start | bytes 4718600 | tf_op jit(solution)/shard_map/ppermute | solution.py:605
  645.5 92.8 %collective-permute-start.14 = (f32[1536,256]{1,0:T(8,128)S(1)}, f32[1536,256]{1,0:T(8,128)}, u32[]{:S(2)}, u32[]{:S(2)}) collective-permute-start(f32[1536,256]{1,0:T(8,128)S(1)} %add_add_fusion.rest_12_), channel_id=1, source_target_pairs={{0,8},{2,10},{5,13},{7,15},{24,16},{26,18},{29,21},{31,23}} | collective-permute-start | bytes 4718600 | tf_op jit(solution)/shard_map/ppermute | solution.py:605
  647.9 107.2 %collective-permute-start.15 = (f32[1536,256]{1,0:T(8,128)S(1)}, f32[1536,256]{1,0:T(8,128)}, u32[]{:S(2)}, u32[]{:S(2)}) collective-permute-start(f32[1536,256]{1,0:T(8,128)S(1)} %add_add_fusion.rest_12_), channel_id=1, source_target_pairs={{0,4},{2,6},{5,9},{7,11},{24,28},{26,30},{29,17},{31,19}} | collective-permute-start | bytes 4718600 | tf_op jit(solution)/shard_map/ppermute | solution.py:605
  721.5 16.9 %copy-start.3 = (f32[1536,256]{1,0:T(8,128)}, f32[1536,256]{1,0:T(8,128)S(1)}, u32[]{:S(2)}) copy-start(f32[1536,256]{1,0:T(8,128)S(1)} %collective-permute-done.13) | copy-start | bytes 4718596
  755.6 29.0 %collective-permute-start.16 = (f32[1536,256]{1,0:T(8,128)S(1)}, f32[1536,256]{1,0:T(8,128)}, u32[]{:S(2)}, u32[]{:S(2)}) collective-permute-start(f32[1536,256]{1,0:T(8,128)S(1)} %select_select_fusion), channel_id=1, source_target_pairs={{0,2},{2,0},{4,6},{6,4},{8,10},{10,8},{12,14},{14,12},{1,3},{3,1},... | collective-permute-start | bytes 4718600 | tf_op jit(solution)/shard_map/ppermute | solution.py:612
Sparse Core Ops, SparseCore 0:
  17.5 127.5 all-gather.2
  147.2 214.0 all-gather.4

commit v6 on v5

--- a/solution.py
+++ b/solution.py
@@ -545,7 +545,9 @@
     for h, first in spans:
         at = slice(h * half_col + first, h * half_col + first + width)
         col_places.append(col_local[:, :, at].reshape(2, -1))
-        if outgoing:
+        if len(outgoing) == 1:
+            origins, outgoing[0], arrived = lax.optimization_barrier((origins, outgoing[0], arrived))
+        elif outgoing:
             origins, outgoing[-1] = lax.optimization_barrier((origins, outgoing[-1]))
         outgoing.append(
             schur_rows(
@@ -576,12 +578,13 @@
                 pairs = [(r, r ^ step) for r in range(row_count)]
                 pivot = pivot + lax.ppermute(pivot, "prow", pairs)
                 step *= 2
-            factor = jnp.linalg.cholesky(pivot)
-            inverse = lax.linalg.triangular_solve(
-                factor, jnp.eye(RP, dtype=F32), left_side=True, lower=True
-            )
-            origins, inverse = lax.optimization_barrier((origins, inverse))
-    row_slot, outgoing[-1] = lax.optimization_barrier((row_slot, outgoing[-1]))
+            origins, pivot = lax.optimization_barrier((origins, pivot))
+        elif len(outgoing) == early + 1:
+            pivot, outgoing[-1] = lax.optimization_barrier((pivot, outgoing[-1]))
+    factor = jnp.linalg.cholesky(pivot)
+    inverse = lax.linalg.triangular_solve(
+        factor, jnp.eye(RP, dtype=F32), left_side=True, lower=True
+    )
     for value in outgoing:
         parts.append(lax.all_to_all(value, "prow", split_axis=0, concat_axis=0, tiled=True))
 

time: 849 us -> 786 us (0.926)
  waiting for transfers between devices: 536 us -> 469 us
    ppermute x6, waiting for transfers between devices: 168 us -> 125 us  [shards(): got.append(lax.ppermute(packed[h][d], everyone, pairs))]
    ppermute x3, waiting for transfers between devices: 158 us -> 119 us  [shards(): pivot = pivot + lax.ppermute(pivot, 'prow', pairs)]
    all_to_all x4, waiting for transfers between devices: 54 us -> 76.2 us  [shards(): lax.all_to_all(value, 'prow', split_axis=0, concat_axis=0, tiled=True)]
    ppermute x3, waiting for transfers between devices: 105 us -> 92.6 us  [shards(): got = lax.ppermute(own_rows, everyone, pairs)]
    another operation x4 -> x3, other arithmetic: 19.7 us -> 19.9 us  [shards(): lax.linalg.triangular_solve(factor, jnp.eye(RP, dtype=F32), left_side=Tru...]
  transfers between devices with their start and end apart: 23 -> 23, of which waited for: 14 -> 15; matrix products, arithmetic and copies ran while one was open for 11% -> 11% of each run, Pallas kernels for 15% -> 16%
where the time goes in v6:
time: 786 us; the launch traced here: 775 us
  waiting for transfers between devices  469 us (60%)
  Pallas kernels  145 us (18%)
  other arithmetic  69.6 us (9%)
  starting transfers between devices  57.2 us (7%)
  local copies, waits for them, and re-layouts  15.3 us (2%)
  between operations  15 us (2%)
    ppermute x6, waiting for transfers between devices, shards(): got.append(lax.ppermute(packed[h][d], everyone, pairs))  125 us
    ppermute x3, waiting for transfers between devices, shards(): pivot = pivot + lax.ppermute(pivot, 'prow', pairs)  119 us
    ppermute x3, waiting for transfers between devices, shards(): got = lax.ppermute(own_rows, everyone, pairs)  92.6 us
    all_to_all x4, waiting for transfers between devices, shards(): lax.all_to_all(value, 'prow', split_axis=0, concat_axis=0, tiled=True)  76.2 us
    pallas_call x4, Pallas kernels, schur_rows(): pl.pallas_call(body, grid_spec=pltpu.PrefetchScalarGridSpec(num_scalar_pr...  65.9 us
    another operation x7, other arithmetic, shards(): factor = jnp.linalg.cholesky(pivot)  34.6 us
    ppermute x1, waiting for transfers between devices, shards(): tiles.append(lax.ppermute(tile, 'prow', pairs))  25.3 us
    pallas_call x1, Pallas kernels, advance(): pl.pallas_call(body, grid_spec=pltpu.PrefetchScalarGridSpec(num_scalar_pr...  24.7 us
  transfers between devices with their start and end apart: 23, of which 15 were waited for; matrix products, arithmetic and copies ran while one was open for 11% of the time, Pallas kernels for 16%

profile of v6, /device:TPU:0, one launch (start us, length us, event | category | flops | bytes accessed | tf_op | source)
XLA Modules:
  0.0 775.3 jit_solution(352735910295841392)
XLA Ops:
  7.0 0.8 eq.188
  8.6 0.7 reduce_window_sum.13
  11.4 0.7 fusion.45
  12.1 2.0 collective-permute-done.other_ref
  14.1 3.2 shard_map.49
  19.6 7.7 shard_map.48
  27.7 2.7 collective-permute-start.1
  30.9 0.7 reshape.440.chosen_ref
  31.6 7.7 shard_map.47
  39.8 3.1 shard_map.46
  42.9 2.0 collective-permute-start.4
  47.0 29.6 %collective-permute-done.1.rest_1_ = f32[4,1024,128]{2,1,0:T(8,128)} collective-permute-done((f32[4,1024,128]{2,1,0:T(8,128)}, f32[4,1024,128]{2,1,0:T(8,128)}, u32[]{:S(2)}, u32[]{:S(2)}) %collective-permute-start.1) | collective-permute-done | bytes 2097184 | tf_op jit(solution)/shard_map/ppermute | solution.py:535
  76.6 45.4 %collective-permute-done.3.rest_3_ = f32[4,1024,128]{2,1,0:T(8,128)} collective-permute-done((f32[4,1024,128]{2,1,0:T(8,128)}, f32[4,1024,128]{2,1,0:T(8,128)}, u32[]{:S(2)}, u32[]{:S(2)}) %collective-permute-start.3) | collective-permute-done | bytes 2097184 | tf_op jit(solution)/shard_map/ppermute | solution.py:535
  122.1 23.0 %all-gather.3.cloned.1.call-done.rest_4_ = f32[16,128,1024]{2,1,0:T(8,128)} async-done(((f32[2,128,1024]{2,1,0:T(8,128)}), f32[16,128,1024]{2,1,0:T(8,128)}) %all-gather.3.cloned.1.call-update) | async-done | bytes 8388624 | tf_op jit(solution)/shard_map/all_gather | solution.py:522
  145.0 16.6 %shard_map.50.rest_0_ = f32[16,2,2,128,128]{4,3,2,1,0:T(8,128)} custom-call(s32[1]{0:T(128)} %bitcast.11.half_ref, s32[16]{0:T(128)} %get-tuple-element.103.slot_ref, s32[8]{0:T(128)} %reshape.442.place_ref, s32[4]{0:T(128)} %and_select_fusion.5.origin_ref, f32[1024,1024]{1,0:T(8,128)} %bitcast.82, f32[1024,1024]{1,0:T(8,128)} %collective-permute-done.other_ref, ...), custom_call_target="tpu_custom_call" | custom-call | flops 6442450944 | bytes 20971520 | tf_op jit(solution)/shard_map/pallas_call | solution.py:176
  161.7 4.8 collective-permute-done.4.rest_1_
  166.5 45.1 %collective-permute-done.6.rest_3_ = f32[4,1024,128]{2,1,0:T(8,128)} collective-permute-done((f32[4,1024,128]{2,1,0:T(8,128)}, f32[4,1024,128]{2,1,0:T(8,128)}, u32[]{:S(2)}, u32[]{:S(2)}) %collective-permute-start.6) | collective-permute-done | bytes 2097184 | tf_op jit(solution)/shard_map/ppermute | solution.py:535
  211.6 6.1 all-to-all-start
  217.7 0.7 reshape.446.place_ref
  218.6 0.7 pad_add_fusion.2.place_ref
  220.5 16.5 %shard_map.51.rest_1_ = f32[16,2,2,128,128]{4,3,2,1,0:T(8,128)} custom-call(s32[1]{0:T(128)} %bitcast.11.half_ref, s32[16]{0:T(128)} %get-tuple-element.103.slot_ref, s32[8]{0:T(128)} %reshape.446.place_ref, s32[4]{0:T(128)} %and_select_fusion.5.origin_ref, f32[1024,1024]{1,0:T(8,128)} %bitcast.83, f32[1024,1024]{1,0:T(8,128)} %collective-permute-done.other_ref, ...), custom_call_target="tpu_custom_call" | custom-call | flops 6442450944 | bytes 20971520 | tf_op jit(solution)/shard_map/pallas_call | solution.py:176
  237.0 3.0 shard_map.52
  239.9 1.1 copy.26
  241.0 2.1 collective-permute-start.7
  243.1 31.6 %collective-permute-done.7 = f32[256,256]{0,1:T(8,128)S(1)} collective-permute-done((f32[256,256]{0,1:T(8,128)S(1)}, f32[256,256]{0,1:T(8,128)S(1)}, u32[]{:S(2)}, u32[]{:S(2)}) %collective-permute-start.7) | collective-permute-done | bytes 262176 | tf_op jit(solution)/shard_map/ppermute | solution.py:579
  274.7 1.9 collective-permute-start.8
  276.6 60.5 %collective-permute-done.8 = f32[256,256]{0,1:T(8,128)S(1)} collective-permute-done((f32[256,256]{0,1:T(8,128)S(1)}, f32[256,256]{0,1:T(8,128)S(1)}, u32[]{:S(2)}, u32[]{:S(2)}) %collective-permute-start.8) | collective-permute-done | bytes 262176 | tf_op jit(solution)/shard_map/ppermute | solution.py:579
  337.1 4.7 collective-permute-start.9
  341.8 26.5 %collective-permute-done.9 = f32[256,256]{0,1:T(8,128)S(1)} collective-permute-done((f32[256,256]{0,1:T(8,128)S(1)}, f32[256,256]{0,1:T(8,128)S(1)}, u32[]{:S(2)}, u32[]{:S(2)}) %collective-permute-start.9) | collective-permute-done | bytes 262176 | tf_op jit(solution)/shard_map/ppermute | solution.py:579
  368.3 4.6 all-to-all-start.1
  373.5 16.4 %shard_map.53 = f32[16,2,2,128,128]{4,3,2,1,0:T(8,128)} custom-call(s32[1]{0:T(128)} %bitcast.11.half_ref, s32[16]{0:T(128)} %get-tuple-element.103.slot_ref, s32[8]{0:T(128)} %reshape.447.place_ref, s32[4]{0:T(128)} %and_select_fusion.5.origin_ref, f32[1024,1024]{1,0:T(8,128)} %bitcast.84, f32[1024,1024]{1,0:T(8,128)} %collective-permute-done.other_ref, ...), custom_call_target="tpu_custom_call" | custom-call | flops 6442450944 | bytes 20971520 | tf_op jit(solution)/shard_map/pallas_call | solution.py:176
  389.9 76.2 %all-to-all-done.1.rest_1_.rest_3_.rest_4_.rest_7_.rest_10_ = f32[16,2,2,128,128]{4,3,2,1,0:T(8,128)} async-done(((f32[16,2,2,128,128]{4,3,2,1,0:T(8,128)}), f32[16,2,2,128,128]{4,3,2,1,0:T(8,128)}, u32[]{:S(2)}, u32[]{:S(2)}) %all-to-all-start.1) | async-done | bytes 4194336 | tf_op jit(solution)/shard_map/all_to_all | solution.py:589
  466.1 4.8 all-to-all-start.2
  470.9 0.7 reshape.448.place_ref
  473.1 11.7 %cholesky.50 = f32[128,128]{1,0:T(8,128)S(1)} custom-call(f32[128,128]{1,0:T(8,128)S(1)} %cholesky.118), custom_call_target="Cholesky" | custom-call | tf_op jit(solution)/shard_map/jit(cholesky)/cholesky | solution.py:584
  484.9 9.8 %custom-call.14 = f32[1,128,128]{1,2,0:T(8,128)S(1)} custom-call(f32[1,128,128]{2,1,0:T(8,128)S(1)} %get-tuple-element.116), custom_call_target="InvertDiagBlocksLowerTriangular" | custom-call | tf_op jit(solution)/shard_map/jit(cholesky)/cholesky | solution.py:584
  495.2 11.7 %cholesky.105 = f32[128,128]{1,0:T(8,128)S(1)} custom-call(f32[128,128]{1,0:T(8,128)S(1)} %convolution_subtract_fusion.1), custom_call_target="Cholesky" | custom-call | tf_op jit(solution)/shard_map/jit(cholesky)/cholesky | solution.py:584
  509.5 3.8 while.1
  510.1 1.3 bitcast_dynamic-update-slice_fusion.2
  512.0 1.3 bitcast_dynamic-update-slice_fusion.2
  513.2 19.9 %custom-call.15 = f32[2,128,128]{1,2,0:T(8,128)S(1)} custom-call(f32[2,128,128]{2,1,0:T(8,128)S(1)} %get-tuple-element.86), custom_call_target="InvertDiagBlocksLowerTriangular" | custom-call | tf_op jit(solution)/shard_map/triangular_solve | solution.py:585
  534.0 10.8 %shard_map.54 = f32[1536,256]{1,0:T(8,128)} custom-call(s32[24]{0:T(128)} %max.46.slot_ref, s32[24]{0:T(128)} %reshape.468.valid_ref, s32[2,8]{1,0:T(2,128)} %pad_add_fusion.2.place_ref, f32[1536,3072]{1,0:T(8,128)} %root_ref.5, f32[16,2,2,128,128]{4,3,2,1,0:T(8,128)} %all-to-all-done.rest_0_.rest_2_.rest_3_.rest_6_.rest_9_, ...), custom_call_target="tpu_custom_call" | custom-call | bytes 11534336 | tf_op jit(solution)/shard_map/pallas_call | solution.py:232
  544.8 2.8 fusion
  547.9 5.0 collective-permute-start.10
  552.9 2.5 collective-permute-start.11
  555.3 2.5 collective-permute-start.12
  557.9 16.4 %shard_map.56 = f32[16,2,2,128,128]{4,3,2,1,0:T(8,128)} custom-call(s32[1]{0:T(128)} %bitcast.11.half_ref, s32[16]{0:T(128)} %get-tuple-element.103.slot_ref, s32[8]{0:T(128)} %reshape.448.place_ref, s32[4]{0:T(128)} %and_select_fusion.5.origin_ref, f32[1024,1024]{1,0:T(8,128)} %bitcast.85, f32[1024,1024]{1,0:T(8,128)} %collective-permute-done.other_ref, ...), custom_call_target="tpu_custom_call" | custom-call | flops 6442450944 | bytes 20971520 | tf_op jit(solution)/shard_map/pallas_call | solution.py:176
  574.3 5.7 all-to-all-start.3
  579.9 6.5 collective-permute-done.12
  586.5 2.8 add_add_fusion.rest_12_
  589.2 5.5 collective-permute-start.13
  594.8 2.5 collective-permute-start.14
  597.2 2.4 collective-permute-start.15
  599.7 58.9 %collective-permute-done.13 = f32[1536,256]{1,0:T(8,128)S(1)} collective-permute-done((f32[1536,256]{1,0:T(8,128)S(1)}, f32[1536,256]{1,0:T(8,128)S(1)}, u32[]{:S(2)}, u32[]{:S(2)}) %collective-permute-start.13) | collective-permute-done | bytes 1572896 | tf_op jit(solution)/shard_map/ppermute | solution.py:608
  658.6 16.9 %collective-permute-done.14 = f32[1536,256]{1,0:T(8,128)} collective-permute-done((f32[1536,256]{1,0:T(8,128)S(1)}, f32[1536,256]{1,0:T(8,128)}, u32[]{:S(2)}, u32[]{:S(2)}) %collective-permute-start.14) | collective-permute-done | bytes 1572896 | tf_op jit(solution)/shard_map/ppermute | solution.py:608
  675.5 16.9 %collective-permute-done.15 = f32[1536,256]{1,0:T(8,128)} collective-permute-done((f32[1536,256]{1,0:T(8,128)S(1)}, f32[1536,256]{1,0:T(8,128)}, u32[]{:S(2)}, u32[]{:S(2)}) %collective-permute-start.15) | collective-permute-done | bytes 1572896 | tf_op jit(solution)/shard_map/ppermute | solution.py:608
  692.7 1.4 collective-permute-start.16
  694.2 0.7 reshape.434.place_ref
  694.8 0.7 add_convert_fusion.flag_ref
  696.1 25.3 %collective-permute-done.16 = f32[1536,256]{1,0:T(8,128)} collective-permute-done((f32[1536,256]{1,0:T(8,128)S(1)}, f32[1536,256]{1,0:T(8,128)}, u32[]{:S(2)}, u32[]{:S(2)}) %collective-permute-start.16) | collective-permute-done | bytes 1572896 | tf_op jit(solution)/shard_map/ppermute | solution.py:615
  721.4 1.6 broadcast_select_fusion.1
  723.0 1.9 pad_maximum_fusion.rest_13_
  724.9 24.7 %shard_map.55.root_ref = f32[1536,3072]{1,0:T(8,128)} custom-call(s32[24]{0:T(128)} %max.46.slot_ref, s32[24]{0:T(128)} %reshape.468.valid_ref, s32[2,12]{1,0:T(2,128)} %pad_add_fusion.1.place_ref, s32[2]{0:T(128)} %add_convert_fusion.flag_ref, f32[1536,3072]{1,0:T(8,128)} %root_ref.5, ...), custom_call_target="tpu_custom_call" | custom-call | flops 7247757312 | bytes 50331648 | tf_op jit(solution)/shard_map/pallas_call | solution.py:343
  749.6 18.8 %shard_map.57 = f32[1536,3072]{1,0:T(8,128)} custom-call(s32[24]{0:T(128)} %max.46.slot_ref, s32[24]{0:T(128)} %reshape.468.valid_ref, s32[2,4]{1,0:T(2,128)} %reshape.434.place_ref, f32[1536,3072]{1,0:T(8,128)} %shard_map.55.root_ref, f32[16,2,2,128,128]{4,3,2,1,0:T(8,128)} %all-to-all-done.3.a0_ref.a1_ref, f32[16,2,2,128,128]{4,3,2,1,0:T(8,128)} %all-to-all-done.3.a0_ref.a1_ref), custom_call_target="tpu_custom_call" | custom-call | bytes 41943040 | tf_op jit(solution)/shard_map/pallas_call | solution.py:399
  (134 shorter events, 18.2 us)
Async XLA Ops:
  6.5 138.5 %all-gather.3.cloned.1.call-start = ((), (), s32[]{:S(2)}) async-start(), calls=%async_computation.4 | async-start | bytes 9437184 | tf_op jit(solution)/shard_map/all_gather | solution.py:522
  6.5 7.6 collective-permute-start
  14.1 3.4 copy-start.3
  17.3 356.2 %all-gather.5.cloned.1.call-start = ((), (), s32[]{:S(2)}) async-start(), calls=%async_computation.5 | async-start | bytes 9437184 | tf_op jit(solution)/shard_map/all_gather | solution.py:522
  27.3 15.6 %collective-permute-start.2 = (f32[4,1024,128]{2,1,0:T(8,128)}, f32[4,1024,128]{2,1,0:T(8,128)}, u32[]{:S(2)}, u32[]{:S(2)}) collective-permute-start(f32[4,1024,128]{2,1,0:T(8,128)} %get-tuple-element.53), channel_id=1, source_target_pairs={{0,16},{2,18},{4,20},{6,22},{8,24},{10,26},{12,28},{14,30},{1,17},... | collective-permute-start | bytes 6291464 | tf_op jit(solution)/shard_map/ppermute | solution.py:535
  27.7 49.0 %collective-permute-start.1 = (f32[4,1024,128]{2,1,0:T(8,128)}, f32[4,1024,128]{2,1,0:T(8,128)}, u32[]{:S(2)}, u32[]{:S(2)}) collective-permute-start(f32[4,1024,128]{2,1,0:T(8,128)} %get-tuple-element.48), channel_id=1, source_target_pairs={{0,1},{2,3},{4,5},{6,7},{8,9},{10,11},{12,13},{14,15},{1,16},{3,18... | collective-permute-start | bytes 6291464 | tf_op jit(solution)/shard_map/ppermute | solution.py:535
  30.4 91.7 %collective-permute-start.3 = (f32[4,1024,128]{2,1,0:T(8,128)}, f32[4,1024,128]{2,1,0:T(8,128)}, u32[]{:S(2)}, u32[]{:S(2)}) collective-permute-start(f32[4,1024,128]{2,1,0:T(8,128)} %get-tuple-element.55), channel_id=1, source_target_pairs={{0,17},{2,19},{4,21},{6,23},{8,25},{10,27},{12,29},{14,31},{1,0},{... | collective-permute-start | bytes 6291464 | tf_op jit(solution)/shard_map/ppermute | solution.py:535
  42.9 123.6 %collective-permute-start.4 = (f32[4,1024,128]{2,1,0:T(8,128)}, f32[4,1024,128]{2,1,0:T(8,128)S(1)}, u32[]{:S(2)}, u32[]{:S(2)}) collective-permute-start(f32[4,1024,128]{2,1,0:T(8,128)} %get-tuple-element.57), channel_id=1, source_target_pairs={{0,1},{2,3},{4,5},{6,7},{8,9},{10,11},{12,13},{14,15},{1,16},{3,18... | collective-permute-start | bytes 6291464 | tf_op jit(solution)/shard_map/ppermute | solution.py:535
  44.9 121.6 %collective-permute-start.5 = (f32[4,1024,128]{2,1,0:T(8,128)}, f32[4,1024,128]{2,1,0:T(8,128)}, u32[]{:S(2)}, u32[]{:S(2)}) collective-permute-start(f32[4,1024,128]{2,1,0:T(8,128)} %get-tuple-element.58), channel_id=1, source_target_pairs={{0,16},{2,18},{4,20},{6,22},{8,24},{10,26},{12,28},{14,30},{1,17},... | collective-permute-start | bytes 6291464 | tf_op jit(solution)/shard_map/ppermute | solution.py:535
  44.9 166.7 %collective-permute-start.6 = (f32[4,1024,128]{2,1,0:T(8,128)}, f32[4,1024,128]{2,1,0:T(8,128)}, u32[]{:S(2)}, u32[]{:S(2)}) collective-permute-start(f32[4,1024,128]{2,1,0:T(8,128)} %get-tuple-element.59), channel_id=1, source_target_pairs={{0,17},{2,19},{4,21},{6,23},{8,25},{10,27},{12,29},{14,31},{1,0},{... | collective-permute-start | bytes 6291464 | tf_op jit(solution)/shard_map/ppermute | solution.py:535
  166.5 45.1 %copy-start.1 = (f32[4,1024,128]{2,1,0:T(8,128)}, f32[4,1024,128]{2,1,0:T(8,128)S(1)}, u32[]{:S(2)}) copy-start(f32[4,1024,128]{2,1,0:T(8,128)S(1)} %collective-permute-done.4.rest_1_) | copy-start | bytes 6291460
  211.6 156.6 %all-to-all-start = ((f32[16,2,2,128,128]{4,3,2,1,0:T(8,128)}), f32[16,2,2,128,128]{4,3,2,1,0:T(8,128)}, u32[]{:S(2)}, u32[]{:S(2)}) async-start(f32[16,2,2,128,128]{4,3,2,1,0:T(8,128)} %shard_map.50.rest_0_), calls=%async_computation | async-start | bytes 8388608 | tf_op jit(solution)/shard_map/all_to_all | solution.py:589
  241.0 33.6 %collective-permute-start.7 = (f32[256,256]{0,1:T(8,128)S(1)}, f32[256,256]{0,1:T(8,128)S(1)}, u32[]{:S(2)}, u32[]{:S(2)}) collective-permute-start(f32[256,256]{0,1:T(8,128)S(1)} %copy.26), channel_id=1, source_target_pairs={{0,2},{2,0},{4,6},{6,4},{8,10},{10,8},{12,14},{14,12},{1,3},{3,1},... | collective-permute-start | bytes 786440 | tf_op jit(solution)/shard_map/ppermute | solution.py:579
  274.7 62.4 %collective-permute-start.8 = (f32[256,256]{0,1:T(8,128)S(1)}, f32[256,256]{0,1:T(8,128)S(1)}, u32[]{:S(2)}, u32[]{:S(2)}) collective-permute-start(f32[256,256]{0,1:T(8,128)S(1)} %add.312), channel_id=1, source_target_pairs={{0,4},{2,6},{4,0},{6,2},{8,12},{10,14},{12,8},{14,10},{1,5},{3,7},... | collective-permute-start | bytes 786440 | tf_op jit(solution)/shard_map/ppermute | solution.py:579
  337.1 31.1 %collective-permute-start.9 = (f32[256,256]{0,1:T(8,128)S(1)}, f32[256,256]{0,1:T(8,128)S(1)}, u32[]{:S(2)}, u32[]{:S(2)}) collective-permute-start(f32[256,256]{0,1:T(8,128)S(1)} %add.313), channel_id=1, source_target_pairs={{0,8},{2,10},{4,12},{6,14},{8,0},{10,2},{12,4},{14,6},{1,9},{3,11}... | collective-permute-start | bytes 786440 | tf_op jit(solution)/shard_map/ppermute | solution.py:579
  368.3 97.8 %all-to-all-start.1 = ((f32[16,2,2,128,128]{4,3,2,1,0:T(8,128)}), f32[16,2,2,128,128]{4,3,2,1,0:T(8,128)}, u32[]{:S(2)}, u32[]{:S(2)}) async-start(f32[16,2,2,128,128]{4,3,2,1,0:T(8,128)} %shard_map.51.rest_1_), calls=%async_computation.1 | async-start | bytes 8388608 | tf_op jit(solution)/shard_map/all_to_all | solution.py:589
  466.1 108.2 %all-to-all-start.2 = ((f32[16,2,2,128,128]{4,3,2,1,0:T(8,128)}), f32[16,2,2,128,128]{4,3,2,1,0:T(8,128)}, u32[]{:S(2)}, u32[]{:S(2)}) async-start(f32[16,2,2,128,128]{4,3,2,1,0:T(8,128)} %shard_map.53), calls=%async_computation.2 | async-start | bytes 8388608 | tf_op jit(solution)/shard_map/all_to_all | solution.py:589
  547.9 32.0 %collective-permute-start.10 = (f32[1536,256]{1,0:T(8,128)S(1)}, f32[1536,256]{1,0:T(8,128)}, u32[]{:S(2)}, u32[]{:S(2)}) collective-permute-start(f32[1536,256]{1,0:T(8,128)S(1)} %pad_maximum_fusion.1), channel_id=1, source_target_pairs={{0,1},{2,3},{4,5},{6,7},{8,9},{10,11},{12,13},{14,15}} | collective-permute-start | bytes 4718600 | tf_op jit(solution)/shard_map/ppermute | solution.py:598
  552.9 27.0 %collective-permute-start.11 = (f32[1536,256]{1,0:T(8,128)S(1)}, f32[1536,256]{1,0:T(8,128)}, u32[]{:S(2)}, u32[]{:S(2)}) collective-permute-start(f32[1536,256]{1,0:T(8,128)S(1)} %pad_maximum_fusion.1), channel_id=1, source_target_pairs={{0,16},{2,18},{4,20},{6,22},{8,24},{10,26},{12,28},{14,30}} | collective-permute-start | bytes 4718600 | tf_op jit(solution)/shard_map/ppermute | solution.py:598
  555.3 31.1 %collective-permute-start.12 = (f32[1536,256]{1,0:T(8,128)S(1)}, f32[1536,256]{1,0:T(8,128)}, u32[]{:S(2)}, u32[]{:S(2)}) collective-permute-start(f32[1536,256]{1,0:T(8,128)S(1)} %pad_maximum_fusion.1), channel_id=1, source_target_pairs={{0,17},{2,19},{4,21},{6,23},{8,25},{10,27},{12,29},{14,31}} | collective-permute-start | bytes 4718600 | tf_op jit(solution)/shard_map/ppermute | solution.py:598
  574.3 175.3 %all-to-all-start.3 = ((f32[16,2,2,128,128]{4,3,2,1,0:T(8,128)}), f32[16,2,2,128,128]{4,3,2,1,0:T(8,128)}, u32[]{:S(2)}, u32[]{:S(2)}) async-start(f32[16,2,2,128,128]{4,3,2,1,0:T(8,128)} %shard_map.56), calls=%async_computation.3 | async-start | bytes 8388608 | tf_op jit(solution)/shard_map/all_to_all | solution.py:589
  589.2 103.5 %copy-start = (f32[1536,256]{1,0:T(8,128)}, f32[1536,256]{1,0:T(8,128)S(1)}, u32[]{:S(2)}) copy-start(f32[1536,256]{1,0:T(8,128)S(1)} %add_add_fusion.rest_12_) | copy-start | bytes 4718596
  589.2 69.4 %collective-permute-start.13 = (f32[1536,256]{1,0:T(8,128)S(1)}, f32[1536,256]{1,0:T(8,128)S(1)}, u32[]{:S(2)}, u32[]{:S(2)}) collective-permute-start(f32[1536,256]{1,0:T(8,128)S(1)} %add_add_fusion.rest_12_), channel_id=1, source_target_pairs={{0,12},{2,14},{5,1},{7,3},{24,20},{26,22},{29,25},{31,27}} | collective-permute-start | bytes 4718600 | tf_op jit(solution)/shard_map/ppermute | solution.py:608
  594.8 80.7 %collective-permute-start.14 = (f32[1536,256]{1,0:T(8,128)S(1)}, f32[1536,256]{1,0:T(8,128)}, u32[]{:S(2)}, u32[]{:S(2)}) collective-permute-start(f32[1536,256]{1,0:T(8,128)S(1)} %add_add_fusion.rest_12_), channel_id=1, source_target_pairs={{0,8},{2,10},{5,13},{7,15},{24,16},{26,18},{29,21},{31,23}} | collective-permute-start | bytes 4718600 | tf_op jit(solution)/shard_map/ppermute | solution.py:608
  597.2 95.1 %collective-permute-start.15 = (f32[1536,256]{1,0:T(8,128)S(1)}, f32[1536,256]{1,0:T(8,128)}, u32[]{:S(2)}, u32[]{:S(2)}) collective-permute-start(f32[1536,256]{1,0:T(8,128)S(1)} %add_add_fusion.rest_12_), channel_id=1, source_target_pairs={{0,4},{2,6},{5,9},{7,11},{24,28},{26,30},{29,17},{31,19}} | collective-permute-start | bytes 4718600 | tf_op jit(solution)/shard_map/ppermute | solution.py:608
  658.6 16.9 %copy-start.2 = (f32[1536,256]{1,0:T(8,128)}, f32[1536,256]{1,0:T(8,128)S(1)}, u32[]{:S(2)}) copy-start(f32[1536,256]{1,0:T(8,128)S(1)} %collective-permute-done.13) | copy-start | bytes 4718596
  692.7 28.7 %collective-permute-start.16 = (f32[1536,256]{1,0:T(8,128)S(1)}, f32[1536,256]{1,0:T(8,128)}, u32[]{:S(2)}, u32[]{:S(2)}) collective-permute-start(f32[1536,256]{1,0:T(8,128)S(1)} %select_select_fusion), channel_id=1, source_target_pairs={{0,2},{2,0},{4,6},{6,4},{8,10},{10,8},{12,14},{14,12},{1,3},{3,1},... | collective-permute-start | bytes 4718600 | tf_op jit(solution)/shard_map/ppermute | solution.py:615
Sparse Core Ops, SparseCore 0:
  17.5 127.5 all-gather.2
  147.2 201.6 all-gather.4

commit v7 on v5

--- a/solution.py
+++ b/solution.py
@@ -535,6 +535,9 @@
             got.append(lax.ppermute(packed[h][d], everyone, pairs))
         arrived.append(got)
 
+    exchange = functools.partial(
+        lax.all_to_all, axis_name="prow", split_axis=0, concat_axis=0, tiled=True
+    )
     spans = [(h, first) for h in range(halves) for first in range(0, half_col, width)]
     early = max(1, len(spans) // halves)
     outgoing, parts, col_places = [], [], []
@@ -545,7 +548,9 @@
     for h, first in spans:
         at = slice(h * half_col + first, h * half_col + first + width)
         col_places.append(col_local[:, :, at].reshape(2, -1))
-        if outgoing:
+        if len(outgoing) == 1:
+            origins, outgoing[0], arrived = lax.optimization_barrier((origins, outgoing[0], arrived))
+        elif outgoing:
             origins, outgoing[-1] = lax.optimization_barrier((origins, outgoing[-1]))
         outgoing.append(
             schur_rows(
@@ -576,14 +581,14 @@
                 pairs = [(r, r ^ step) for r in range(row_count)]
                 pivot = pivot + lax.ppermute(pivot, "prow", pairs)
                 step *= 2
+            parts.append(exchange(outgoing[0]))
+            pivot, parts[0] = lax.optimization_barrier((pivot, parts[0]))
             factor = jnp.linalg.cholesky(pivot)
             inverse = lax.linalg.triangular_solve(
                 factor, jnp.eye(RP, dtype=F32), left_side=True, lower=True
             )
             origins, inverse = lax.optimization_barrier((origins, inverse))
-    row_slot, outgoing[-1] = lax.optimization_barrier((row_slot, outgoing[-1]))
-    for value in outgoing:
-        parts.append(lax.all_to_all(value, "prow", split_axis=0, concat_axis=0, tiled=True))
+    parts += [exchange(value) for value in outgoing[1:]]
 
     raw = first_panel(root_front, parts[:early], row_slot, row_valid, col_places[:early])
     solved = lax.dot_general(raw, inverse, NT, precision=HIGHEST, preferred_element_type=F32)

time: 849 us -> 878 us (1.034)
  waiting for transfers between devices: 536 us -> 564 us
    all_to_all x4, waiting for transfers between devices: 54 us -> 124 us  [the longest x3 124 us: shards(): parts += [exchange(value) for value in outgoing[1:]]]
    ppermute x6, waiting for transfers between devices: 168 us -> 125 us  [shards(): got.append(lax.ppermute(packed[h][d], everyone, pairs))]
  transfers between devices with their start and end apart: 23 -> 23, of which waited for: 14 -> 15; matrix products, arithmetic and copies ran while one was open for 11% -> 10% of each run, Pallas kernels for 15% -> 14%
where the time goes in v7:
time: 878 us; the launch traced here: 868 us
  waiting for transfers between devices  564 us (64%)
  Pallas kernels  145 us (17%)
  other arithmetic  69.4 us (8%)
  starting transfers between devices  55.2 us (6%)
  between operations  15.1 us (2%)
  local copies, waits for them, and re-layouts  14.7 us (2%)
    ppermute x3, waiting for transfers between devices, shards(): pivot = pivot + lax.ppermute(pivot, 'prow', pairs)  159 us
    ppermute x6, waiting for transfers between devices, shards(): got.append(lax.ppermute(packed[h][d], everyone, pairs))  125 us
    all_to_all x3, waiting for transfers between devices, shards(): parts += [exchange(value) for value in outgoing[1:]]  124 us
    ppermute x3, waiting for transfers between devices, shards(): got = lax.ppermute(own_rows, everyone, pairs)  105 us
    pallas_call x4, Pallas kernels, schur_rows(): pl.pallas_call(body, grid_spec=pltpu.PrefetchScalarGridSpec(num_scalar_pr...  65.8 us
    another operation x7, other arithmetic, shards(): factor = jnp.linalg.cholesky(pivot)  34.6 us
    ppermute x1, waiting for transfers between devices, shards(): tiles.append(lax.ppermute(tile, 'prow', pairs))  25.3 us
    pallas_call x1, Pallas kernels, advance(): pl.pallas_call(body, grid_spec=pltpu.PrefetchScalarGridSpec(num_scalar_pr...  25 us
  transfers between devices with their start and end apart: 23, of which 15 were waited for; matrix products, arithmetic and copies ran while one was open for 10% of the time, Pallas kernels for 14%

profile of v7, /device:TPU:0, one launch (start us, length us, event | category | flops | bytes accessed | tf_op | source)
XLA Modules:
  0.0 867.5 jit_solution(13716782485735098003)
XLA Ops:
  7.0 0.8 eq.190
  8.6 0.7 reduce_window_sum.13
  10.8 0.7 and_select_fusion
  11.5 2.6 collective-permute-done.other_ref
  14.1 3.2 shard_map.49
  19.5 7.7 shard_map.48
  27.6 2.7 collective-permute-start.1
  30.9 0.7 reshape.442.chosen_ref
  31.6 7.8 shard_map.47
  39.9 3.1 shard_map.46
  42.9 2.0 collective-permute-start.4
  45.9 0.7 reshape.444.place_ref
  47.1 29.5 %collective-permute-done.1.rest_1_ = f32[4,1024,128]{2,1,0:T(8,128)} collective-permute-done((f32[4,1024,128]{2,1,0:T(8,128)}, f32[4,1024,128]{2,1,0:T(8,128)}, u32[]{:S(2)}, u32[]{:S(2)}) %collective-permute-start.1) | collective-permute-done | bytes 2097184 | tf_op jit(solution)/shard_map/ppermute | solution.py:535
  76.6 45.4 %collective-permute-done.3.rest_3_ = f32[4,1024,128]{2,1,0:T(8,128)} collective-permute-done((f32[4,1024,128]{2,1,0:T(8,128)}, f32[4,1024,128]{2,1,0:T(8,128)}, u32[]{:S(2)}, u32[]{:S(2)}) %collective-permute-start.3) | collective-permute-done | bytes 2097184 | tf_op jit(solution)/shard_map/ppermute | solution.py:535
  122.0 23.0 %all-gather.3.cloned.1.call-done.rest_4_ = f32[16,128,1024]{2,1,0:T(8,128)} async-done(((f32[2,128,1024]{2,1,0:T(8,128)}), f32[16,128,1024]{2,1,0:T(8,128)}) %all-gather.3.cloned.1.call-update) | async-done | bytes 8388624 | tf_op jit(solution)/shard_map/all_gather | solution.py:522
  145.0 16.4 %shard_map.50.rest_0_ = f32[16,2,2,128,128]{4,3,2,1,0:T(8,128)} custom-call(s32[1]{0:T(128)} %bitcast.15.half_ref, s32[16]{0:T(128)} %bitcast_add_fusion.1.slot_ref, s32[8]{0:T(128)} %reshape.444.place_ref, s32[4]{0:T(128)} %and_select_fusion.4.origin_ref, f32[1024,1024]{1,0:T(8,128)} %bitcast.84, f32[1024,1024]{1,0:T(8,128)} %collective-permute-done.other_ref, ...), custom_call_target="tpu_custom_call" | custom-call | flops 6442450944 | bytes 20971520 | tf_op jit(solution)/shard_map/pallas_call | solution.py:176
  161.4 5.1 collective-permute-done.4.rest_1_
  166.5 45.1 %collective-permute-done.6.rest_3_ = f32[4,1024,128]{2,1,0:T(8,128)} collective-permute-done((f32[4,1024,128]{2,1,0:T(8,128)}, f32[4,1024,128]{2,1,0:T(8,128)}, u32[]{:S(2)}, u32[]{:S(2)}) %collective-permute-start.6) | collective-permute-done | bytes 2097184 | tf_op jit(solution)/shard_map/ppermute | solution.py:535
  211.6 6.1 all-to-all-start
  217.7 0.7 all-gather.5.cloned.1.call-update
  220.0 0.7 select_reduce_fusion.6
  221.2 16.7 %shard_map.51.rest_1_ = f32[16,2,2,128,128]{4,3,2,1,0:T(8,128)} custom-call(s32[1]{0:T(128)} %bitcast.15.half_ref, s32[16]{0:T(128)} %bitcast_add_fusion.1.slot_ref, s32[8]{0:T(128)} %reshape.446.place_ref, s32[4]{0:T(128)} %and_select_fusion.4.origin_ref, f32[1024,1024]{1,0:T(8,128)} %bitcast.85, f32[1024,1024]{1,0:T(8,128)} %collective-permute-done.other_ref, ...), custom_call_target="tpu_custom_call" | custom-call | flops 6442450944 | bytes 20971520 | tf_op jit(solution)/shard_map/pallas_call | solution.py:176
  237.8 3.1 shard_map.52
  240.9 1.1 copy.26
  242.0 2.1 collective-permute-start.7
  244.1 24.1 %collective-permute-done.7 = f32[256,256]{0,1:T(8,128)S(1)} collective-permute-done((f32[256,256]{0,1:T(8,128)S(1)}, f32[256,256]{0,1:T(8,128)S(1)}, u32[]{:S(2)}, u32[]{:S(2)}) %collective-permute-start.7) | collective-permute-done | bytes 262176 | tf_op jit(solution)/shard_map/ppermute | solution.py:582
  268.2 1.8 collective-permute-start.8
  270.0 54.5 %collective-permute-done.8 = f32[256,256]{0,1:T(8,128)S(1)} collective-permute-done((f32[256,256]{0,1:T(8,128)S(1)}, f32[256,256]{0,1:T(8,128)S(1)}, u32[]{:S(2)}, u32[]{:S(2)}) %collective-permute-start.8) | collective-permute-done | bytes 262176 | tf_op jit(solution)/shard_map/ppermute | solution.py:582
  324.6 4.6 collective-permute-start.9
  329.2 80.2 %collective-permute-done.9 = f32[256,256]{0,1:T(8,128)S(1)} collective-permute-done((f32[256,256]{0,1:T(8,128)S(1)}, f32[256,256]{0,1:T(8,128)S(1)}, u32[]{:S(2)}, u32[]{:S(2)}) %collective-permute-start.9) | collective-permute-done | bytes 262176 | tf_op jit(solution)/shard_map/ppermute | solution.py:582
  409.6 11.7 %cholesky.50 = f32[128,128]{1,0:T(8,128)S(1)} custom-call(f32[128,128]{1,0:T(8,128)S(1)} %cholesky.118), custom_call_target="Cholesky" | custom-call | tf_op jit(solution)/shard_map/jit(cholesky)/cholesky | solution.py:586
  421.4 9.8 %custom-call.14 = f32[1,128,128]{1,2,0:T(8,128)S(1)} custom-call(f32[1,128,128]{2,1,0:T(8,128)S(1)} %get-tuple-element.114), custom_call_target="InvertDiagBlocksLowerTriangular" | custom-call | tf_op jit(solution)/shard_map/jit(cholesky)/cholesky | solution.py:586
  431.7 11.7 %cholesky.105 = f32[128,128]{1,0:T(8,128)S(1)} custom-call(f32[128,128]{1,0:T(8,128)S(1)} %convolution_subtract_fusion.1), custom_call_target="Cholesky" | custom-call | tf_op jit(solution)/shard_map/jit(cholesky)/cholesky | solution.py:586
  446.0 4.0 while.1
  446.8 1.3 bitcast_dynamic-update-slice_fusion.2
  448.7 1.3 bitcast_dynamic-update-slice_fusion.2
  450.0 19.7 %custom-call.15 = f32[2,128,128]{1,2,0:T(8,128)S(1)} custom-call(f32[2,128,128]{2,1,0:T(8,128)S(1)} %get-tuple-element.86), custom_call_target="InvertDiagBlocksLowerTriangular" | custom-call | tf_op jit(solution)/shard_map/triangular_solve | solution.py:587
  470.6 4.6 all-to-all-start.1
  475.9 16.4 %shard_map.53 = f32[16,2,2,128,128]{4,3,2,1,0:T(8,128)} custom-call(s32[1]{0:T(128)} %bitcast.15.half_ref, s32[16]{0:T(128)} %bitcast_add_fusion.1.slot_ref, s32[8]{0:T(128)} %reshape.447.place_ref, s32[4]{0:T(128)} %and_select_fusion.4.origin_ref, f32[1024,1024]{1,0:T(8,128)} %bitcast.86, f32[1024,1024]{1,0:T(8,128)} %collective-permute-done.other_ref, ...), custom_call_target="tpu_custom_call" | custom-call | flops 6442450944 | bytes 20971520 | tf_op jit(solution)/shard_map/pallas_call | solution.py:176
  492.2 72.0 %all-to-all-done.1.rest_1_.rest_3_.rest_4_.rest_7_.rest_10_ = f32[16,2,2,128,128]{4,3,2,1,0:T(8,128)} async-done(((f32[16,2,2,128,128]{4,3,2,1,0:T(8,128)}), f32[16,2,2,128,128]{4,3,2,1,0:T(8,128)}, u32[]{:S(2)}, u32[]{:S(2)}) %all-to-all-start.1) | async-done | bytes 4194336 | tf_op jit(solution)/shard_map/all_to_all | solution.py:591
  564.3 4.6 all-to-all-start.2
  570.8 10.6 %shard_map.54 = f32[1536,256]{1,0:T(8,128)} custom-call(s32[24]{0:T(128)} %max.46.slot_ref, s32[24]{0:T(128)} %reshape.468.valid_ref, s32[2,8]{1,0:T(2,128)} %pad_add_fusion.2.place_ref, f32[1536,3072]{1,0:T(8,128)} %root_ref.5, f32[16,2,2,128,128]{4,3,2,1,0:T(8,128)} %all-to-all-done.rest_0_.rest_2_.rest_3_.rest_6_.rest_9_, ...), custom_call_target="tpu_custom_call" | custom-call | bytes 11534336 | tf_op jit(solution)/shard_map/pallas_call | solution.py:232
  581.5 2.8 fusion.40
  584.6 3.9 collective-permute-start.10
  588.5 2.4 collective-permute-start.11
  590.9 2.5 collective-permute-start.12
  593.4 16.4 %shard_map.56 = f32[16,2,2,128,128]{4,3,2,1,0:T(8,128)} custom-call(s32[1]{0:T(128)} %bitcast.15.half_ref, s32[16]{0:T(128)} %bitcast_add_fusion.1.slot_ref, s32[8]{0:T(128)} %reshape.448.place_ref, s32[4]{0:T(128)} %and_select_fusion.4.origin_ref, f32[1024,1024]{1,0:T(8,128)} %bitcast.87, f32[1024,1024]{1,0:T(8,128)} %collective-permute-done.other_ref, ...), custom_call_target="tpu_custom_call" | custom-call | flops 6442450944 | bytes 20971520 | tf_op jit(solution)/shard_map/pallas_call | solution.py:176
  609.8 51.6 %all-to-all-done.2.rest_2_.rest_5_.rest_8_.rest_11_ = f32[16,2,2,128,128]{4,3,2,1,0:T(8,128)} async-done(((f32[16,2,2,128,128]{4,3,2,1,0:T(8,128)}), f32[16,2,2,128,128]{4,3,2,1,0:T(8,128)}, u32[]{:S(2)}, u32[]{:S(2)}) %all-to-all-start.2) | async-done | bytes 4194336 | tf_op jit(solution)/shard_map/all_to_all | solution.py:591
  661.4 4.6 all-to-all-start.3
  666.0 2.8 add_add_fusion.rest_12_
  668.8 5.7 collective-permute-start.13
  674.5 2.5 collective-permute-start.14
  677.0 2.4 collective-permute-start.15
  679.4 71.0 %collective-permute-done.13 = f32[1536,256]{1,0:T(8,128)S(1)} collective-permute-done((f32[1536,256]{1,0:T(8,128)S(1)}, f32[1536,256]{1,0:T(8,128)S(1)}, u32[]{:S(2)}, u32[]{:S(2)}) %collective-permute-start.13) | collective-permute-done | bytes 1572896 | tf_op jit(solution)/shard_map/ppermute | solution.py:610
  750.4 16.9 %collective-permute-done.14 = f32[1536,256]{1,0:T(8,128)} collective-permute-done((f32[1536,256]{1,0:T(8,128)S(1)}, f32[1536,256]{1,0:T(8,128)}, u32[]{:S(2)}, u32[]{:S(2)}) %collective-permute-start.14) | collective-permute-done | bytes 1572896 | tf_op jit(solution)/shard_map/ppermute | solution.py:610
  767.3 16.9 %collective-permute-done.15 = f32[1536,256]{1,0:T(8,128)} collective-permute-done((f32[1536,256]{1,0:T(8,128)S(1)}, f32[1536,256]{1,0:T(8,128)}, u32[]{:S(2)}, u32[]{:S(2)}) %collective-permute-start.15) | collective-permute-done | bytes 1572896 | tf_op jit(solution)/shard_map/ppermute | solution.py:610
  784.5 1.7 collective-permute-start.16
  786.3 0.7 reshape.434.place_ref
  787.6 0.7 pad_add_fusion.1.place_ref
  788.2 25.3 %collective-permute-done.16 = f32[1536,256]{1,0:T(8,128)} collective-permute-done((f32[1536,256]{1,0:T(8,128)S(1)}, f32[1536,256]{1,0:T(8,128)}, u32[]{:S(2)}, u32[]{:S(2)}) %collective-permute-start.16) | collective-permute-done | bytes 1572896 | tf_op jit(solution)/shard_map/ppermute | solution.py:617
  813.5 1.6 broadcast_select_fusion.1
  815.2 1.9 pad_maximum_fusion.rest_13_
  817.0 25.0 %shard_map.55.root_ref = f32[1536,3072]{1,0:T(8,128)} custom-call(s32[24]{0:T(128)} %max.46.slot_ref, s32[24]{0:T(128)} %reshape.468.valid_ref, s32[2,12]{1,0:T(2,128)} %pad_add_fusion.1.place_ref, s32[2]{0:T(128)} %add_convert_fusion.flag_ref, f32[1536,3072]{1,0:T(8,128)} %root_ref.5, ...), custom_call_target="tpu_custom_call" | custom-call | flops 7247757312 | bytes 50331648 | tf_op jit(solution)/shard_map/pallas_call | solution.py:343
  842.0 18.7 %shard_map.57 = f32[1536,3072]{1,0:T(8,128)} custom-call(s32[24]{0:T(128)} %max.46.slot_ref, s32[24]{0:T(128)} %reshape.468.valid_ref, s32[2,4]{1,0:T(2,128)} %reshape.434.place_ref, f32[1536,3072]{1,0:T(8,128)} %shard_map.55.root_ref, f32[16,2,2,128,128]{4,3,2,1,0:T(8,128)} %all-to-all-done.3.a0_ref.a1_ref, f32[16,2,2,128,128]{4,3,2,1,0:T(8,128)} %all-to-all-done.3.a0_ref.a1_ref), custom_call_target="tpu_custom_call" | custom-call | bytes 41943040 | tf_op jit(solution)/shard_map/pallas_call | solution.py:399
  (135 shorter events, 18.2 us)
Async XLA Ops:
  6.5 138.5 %all-gather.3.cloned.1.call-start = ((), (), s32[]{:S(2)}) async-start(), calls=%async_computation.4 | async-start | bytes 9437184 | tf_op jit(solution)/shard_map/all_gather | solution.py:522
  6.5 7.6 collective-permute-start
  14.1 3.4 copy-start.3
  27.3 15.7 %collective-permute-start.2 = (f32[4,1024,128]{2,1,0:T(8,128)}, f32[4,1024,128]{2,1,0:T(8,128)}, u32[]{:S(2)}, u32[]{:S(2)}) collective-permute-start(f32[4,1024,128]{2,1,0:T(8,128)} %get-tuple-element.53), channel_id=1, source_target_pairs={{0,16},{2,18},{4,20},{6,22},{8,24},{10,26},{12,28},{14,30},{1,17},... | collective-permute-start | bytes 6291464 | tf_op jit(solution)/shard_map/ppermute | solution.py:535
  27.6 49.0 %collective-permute-start.1 = (f32[4,1024,128]{2,1,0:T(8,128)}, f32[4,1024,128]{2,1,0:T(8,128)}, u32[]{:S(2)}, u32[]{:S(2)}) collective-permute-start(f32[4,1024,128]{2,1,0:T(8,128)} %get-tuple-element.48), channel_id=1, source_target_pairs={{0,1},{2,3},{4,5},{6,7},{8,9},{10,11},{12,13},{14,15},{1,16},{3,18... | collective-permute-start | bytes 6291464 | tf_op jit(solution)/shard_map/ppermute | solution.py:535
  30.3 91.7 %collective-permute-start.3 = (f32[4,1024,128]{2,1,0:T(8,128)}, f32[4,1024,128]{2,1,0:T(8,128)}, u32[]{:S(2)}, u32[]{:S(2)}) collective-permute-start(f32[4,1024,128]{2,1,0:T(8,128)} %get-tuple-element.55), channel_id=1, source_target_pairs={{0,17},{2,19},{4,21},{6,23},{8,25},{10,27},{12,29},{14,31},{1,0},{... | collective-permute-start | bytes 6291464 | tf_op jit(solution)/shard_map/ppermute | solution.py:535
  42.9 123.6 %collective-permute-start.4 = (f32[4,1024,128]{2,1,0:T(8,128)}, f32[4,1024,128]{2,1,0:T(8,128)S(1)}, u32[]{:S(2)}, u32[]{:S(2)}) collective-permute-start(f32[4,1024,128]{2,1,0:T(8,128)} %get-tuple-element.57), channel_id=1, source_target_pairs={{0,1},{2,3},{4,5},{6,7},{8,9},{10,11},{12,13},{14,15},{1,16},{3,18... | collective-permute-start | bytes 6291464 | tf_op jit(solution)/shard_map/ppermute | solution.py:535
  44.9 121.5 %collective-permute-start.5 = (f32[4,1024,128]{2,1,0:T(8,128)}, f32[4,1024,128]{2,1,0:T(8,128)}, u32[]{:S(2)}, u32[]{:S(2)}) collective-permute-start(f32[4,1024,128]{2,1,0:T(8,128)} %get-tuple-element.58), channel_id=1, source_target_pairs={{0,16},{2,18},{4,20},{6,22},{8,24},{10,26},{12,28},{14,30},{1,17},... | collective-permute-start | bytes 6291464 | tf_op jit(solution)/shard_map/ppermute | solution.py:535
  44.9 166.6 %collective-permute-start.6 = (f32[4,1024,128]{2,1,0:T(8,128)}, f32[4,1024,128]{2,1,0:T(8,128)}, u32[]{:S(2)}, u32[]{:S(2)}) collective-permute-start(f32[4,1024,128]{2,1,0:T(8,128)} %get-tuple-element.59), channel_id=1, source_target_pairs={{0,17},{2,19},{4,21},{6,23},{8,25},{10,27},{12,29},{14,31},{1,0},{... | collective-permute-start | bytes 6291464 | tf_op jit(solution)/shard_map/ppermute | solution.py:535
  166.5 45.1 %copy-start.1 = (f32[4,1024,128]{2,1,0:T(8,128)}, f32[4,1024,128]{2,1,0:T(8,128)S(1)}, u32[]{:S(2)}) copy-start(f32[4,1024,128]{2,1,0:T(8,128)S(1)} %collective-permute-done.4.rest_1_) | copy-start | bytes 6291460
  211.6 197.8 %all-to-all-start = ((f32[16,2,2,128,128]{4,3,2,1,0:T(8,128)}), f32[16,2,2,128,128]{4,3,2,1,0:T(8,128)}, u32[]{:S(2)}, u32[]{:S(2)}) async-start(f32[16,2,2,128,128]{4,3,2,1,0:T(8,128)} %shard_map.50.rest_0_), calls=%async_computation | async-start | bytes 8388608 | tf_op jit(solution)/shard_map/all_to_all | solution.py:584
  217.7 258.2 %all-gather.5.cloned.1.call-start = ((), (), s32[]{:S(2)}) async-start(), calls=%async_computation.5 | async-start | bytes 9437184 | tf_op jit(solution)/shard_map/all_gather | solution.py:522
  242.0 26.2 %collective-permute-start.7 = (f32[256,256]{0,1:T(8,128)S(1)}, f32[256,256]{0,1:T(8,128)S(1)}, u32[]{:S(2)}, u32[]{:S(2)}) collective-permute-start(f32[256,256]{0,1:T(8,128)S(1)} %copy.26), channel_id=1, source_target_pairs={{0,2},{2,0},{4,6},{6,4},{8,10},{10,8},{12,14},{14,12},{1,3},{3,1},... | collective-permute-start | bytes 786440 | tf_op jit(solution)/shard_map/ppermute | solution.py:582
  268.2 56.3 %collective-permute-start.8 = (f32[256,256]{0,1:T(8,128)S(1)}, f32[256,256]{0,1:T(8,128)S(1)}, u32[]{:S(2)}, u32[]{:S(2)}) collective-permute-start(f32[256,256]{0,1:T(8,128)S(1)} %add.312), channel_id=1, source_target_pairs={{0,4},{2,6},{4,0},{6,2},{8,12},{10,14},{12,8},{14,10},{1,5},{3,7},... | collective-permute-start | bytes 786440 | tf_op jit(solution)/shard_map/ppermute | solution.py:582
  324.6 84.8 %collective-permute-start.9 = (f32[256,256]{0,1:T(8,128)S(1)}, f32[256,256]{0,1:T(8,128)S(1)}, u32[]{:S(2)}, u32[]{:S(2)}) collective-permute-start(f32[256,256]{0,1:T(8,128)S(1)} %add.313), channel_id=1, source_target_pairs={{0,8},{2,10},{4,12},{6,14},{8,0},{10,2},{12,4},{14,6},{1,9},{3,11}... | collective-permute-start | bytes 786440 | tf_op jit(solution)/shard_map/ppermute | solution.py:582
  470.6 93.7 %all-to-all-start.1 = ((f32[16,2,2,128,128]{4,3,2,1,0:T(8,128)}), f32[16,2,2,128,128]{4,3,2,1,0:T(8,128)}, u32[]{:S(2)}, u32[]{:S(2)}) async-start(f32[16,2,2,128,128]{4,3,2,1,0:T(8,128)} %shard_map.51.rest_1_), calls=%async_computation.1 | async-start | bytes 8388608 | tf_op jit(solution)/shard_map/all_to_all | solution.py:591
  564.3 97.1 %all-to-all-start.2 = ((f32[16,2,2,128,128]{4,3,2,1,0:T(8,128)}), f32[16,2,2,128,128]{4,3,2,1,0:T(8,128)}, u32[]{:S(2)}, u32[]{:S(2)}) async-start(f32[16,2,2,128,128]{4,3,2,1,0:T(8,128)} %shard_map.53), calls=%async_computation.2 | async-start | bytes 8388608 | tf_op jit(solution)/shard_map/all_to_all | solution.py:591
  584.6 81.4 %collective-permute-start.10 = (f32[1536,256]{1,0:T(8,128)S(1)}, f32[1536,256]{1,0:T(8,128)}, u32[]{:S(2)}, u32[]{:S(2)}) collective-permute-start(f32[1536,256]{1,0:T(8,128)S(1)} %pad_maximum_fusion.1), channel_id=1, source_target_pairs={{0,1},{2,3},{4,5},{6,7},{8,9},{10,11},{12,13},{14,15}} | collective-permute-start | bytes 4718600 | tf_op jit(solution)/shard_map/ppermute | solution.py:600
  588.5 77.5 %collective-permute-start.11 = (f32[1536,256]{1,0:T(8,128)S(1)}, f32[1536,256]{1,0:T(8,128)}, u32[]{:S(2)}, u32[]{:S(2)}) collective-permute-start(f32[1536,256]{1,0:T(8,128)S(1)} %pad_maximum_fusion.1), channel_id=1, source_target_pairs={{0,16},{2,18},{4,20},{6,22},{8,24},{10,26},{12,28},{14,30}} | collective-permute-start | bytes 4718600 | tf_op jit(solution)/shard_map/ppermute | solution.py:600
  590.9 75.1 %collective-permute-start.12 = (f32[1536,256]{1,0:T(8,128)S(1)}, f32[1536,256]{1,0:T(8,128)}, u32[]{:S(2)}, u32[]{:S(2)}) collective-permute-start(f32[1536,256]{1,0:T(8,128)S(1)} %pad_maximum_fusion.1), channel_id=1, source_target_pairs={{0,17},{2,19},{4,21},{6,23},{8,25},{10,27},{12,29},{14,31}} | collective-permute-start | bytes 4718600 | tf_op jit(solution)/shard_map/ppermute | solution.py:600
  661.4 180.6 %all-to-all-start.3 = ((f32[16,2,2,128,128]{4,3,2,1,0:T(8,128)}), f32[16,2,2,128,128]{4,3,2,1,0:T(8,128)}, u32[]{:S(2)}, u32[]{:S(2)}) async-start(f32[16,2,2,128,128]{4,3,2,1,0:T(8,128)} %shard_map.56), calls=%async_computation.3 | async-start | bytes 8388608 | tf_op jit(solution)/shard_map/all_to_all | solution.py:591
  668.8 115.8 %copy-start = (f32[1536,256]{1,0:T(8,128)}, f32[1536,256]{1,0:T(8,128)S(1)}, u32[]{:S(2)}) copy-start(f32[1536,256]{1,0:T(8,128)S(1)} %add_add_fusion.rest_12_) | copy-start | bytes 4718596
  668.8 81.6 %collective-permute-start.13 = (f32[1536,256]{1,0:T(8,128)S(1)}, f32[1536,256]{1,0:T(8,128)S(1)}, u32[]{:S(2)}, u32[]{:S(2)}) collective-permute-start(f32[1536,256]{1,0:T(8,128)S(1)} %add_add_fusion.rest_12_), channel_id=1, source_target_pairs={{0,12},{2,14},{5,1},{7,3},{24,20},{26,22},{29,25},{31,27}} | collective-permute-start | bytes 4718600 | tf_op jit(solution)/shard_map/ppermute | solution.py:610
  674.5 92.7 %collective-permute-start.14 = (f32[1536,256]{1,0:T(8,128)S(1)}, f32[1536,256]{1,0:T(8,128)}, u32[]{:S(2)}, u32[]{:S(2)}) collective-permute-start(f32[1536,256]{1,0:T(8,128)S(1)} %add_add_fusion.rest_12_), channel_id=1, source_target_pairs={{0,8},{2,10},{5,13},{7,15},{24,16},{26,18},{29,21},{31,23}} | collective-permute-start | bytes 4718600 | tf_op jit(solution)/shard_map/ppermute | solution.py:610
  677.0 107.1 %collective-permute-start.15 = (f32[1536,256]{1,0:T(8,128)S(1)}, f32[1536,256]{1,0:T(8,128)}, u32[]{:S(2)}, u32[]{:S(2)}) collective-permute-start(f32[1536,256]{1,0:T(8,128)S(1)} %add_add_fusion.rest_12_), channel_id=1, source_target_pairs={{0,4},{2,6},{5,9},{7,11},{24,28},{26,30},{29,17},{31,19}} | collective-permute-start | bytes 4718600 | tf_op jit(solution)/shard_map/ppermute | solution.py:610
  750.4 16.9 %copy-start.2 = (f32[1536,256]{1,0:T(8,128)}, f32[1536,256]{1,0:T(8,128)S(1)}, u32[]{:S(2)}) copy-start(f32[1536,256]{1,0:T(8,128)S(1)} %collective-permute-done.13) | copy-start | bytes 4718596
  784.5 29.0 %collective-permute-start.16 = (f32[1536,256]{1,0:T(8,128)S(1)}, f32[1536,256]{1,0:T(8,128)}, u32[]{:S(2)}, u32[]{:S(2)}) collective-permute-start(f32[1536,256]{1,0:T(8,128)S(1)} %select_select_fusion), channel_id=1, source_target_pairs={{0,2},{2,0},{4,6},{6,4},{8,10},{10,8},{12,14},{14,12},{1,3},{3,1},... | collective-permute-start | bytes 4718600 | tf_op jit(solution)/shard_map/ppermute | solution.py:617
Sparse Core Ops, SparseCore 0:
  17.4 127.5 all-gather.2
  220.6 203.4 all-gather.4

commit v8 on v6

--- a/solution.py
+++ b/solution.py
@@ -535,6 +535,9 @@
             got.append(lax.ppermute(packed[h][d], everyone, pairs))
         arrived.append(got)
 
+    exchange = functools.partial(
+        lax.all_to_all, axis_name="prow", split_axis=0, concat_axis=0, tiled=True
+    )
     spans = [(h, first) for h in range(halves) for first in range(0, half_col, width)]
     early = max(1, len(spans) // halves)
     outgoing, parts, col_places = [], [], []
@@ -546,6 +549,7 @@
         at = slice(h * half_col + first, h * half_col + first + width)
         col_places.append(col_local[:, :, at].reshape(2, -1))
         if len(outgoing) == 1:
+            parts.append(exchange(outgoing[0]))
             origins, outgoing[0], arrived = lax.optimization_barrier((origins, outgoing[0], arrived))
         elif outgoing:
             origins, outgoing[-1] = lax.optimization_barrier((origins, outgoing[-1]))
@@ -585,8 +589,7 @@
     inverse = lax.linalg.triangular_solve(
         factor, jnp.eye(RP, dtype=F32), left_side=True, lower=True
     )
-    for value in outgoing:
-        parts.append(lax.all_to_all(value, "prow", split_axis=0, concat_axis=0, tiled=True))
+    parts += [exchange(value) for value in outgoing[len(parts) :]]
 
     raw = first_panel(root_front, parts[:early], row_slot, row_valid, col_places[:early])
     solved = lax.dot_general(raw, inverse, NT, precision=HIGHEST, preferred_element_type=F32)

time: 786 us -> 775 us (0.986)
  waiting for transfers between devices: 469 us -> 461 us
    ppermute x3, waiting for transfers between devices: 119 us -> 69.1 us  [shards(): pivot = pivot + lax.ppermute(pivot, 'prow', pairs)]
    ppermute x6, waiting for transfers between devices: 125 us -> 166 us  [shards(): got.append(lax.ppermute(packed[h][d], everyone, pairs))]
  transfers between devices with their start and end apart: 23 -> 23, of which waited for: 15 -> 15; matrix products, arithmetic and copies ran while one was open for 11% -> 12% of each run, Pallas kernels for 16% -> 16%
where the time goes in v8:
time: 775 us; the launch traced here: 764 us
  waiting for transfers between devices  461 us (59%)
  Pallas kernels  145 us (19%)
  other arithmetic  69.7 us (9%)
  starting transfers between devices  55.2 us (7%)
  between operations  15.1 us (2%)
  local copies, waits for them, and re-layouts  15 us (2%)
    ppermute x6, waiting for transfers between devices, shards(): got.append(lax.ppermute(packed[h][d], everyone, pairs))  166 us
    ppermute x3, waiting for transfers between devices, shards(): got = lax.ppermute(own_rows, everyone, pairs)  93 us
    all_to_all x3, waiting for transfers between devices, shards(): parts += [exchange(value) for value in outgoing[len(parts):]]  76.7 us
    ppermute x3, waiting for transfers between devices, shards(): pivot = pivot + lax.ppermute(pivot, 'prow', pairs)  69.1 us
    pallas_call x4, Pallas kernels, schur_rows(): pl.pallas_call(body, grid_spec=pltpu.PrefetchScalarGridSpec(num_scalar_pr...  65.8 us
    another operation x7, other arithmetic, shards(): factor = jnp.linalg.cholesky(pivot)  34.6 us
    pallas_call x1, Pallas kernels, advance(): pl.pallas_call(body, grid_spec=pltpu.PrefetchScalarGridSpec(num_scalar_pr...  24.5 us
    ppermute x1, waiting for transfers between devices, shards(): tiles.append(lax.ppermute(tile, 'prow', pairs))  24.2 us
  transfers between devices with their start and end apart: 23, of which 15 were waited for; matrix products, arithmetic and copies ran while one was open for 12% of the time, Pallas kernels for 16%

profile of v8, /device:TPU:0, one launch (start us, length us, event | category | flops | bytes accessed | tf_op | source)
XLA Modules:
  0.0 764.3 jit_solution(12453914292961174045)
XLA Ops:
  7.0 0.8 eq.190
  8.6 0.7 reduce_window_sum.13
  12.0 2.1 collective-permute-done.other_ref
  14.1 3.2 shard_map.49
  19.6 7.7 %shard_map.48 = (f32[4,1024,128]{2,1,0:T(8,128)}, f32[4,1024,128]{2,1,0:T(8,128)}, f32[4,1024,128]{2,1,0:T(8,128)}, f32[4,1024,128]{2,1,0:T(8,128)}) custom-call(s32[16]{0:T(128)} %reshape.440.chosen_ref, f32[1024,4096]{1,0:T(8,128)} %bitcast.71, f32[1024,4096]{1,0:T(8,128)} %bitcast.72, f32[1024,4096]{1,0:T(8,128)} %bitcast.73, f32[1024,4096]{1,0:T(8,128)} %bitcast.74), custom_call_target="tpu_custom_call" | custom-call | bytes 16777216 | tf_op jit(solution)/shard_map/pallas_call | solution.py:48
  27.7 2.7 collective-permute-start.1
  31.0 0.6 reshape.439.chosen_ref
  31.6 7.7 %shard_map.47 = (f32[4,1024,128]{2,1,0:T(8,128)}, f32[4,1024,128]{2,1,0:T(8,128)}, f32[4,1024,128]{2,1,0:T(8,128)}, f32[4,1024,128]{2,1,0:T(8,128)}) custom-call(s32[16]{0:T(128)} %reshape.439.chosen_ref, f32[1024,4096]{1,0:T(8,128)} %bitcast.75, f32[1024,4096]{1,0:T(8,128)} %bitcast.76, f32[1024,4096]{1,0:T(8,128)} %bitcast.77, f32[1024,4096]{1,0:T(8,128)} %bitcast.78), custom_call_target="tpu_custom_call" | custom-call | bytes 16777216 | tf_op jit(solution)/shard_map/pallas_call | solution.py:48
  40.0 0.6 reshape.437.place_ref
  41.7 3.1 shard_map.46
  44.9 31.8 %collective-permute-done.1.rest_1_ = f32[4,1024,128]{2,1,0:T(8,128)} collective-permute-done((f32[4,1024,128]{2,1,0:T(8,128)}, f32[4,1024,128]{2,1,0:T(8,128)}, u32[]{:S(2)}, u32[]{:S(2)}) %collective-permute-start.1) | collective-permute-done | bytes 2097184 | tf_op jit(solution)/shard_map/ppermute | solution.py:535
  76.6 45.1 %collective-permute-done.3.rest_3_ = f32[4,1024,128]{2,1,0:T(8,128)} collective-permute-done((f32[4,1024,128]{2,1,0:T(8,128)}, f32[4,1024,128]{2,1,0:T(8,128)}, u32[]{:S(2)}, u32[]{:S(2)}) %collective-permute-start.3) | collective-permute-done | bytes 2097184 | tf_op jit(solution)/shard_map/ppermute | solution.py:535
  121.8 23.3 %all-gather.3.cloned.1.call-done.rest_4_ = f32[16,128,1024]{2,1,0:T(8,128)} async-done(((f32[2,128,1024]{2,1,0:T(8,128)}), f32[16,128,1024]{2,1,0:T(8,128)}) %all-gather.3.cloned.1.call-update) | async-done | bytes 8388624 | tf_op jit(solution)/shard_map/all_gather | solution.py:522
  145.0 16.6 %shard_map.50.rest_0_ = f32[16,2,2,128,128]{4,3,2,1,0:T(8,128)} custom-call(s32[1]{0:T(128)} %bitcast.4.half_ref, s32[16]{0:T(128)} %get-tuple-element.103.slot_ref, s32[8]{0:T(128)} %reshape.437.place_ref, s32[4]{0:T(128)} %and_select_fusion.5.origin_ref, f32[1024,1024]{1,0:T(8,128)} %bitcast.82, f32[1024,1024]{1,0:T(8,128)} %collective-permute-done.other_ref, ...), custom_call_target="tpu_custom_call" | custom-call | flops 6442450944 | bytes 20971520 | tf_op jit(solution)/shard_map/pallas_call | solution.py:176
  161.7 4.6 all-to-all-start
  166.2 1.5 collective-permute-start.4
  168.0 0.7 reshape.443.place_ref
  169.6 0.7 select_reduce_fusion.6
  170.8 43.6 %collective-permute-done.4.rest_1_ = f32[4,1024,128]{2,1,0:T(8,128)S(1)} collective-permute-done((f32[4,1024,128]{2,1,0:T(8,128)}, f32[4,1024,128]{2,1,0:T(8,128)S(1)}, u32[]{:S(2)}, u32[]{:S(2)}) %collective-permute-start.4) | collective-permute-done | bytes 2097184 | tf_op jit(solution)/shard_map/ppermute | solution.py:535
  214.4 45.1 %collective-permute-done.6.rest_3_ = f32[4,1024,128]{2,1,0:T(8,128)} collective-permute-done((f32[4,1024,128]{2,1,0:T(8,128)}, f32[4,1024,128]{2,1,0:T(8,128)}, u32[]{:S(2)}, u32[]{:S(2)}) %collective-permute-start.6) | collective-permute-done | bytes 2097184 | tf_op jit(solution)/shard_map/ppermute | solution.py:535
  259.5 16.4 %shard_map.51.rest_1_ = f32[16,2,2,128,128]{4,3,2,1,0:T(8,128)} custom-call(s32[1]{0:T(128)} %bitcast.4.half_ref, s32[16]{0:T(128)} %get-tuple-element.103.slot_ref, s32[8]{0:T(128)} %reshape.443.place_ref, s32[4]{0:T(128)} %and_select_fusion.5.origin_ref, f32[1024,1024]{1,0:T(8,128)} %bitcast.83, f32[1024,1024]{1,0:T(8,128)} %collective-permute-done.other_ref, ...), custom_call_target="tpu_custom_call" | custom-call | flops 6442450944 | bytes 20971520 | tf_op jit(solution)/shard_map/pallas_call | solution.py:176
  275.9 2.9 shard_map.52
  278.8 1.1 copy.26
  279.9 1.9 collective-permute-start.7
  281.8 14.7 %collective-permute-done.7 = f32[256,256]{0,1:T(8,128)S(1)} collective-permute-done((f32[256,256]{0,1:T(8,128)S(1)}, f32[256,256]{0,1:T(8,128)S(1)}, u32[]{:S(2)}, u32[]{:S(2)}) %collective-permute-start.7) | collective-permute-done | bytes 262176 | tf_op jit(solution)/shard_map/ppermute | solution.py:583
  296.5 3.5 collective-permute-start.8
  300.0 33.0 %collective-permute-done.8 = f32[256,256]{0,1:T(8,128)S(1)} collective-permute-done((f32[256,256]{0,1:T(8,128)S(1)}, f32[256,256]{0,1:T(8,128)S(1)}, u32[]{:S(2)}, u32[]{:S(2)}) %collective-permute-start.8) | collective-permute-done | bytes 262176 | tf_op jit(solution)/shard_map/ppermute | solution.py:583
  333.2 21.4 %collective-permute-done.9 = f32[256,256]{0,1:T(8,128)S(1)} collective-permute-done((f32[256,256]{0,1:T(8,128)S(1)}, f32[256,256]{0,1:T(8,128)S(1)}, u32[]{:S(2)}, u32[]{:S(2)}) %collective-permute-start.9) | collective-permute-done | bytes 262176 | tf_op jit(solution)/shard_map/ppermute | solution.py:583
  354.6 7.4 all-to-all-start.1
  362.6 16.4 %shard_map.53 = f32[16,2,2,128,128]{4,3,2,1,0:T(8,128)} custom-call(s32[1]{0:T(128)} %bitcast.4.half_ref, s32[16]{0:T(128)} %get-tuple-element.103.slot_ref, s32[8]{0:T(128)} %reshape.444.place_ref, s32[4]{0:T(128)} %and_select_fusion.5.origin_ref, f32[1024,1024]{1,0:T(8,128)} %bitcast.84, f32[1024,1024]{1,0:T(8,128)} %collective-permute-done.other_ref, ...), custom_call_target="tpu_custom_call" | custom-call | flops 6442450944 | bytes 20971520 | tf_op jit(solution)/shard_map/pallas_call | solution.py:176
  378.9 76.7 %all-to-all-done.1.rest_1_.rest_3_.rest_4_.rest_7_.rest_10_ = f32[16,2,2,128,128]{4,3,2,1,0:T(8,128)} async-done(((f32[16,2,2,128,128]{4,3,2,1,0:T(8,128)}), f32[16,2,2,128,128]{4,3,2,1,0:T(8,128)}, u32[]{:S(2)}, u32[]{:S(2)}) %all-to-all-start.1) | async-done | bytes 4194336 | tf_op jit(solution)/shard_map/all_to_all | solution.py:592
  455.7 4.8 all-to-all-start.2
  461.7 0.7 reshape.465.valid_ref
  462.6 11.7 %cholesky.50 = f32[128,128]{1,0:T(8,128)S(1)} custom-call(f32[128,128]{1,0:T(8,128)S(1)} %cholesky.118), custom_call_target="Cholesky" | custom-call | tf_op jit(solution)/shard_map/jit(cholesky)/cholesky | solution.py:588
  474.4 9.8 %custom-call.14 = f32[1,128,128]{1,2,0:T(8,128)S(1)} custom-call(f32[1,128,128]{2,1,0:T(8,128)S(1)} %get-tuple-element.116), custom_call_target="InvertDiagBlocksLowerTriangular" | custom-call | tf_op jit(solution)/shard_map/jit(cholesky)/cholesky | solution.py:588
  484.7 11.7 %cholesky.105 = f32[128,128]{1,0:T(8,128)S(1)} custom-call(f32[128,128]{1,0:T(8,128)S(1)} %convolution_subtract_fusion.1), custom_call_target="Cholesky" | custom-call | tf_op jit(solution)/shard_map/jit(cholesky)/cholesky | solution.py:588
  496.4 0.7 compare_reduce_fusion
  499.0 3.7 while.1
  499.6 1.3 bitcast_dynamic-update-slice_fusion.2
  501.4 1.3 bitcast_dynamic-update-slice_fusion.2
  502.7 19.9 %custom-call.15 = f32[2,128,128]{1,2,0:T(8,128)S(1)} custom-call(f32[2,128,128]{2,1,0:T(8,128)S(1)} %get-tuple-element.86), custom_call_target="InvertDiagBlocksLowerTriangular" | custom-call | tf_op jit(solution)/shard_map/triangular_solve | solution.py:589
  523.5 10.8 %shard_map.54 = f32[1536,256]{1,0:T(8,128)} custom-call(s32[24]{0:T(128)} %max.46.slot_ref, s32[24]{0:T(128)} %reshape.465.valid_ref, s32[2,8]{1,0:T(2,128)} %pad_add_fusion.2.place_ref, f32[1536,3072]{1,0:T(8,128)} %root_ref.5, f32[16,2,2,128,128]{4,3,2,1,0:T(8,128)} %all-to-all-done.rest_0_.rest_2_.rest_3_.rest_6_.rest_9_, ...), custom_call_target="tpu_custom_call" | custom-call | bytes 11534336 | tf_op jit(solution)/shard_map/pallas_call | solution.py:232
  534.3 2.8 fusion
  537.4 4.3 collective-permute-start.10
  541.7 2.4 collective-permute-start.11
  544.2 2.5 collective-permute-start.12
  546.7 16.4 %shard_map.56 = f32[16,2,2,128,128]{4,3,2,1,0:T(8,128)} custom-call(s32[1]{0:T(128)} %bitcast.4.half_ref, s32[16]{0:T(128)} %get-tuple-element.103.slot_ref, s32[8]{0:T(128)} %reshape.445.place_ref, s32[4]{0:T(128)} %and_select_fusion.5.origin_ref, f32[1024,1024]{1,0:T(8,128)} %bitcast.85, f32[1024,1024]{1,0:T(8,128)} %collective-permute-done.other_ref, ...), custom_call_target="tpu_custom_call" | custom-call | flops 6442450944 | bytes 20971520 | tf_op jit(solution)/shard_map/pallas_call | solution.py:176
  563.1 5.7 all-to-all-start.3
  568.9 6.5 collective-permute-done.12
  575.3 2.8 add_add_fusion.rest_12_
  578.1 5.8 collective-permute-start.13
  583.9 2.5 collective-permute-start.14
  586.4 2.4 collective-permute-start.15
  588.8 59.3 %collective-permute-done.13 = f32[1536,256]{1,0:T(8,128)S(1)} collective-permute-done((f32[1536,256]{1,0:T(8,128)S(1)}, f32[1536,256]{1,0:T(8,128)S(1)}, u32[]{:S(2)}, u32[]{:S(2)}) %collective-permute-start.13) | collective-permute-done | bytes 1572896 | tf_op jit(solution)/shard_map/ppermute | solution.py:611
  648.1 16.9 %collective-permute-done.14 = f32[1536,256]{1,0:T(8,128)} collective-permute-done((f32[1536,256]{1,0:T(8,128)S(1)}, f32[1536,256]{1,0:T(8,128)}, u32[]{:S(2)}, u32[]{:S(2)}) %collective-permute-start.14) | collective-permute-done | bytes 1572896 | tf_op jit(solution)/shard_map/ppermute | solution.py:611
  665.0 16.9 %collective-permute-done.15 = f32[1536,256]{1,0:T(8,128)} collective-permute-done((f32[1536,256]{1,0:T(8,128)S(1)}, f32[1536,256]{1,0:T(8,128)}, u32[]{:S(2)}, u32[]{:S(2)}) %collective-permute-start.15) | collective-permute-done | bytes 1572896 | tf_op jit(solution)/shard_map/ppermute | solution.py:611
  682.3 1.9 collective-permute-start.16
  684.9 0.7 add_convert_fusion.flag_ref
  685.5 0.7 pad_add_fusion.1.place_ref
  686.2 24.2 %collective-permute-done.16 = f32[1536,256]{1,0:T(8,128)} collective-permute-done((f32[1536,256]{1,0:T(8,128)S(1)}, f32[1536,256]{1,0:T(8,128)}, u32[]{:S(2)}, u32[]{:S(2)}) %collective-permute-start.16) | collective-permute-done | bytes 1572896 | tf_op jit(solution)/shard_map/ppermute | solution.py:618
  710.4 1.6 broadcast_select_fusion.1
  712.0 1.9 pad_maximum_fusion.rest_13_
  713.9 24.5 %shard_map.55.root_ref = f32[1536,3072]{1,0:T(8,128)} custom-call(s32[24]{0:T(128)} %max.46.slot_ref, s32[24]{0:T(128)} %reshape.465.valid_ref, s32[2,12]{1,0:T(2,128)} %pad_add_fusion.1.place_ref, s32[2]{0:T(128)} %add_convert_fusion.flag_ref, f32[1536,3072]{1,0:T(8,128)} %root_ref.5, ...), custom_call_target="tpu_custom_call" | custom-call | flops 7247757312 | bytes 50331648 | tf_op jit(solution)/shard_map/pallas_call | solution.py:343
  738.4 19.1 %shard_map.57 = f32[1536,3072]{1,0:T(8,128)} custom-call(s32[24]{0:T(128)} %max.46.slot_ref, s32[24]{0:T(128)} %reshape.465.valid_ref, s32[2,4]{1,0:T(2,128)} %reshape.432.place_ref, f32[1536,3072]{1,0:T(8,128)} %shard_map.55.root_ref, f32[16,2,2,128,128]{4,3,2,1,0:T(8,128)} %all-to-all-done.3.a0_ref.a1_ref, f32[16,2,2,128,128]{4,3,2,1,0:T(8,128)} %all-to-all-done.3.a0_ref.a1_ref), custom_call_target="tpu_custom_call" | custom-call | bytes 41943040 | tf_op jit(solution)/shard_map/pallas_call | solution.py:399
  (136 shorter events, 17.5 us)
Async XLA Ops:
  6.5 138.5 %all-gather.3.cloned.1.call-start = ((), (), s32[]{:S(2)}) async-start(), calls=%async_computation.4 | async-start | bytes 9437184 | tf_op jit(solution)/shard_map/all_gather | solution.py:522
  6.5 7.6 collective-permute-start
  14.1 3.4 copy-start.4
  17.3 345.2 %all-gather.5.cloned.1.call-start = ((), (), s32[]{:S(2)}) async-start(), calls=%async_computation.5 | async-start | bytes 9437184 | tf_op jit(solution)/shard_map/all_gather | solution.py:522
  27.3 17.5 %collective-permute-start.2 = (f32[4,1024,128]{2,1,0:T(8,128)}, f32[4,1024,128]{2,1,0:T(8,128)S(1)}, u32[]{:S(2)}, u32[]{:S(2)}) collective-permute-start(f32[4,1024,128]{2,1,0:T(8,128)} %get-tuple-element.53), channel_id=1, source_target_pairs={{0,16},{2,18},{4,20},{6,22},{8,24},{10,26},{12,28},{14,30},{1,17},... | collective-permute-start | bytes 6291464 | tf_op jit(solution)/shard_map/ppermute | solution.py:535
  27.7 49.0 %collective-permute-start.1 = (f32[4,1024,128]{2,1,0:T(8,128)}, f32[4,1024,128]{2,1,0:T(8,128)}, u32[]{:S(2)}, u32[]{:S(2)}) collective-permute-start(f32[4,1024,128]{2,1,0:T(8,128)} %get-tuple-element.48), channel_id=1, source_target_pairs={{0,1},{2,3},{4,5},{6,7},{8,9},{10,11},{12,13},{14,15},{1,16},{3,18... | collective-permute-start | bytes 6291464 | tf_op jit(solution)/shard_map/ppermute | solution.py:535
  30.4 91.4 %collective-permute-start.3 = (f32[4,1024,128]{2,1,0:T(8,128)}, f32[4,1024,128]{2,1,0:T(8,128)}, u32[]{:S(2)}, u32[]{:S(2)}) collective-permute-start(f32[4,1024,128]{2,1,0:T(8,128)} %get-tuple-element.55), channel_id=1, source_target_pairs={{0,17},{2,19},{4,21},{6,23},{8,25},{10,27},{12,29},{14,31},{1,0},{... | collective-permute-start | bytes 6291464 | tf_op jit(solution)/shard_map/ppermute | solution.py:535
  44.9 100.2 %copy-start.2 = (f32[4,1024,128]{2,1,0:T(8,128)}, f32[4,1024,128]{2,1,0:T(8,128)S(1)}, u32[]{:S(2)}) copy-start(f32[4,1024,128]{2,1,0:T(8,128)S(1)} %collective-permute-done.2.rest_2_) | copy-start | bytes 6291460
  161.7 193.0 %all-to-all-start = ((f32[16,2,2,128,128]{4,3,2,1,0:T(8,128)}), f32[16,2,2,128,128]{4,3,2,1,0:T(8,128)}, u32[]{:S(2)}, u32[]{:S(2)}) async-start(f32[16,2,2,128,128]{4,3,2,1,0:T(8,128)} %shard_map.50.rest_0_), calls=%async_computation | async-start | bytes 8388608 | tf_op jit(solution)/shard_map/all_to_all | solution.py:552
  166.2 48.1 %collective-permute-start.4 = (f32[4,1024,128]{2,1,0:T(8,128)}, f32[4,1024,128]{2,1,0:T(8,128)S(1)}, u32[]{:S(2)}, u32[]{:S(2)}) collective-permute-start(f32[4,1024,128]{2,1,0:T(8,128)} %get-tuple-element.57), channel_id=1, source_target_pairs={{0,1},{2,3},{4,5},{6,7},{8,9},{10,11},{12,13},{14,15},{1,16},{3,18... | collective-permute-start | bytes 6291464 | tf_op jit(solution)/shard_map/ppermute | solution.py:535
  167.8 46.6 %collective-permute-start.5 = (f32[4,1024,128]{2,1,0:T(8,128)}, f32[4,1024,128]{2,1,0:T(8,128)}, u32[]{:S(2)}, u32[]{:S(2)}) collective-permute-start(f32[4,1024,128]{2,1,0:T(8,128)} %get-tuple-element.58), channel_id=1, source_target_pairs={{0,16},{2,18},{4,20},{6,22},{8,24},{10,26},{12,28},{14,30},{1,17},... | collective-permute-start | bytes 6291464 | tf_op jit(solution)/shard_map/ppermute | solution.py:535
  167.8 91.7 %collective-permute-start.6 = (f32[4,1024,128]{2,1,0:T(8,128)}, f32[4,1024,128]{2,1,0:T(8,128)}, u32[]{:S(2)}, u32[]{:S(2)}) collective-permute-start(f32[4,1024,128]{2,1,0:T(8,128)} %get-tuple-element.59), channel_id=1, source_target_pairs={{0,17},{2,19},{4,21},{6,23},{8,25},{10,27},{12,29},{14,31},{1,0},{... | collective-permute-start | bytes 6291464 | tf_op jit(solution)/shard_map/ppermute | solution.py:535
  214.4 61.5 %copy-start.1 = (f32[4,1024,128]{2,1,0:T(8,128)}, f32[4,1024,128]{2,1,0:T(8,128)S(1)}, u32[]{:S(2)}) copy-start(f32[4,1024,128]{2,1,0:T(8,128)S(1)} %collective-permute-done.4.rest_1_) | copy-start | bytes 6291460
  279.9 16.6 %collective-permute-start.7 = (f32[256,256]{0,1:T(8,128)S(1)}, f32[256,256]{0,1:T(8,128)S(1)}, u32[]{:S(2)}, u32[]{:S(2)}) collective-permute-start(f32[256,256]{0,1:T(8,128)S(1)} %copy.26), channel_id=1, source_target_pairs={{0,2},{2,0},{4,6},{6,4},{8,10},{10,8},{12,14},{14,12},{1,3},{3,1},... | collective-permute-start | bytes 786440 | tf_op jit(solution)/shard_map/ppermute | solution.py:583
  296.5 36.5 %collective-permute-start.8 = (f32[256,256]{0,1:T(8,128)S(1)}, f32[256,256]{0,1:T(8,128)S(1)}, u32[]{:S(2)}, u32[]{:S(2)}) collective-permute-start(f32[256,256]{0,1:T(8,128)S(1)} %add.312), channel_id=1, source_target_pairs={{0,4},{2,6},{4,0},{6,2},{8,12},{10,14},{12,8},{14,10},{1,5},{3,7},... | collective-permute-start | bytes 786440 | tf_op jit(solution)/shard_map/ppermute | solution.py:583
  333.1 21.5 %collective-permute-start.9 = (f32[256,256]{0,1:T(8,128)S(1)}, f32[256,256]{0,1:T(8,128)S(1)}, u32[]{:S(2)}, u32[]{:S(2)}) collective-permute-start(f32[256,256]{0,1:T(8,128)S(1)} %add.313), channel_id=1, source_target_pairs={{0,8},{2,10},{4,12},{6,14},{8,0},{10,2},{12,4},{14,6},{1,9},{3,11}... | collective-permute-start | bytes 786440 | tf_op jit(solution)/shard_map/ppermute | solution.py:583
  354.6 101.0 %all-to-all-start.1 = ((f32[16,2,2,128,128]{4,3,2,1,0:T(8,128)}), f32[16,2,2,128,128]{4,3,2,1,0:T(8,128)}, u32[]{:S(2)}, u32[]{:S(2)}) async-start(f32[16,2,2,128,128]{4,3,2,1,0:T(8,128)} %shard_map.51.rest_1_), calls=%async_computation.1 | async-start | bytes 8388608 | tf_op jit(solution)/shard_map/all_to_all | solution.py:592
  455.7 107.5 %all-to-all-start.2 = ((f32[16,2,2,128,128]{4,3,2,1,0:T(8,128)}), f32[16,2,2,128,128]{4,3,2,1,0:T(8,128)}, u32[]{:S(2)}, u32[]{:S(2)}) async-start(f32[16,2,2,128,128]{4,3,2,1,0:T(8,128)} %shard_map.53), calls=%async_computation.2 | async-start | bytes 8388608 | tf_op jit(solution)/shard_map/all_to_all | solution.py:592
  537.4 31.5 %collective-permute-start.10 = (f32[1536,256]{1,0:T(8,128)S(1)}, f32[1536,256]{1,0:T(8,128)}, u32[]{:S(2)}, u32[]{:S(2)}) collective-permute-start(f32[1536,256]{1,0:T(8,128)S(1)} %pad_maximum_fusion.1), channel_id=1, source_target_pairs={{0,1},{2,3},{4,5},{6,7},{8,9},{10,11},{12,13},{14,15}} | collective-permute-start | bytes 4718600 | tf_op jit(solution)/shard_map/ppermute | solution.py:601
  541.7 27.1 %collective-permute-start.11 = (f32[1536,256]{1,0:T(8,128)S(1)}, f32[1536,256]{1,0:T(8,128)}, u32[]{:S(2)}, u32[]{:S(2)}) collective-permute-start(f32[1536,256]{1,0:T(8,128)S(1)} %pad_maximum_fusion.1), channel_id=1, source_target_pairs={{0,16},{2,18},{4,20},{6,22},{8,24},{10,26},{12,28},{14,30}} | collective-permute-start | bytes 4718600 | tf_op jit(solution)/shard_map/ppermute | solution.py:601
  544.2 31.1 %collective-permute-start.12 = (f32[1536,256]{1,0:T(8,128)S(1)}, f32[1536,256]{1,0:T(8,128)}, u32[]{:S(2)}, u32[]{:S(2)}) collective-permute-start(f32[1536,256]{1,0:T(8,128)S(1)} %pad_maximum_fusion.1), channel_id=1, source_target_pairs={{0,17},{2,19},{4,21},{6,23},{8,25},{10,27},{12,29},{14,31}} | collective-permute-start | bytes 4718600 | tf_op jit(solution)/shard_map/ppermute | solution.py:601
  563.1 175.2 %all-to-all-start.3 = ((f32[16,2,2,128,128]{4,3,2,1,0:T(8,128)}), f32[16,2,2,128,128]{4,3,2,1,0:T(8,128)}, u32[]{:S(2)}, u32[]{:S(2)}) async-start(f32[16,2,2,128,128]{4,3,2,1,0:T(8,128)} %shard_map.56), calls=%async_computation.3 | async-start | bytes 8388608 | tf_op jit(solution)/shard_map/all_to_all | solution.py:592
  578.1 104.2 %copy-start = (f32[1536,256]{1,0:T(8,128)}, f32[1536,256]{1,0:T(8,128)S(1)}, u32[]{:S(2)}) copy-start(f32[1536,256]{1,0:T(8,128)S(1)} %add_add_fusion.rest_12_) | copy-start | bytes 4718596
  578.1 70.0 %collective-permute-start.13 = (f32[1536,256]{1,0:T(8,128)S(1)}, f32[1536,256]{1,0:T(8,128)S(1)}, u32[]{:S(2)}, u32[]{:S(2)}) collective-permute-start(f32[1536,256]{1,0:T(8,128)S(1)} %add_add_fusion.rest_12_), channel_id=1, source_target_pairs={{0,12},{2,14},{5,1},{7,3},{24,20},{26,22},{29,25},{31,27}} | collective-permute-start | bytes 4718600 | tf_op jit(solution)/shard_map/ppermute | solution.py:611
  583.9 81.0 %collective-permute-start.14 = (f32[1536,256]{1,0:T(8,128)S(1)}, f32[1536,256]{1,0:T(8,128)}, u32[]{:S(2)}, u32[]{:S(2)}) collective-permute-start(f32[1536,256]{1,0:T(8,128)S(1)} %add_add_fusion.rest_12_), channel_id=1, source_target_pairs={{0,8},{2,10},{5,13},{7,15},{24,16},{26,18},{29,21},{31,23}} | collective-permute-start | bytes 4718600 | tf_op jit(solution)/shard_map/ppermute | solution.py:611
  586.4 95.4 %collective-permute-start.15 = (f32[1536,256]{1,0:T(8,128)S(1)}, f32[1536,256]{1,0:T(8,128)}, u32[]{:S(2)}, u32[]{:S(2)}) collective-permute-start(f32[1536,256]{1,0:T(8,128)S(1)} %add_add_fusion.rest_12_), channel_id=1, source_target_pairs={{0,4},{2,6},{5,9},{7,11},{24,28},{26,30},{29,17},{31,19}} | collective-permute-start | bytes 4718600 | tf_op jit(solution)/shard_map/ppermute | solution.py:611
  648.1 16.9 %copy-start.3 = (f32[1536,256]{1,0:T(8,128)}, f32[1536,256]{1,0:T(8,128)S(1)}, u32[]{:S(2)}) copy-start(f32[1536,256]{1,0:T(8,128)S(1)} %collective-permute-done.13) | copy-start | bytes 4718596
  682.3 28.1 %collective-permute-start.16 = (f32[1536,256]{1,0:T(8,128)S(1)}, f32[1536,256]{1,0:T(8,128)}, u32[]{:S(2)}, u32[]{:S(2)}) collective-permute-start(f32[1536,256]{1,0:T(8,128)S(1)} %select_select_fusion), channel_id=1, source_target_pairs={{0,2},{2,0},{4,6},{6,4},{8,10},{10,8},{12,14},{14,12},{1,3},{3,1},... | collective-permute-start | bytes 4718600 | tf_op jit(solution)/shard_map/ppermute | solution.py:618
Sparse Core Ops, SparseCore 0:
  17.5 127.5 all-gather.2
  147.1 214.0 all-gather.4
